TPU v7x, 32 devices: a whole 2x2x4 slice. The times are simulated.
32 devices in a mesh: gx: 8 (over z, core), gy: 4 (over y, x).
Axes of the slice: x: 2, y: 2, z: 4, core: 2. Of those that a mesh axis runs over, the one named last changes fastest.
Arguments:
- particles: float32 [8, 262144], P(None, ('gx', 'gy'))
- old_density: float32 [262144], P(('gx', 'gy')), may hold values from 0.5 to 4
- active: int32 [262144], P(('gx', 'gy')), may hold values 0 or 1
- send_rows: int32 [4, 65536], P(None, ('gx', 'gy')), may hold values from 0 to 8191, as said below
- send_count: int32 [4, 32], P(None, ('gx', 'gy')), may hold values from 682 to 2048, as said below
- export_rows: int32 [8, 32768], P(None, ('gx', 'gy')), may hold values from 0 to 8191
- pair_tiles: int32 [2, 16384], P(None, ('gx', 'gy')), may hold values from 0 to 255, as said below
- pair_count: int32 [32], P(('gx', 'gy')), may hold values from 128 to 512, as said below
Outputs:
- density: float32 [262144], P(('gx', 'gy'))
- acceleration: float32 [3, 262144], P(None, ('gx', 'gy'))
- heating: float32 [262144], P(('gx', 'gy'))
Inputs may be any that keep to these rules, and one draw needn't show every extreme that they name: `send_rows`: within one level and one device the 2048 offered rows are distinct local rows. `send_count`: the two devices that a level pairs have the same count; at every level some pair exchanges all 2048 offered rows. `pair_tiles`: a pair's source tile differs from its target tile; target tiles are below 128. `pair_count`: some device uses all 512 slots.
All inputs are finite; a program needn't handle non-finite values. No bound on the sum of `active` on one device may be relied on, other than what follows from the above.
Results may differ from a plain program's by a relative error of at most 0.0003.
Values sent between devices are 32-bit elements; how exact they have to be, the bound alone decides.
No kernel may reach another device: no remote copies, remote signals or barrier semaphores. Data moves between devices by JAX's collectives and lax.ppermute only.
A program may use at most 64 MiB of HBM per device.

v0:
```python
import math

import jax
import jax.numpy as jnp
from jax import lax
from jax.sharding import PartitionSpec as P

TILE = 64


PARTICLE_MASS = 1.0 / 512.0
ADIABATIC = 5.0 / 3.0
directions = ((-1, -1), (-1, 0), (-1, 1), (0, -1), (0, 1), (1, -1), (1, 0), (1, 1))


def from_behind(value, axis, steps):
    count = lax.axis_size(axis)
    pairs = [(source, (source + steps) % count) for source in range(count)]
    return lax.ppermute(value, axis, pairs)


def from_partner(block, axis, bit):
    count = lax.axis_size(axis)
    route = []
    for low in range(count):
        high = low | 1 << bit
        if high != low and high < count:
            route += [(low, high), (high, low)]
    return lax.ppermute(block, axis, route)


def kernel_value(dist_sq, smooth):
    q = jnp.sqrt(dist_sq) / smooth
    inner_part = 1.0 - 1.5 * q * q + 0.75 * q * q * q
    outer_part = 0.25 * (2.0 - q) ** 3
    profile = jnp.where(q < 1.0, inner_part, jnp.where(q < 2.0, outer_part, 0.0))
    return profile / (jnp.pi * smooth * smooth * smooth)


def kernel_slope(dist_sq, smooth):
    q = jnp.sqrt(dist_sq) / smooth
    inner_part = -3.0 + 2.25 * q
    outer_part = -0.75 * (2.0 - q) ** 2 / jnp.maximum(q, 1.0)
    profile = jnp.where(q < 1.0, inner_part, jnp.where(q < 2.0, outer_part, 0.0))
    return profile / (jnp.pi * smooth**5)


def separation(target_rows, source_rows):
    offset = target_rows[0:3, :, :, None] - source_rows[0:3, :, None, :]
    offset = offset - jnp.floor(offset + 0.5)
    return (offset, jnp.sum(offset * offset, axis=0))


def tile_select(targets, in_list, tile_count):
    return ((targets[:, None] == jnp.arange(tile_count)[None, :]) & in_list[:, None]).astype(
        jnp.float32
    )


def tile_matrix_of(pool_fields):
    field_count = pool_fields.shape[0]
    tile_view = pool_fields.reshape(field_count, -1, TILE)
    return jnp.moveaxis(tile_view, 1, 0).reshape(tile_view.shape[1], field_count * TILE)


def select_tiles(tile_matrix, index, field_count):
    onehot = (index[:, None] == jnp.arange(tile_matrix.shape[0])[None, :]).astype(jnp.float32)
    picked = jnp.dot(
        onehot, tile_matrix, precision=lax.Precision.HIGHEST, preferred_element_type=jnp.float32
    )
    return jnp.moveaxis(picked.reshape(index.shape[0], field_count, TILE), 1, 0)


def density_block(tile_matrix, targets, sources, in_list, tile_count):
    target_rows = select_tiles(tile_matrix, targets, 8)
    source_rows = select_tiles(tile_matrix, sources, 8)
    offset, dist_sq = separation(target_rows, source_rows)
    terms = PARTICLE_MASS * jnp.sum(kernel_value(dist_sq, target_rows[6][:, :, None]), axis=2)
    onehot = tile_select(targets, in_list, tile_count)
    return jnp.einsum("bt,br->tr", onehot, terms, precision=lax.Precision.HIGHEST)


def force_block(press_matrix, targets, sources, in_list, tile_count):
    target_rows = select_tiles(press_matrix, targets, 9)
    source_rows = select_tiles(press_matrix, sources, 9)
    target_press = target_rows[8]
    source_press = source_rows[8]
    offset, dist_sq = separation(target_rows, source_rows)
    slope = 0.5 * (
        kernel_slope(dist_sq, target_rows[6][:, :, None])
        + kernel_slope(dist_sq, source_rows[6][:, None, :])
    )
    weight_pair = PARTICLE_MASS * (target_press[:, :, None] + source_press[:, None, :]) * slope
    acceleration = -jnp.sum(weight_pair[None] * offset, axis=3)
    velocity_gap = target_rows[3:6, :, :, None] - source_rows[3:6, :, None, :]
    heating = 0.5 * jnp.sum(weight_pair * jnp.sum(velocity_gap * offset, axis=0), axis=2)
    terms = jnp.concatenate([acceleration, heating[None]], axis=0)
    onehot = tile_select(targets, in_list, tile_count)
    return jnp.einsum("bt,kbr->ktr", onehot, terms, precision=lax.Precision.HIGHEST)


def to_neighbours(outgoing):
    arrived = []
    for number in range(8):
        step_x, step_y = directions[number]
        portion = outgoing[number]
        if step_x != 0:
            portion = from_behind(portion, "gx", step_x)
        if step_y != 0:
            portion = from_behind(portion, "gy", step_y)
        arrived.append(portion)
    return jnp.concatenate(arrived, axis=-1)


def on_device(
    particles, old_density, active, send_rows, send_count, export_rows, pair_tiles, pair_count
):
    row_count = particles.shape[1]
    state = jnp.concatenate(
        [particles, old_density[None, :], active.astype(jnp.float32)[None, :]], axis=0
    )
    bits_x = lax.axis_size("gx").bit_length() - 1
    bits_y = lax.axis_size("gy").bit_length() - 1
    for section_level in range(4):
        slots = send_rows[section_level]
        taken = jnp.arange(slots.shape[0]) < send_count[section_level, 0]
        outgoing = jnp.take(state, slots, axis=1)
        if section_level < 2:
            incoming = from_partner(outgoing, "gx", bits_x - 1 - section_level)
        else:
            incoming = from_partner(outgoing, "gy", bits_y + 1 - section_level)
        state = state.at[:, slots].set(jnp.where(taken[None, :], incoming, outgoing))
    fields = state[0:8]
    density_rows = state[8]
    active_flag = state[9] == 1.0
    ghost_out = jnp.moveaxis(jnp.take(fields, export_rows, axis=1), 1, 0)
    pooled = jnp.concatenate([fields, to_neighbours(ghost_out)], axis=1)
    tile_matrix = tile_matrix_of(pooled)
    tile_count = row_count // TILE
    pair_total = pair_tiles.shape[1]
    block_size = math.gcd(pair_total, 64)
    used = pair_count[0]
    block_count = (used + block_size - 1) // block_size

    def density_step(which, running):
        begin = which * block_size
        targets = lax.dynamic_slice_in_dim(pair_tiles[0], begin, block_size)
        sources = lax.dynamic_slice_in_dim(pair_tiles[1], begin, block_size)
        in_list = begin + jnp.arange(block_size) < used
        return running + density_block(tile_matrix, targets, sources, in_list, tile_count)

    kernel_sums = lax.fori_loop(
        0, block_count, density_step, jnp.zeros((tile_count, TILE), jnp.float32)
    )
    smooth = fields[6]
    recomputed = PARTICLE_MASS * kernel_value(jnp.zeros_like(smooth), smooth) + kernel_sums.reshape(
        row_count
    )
    density_new = jnp.where(active_flag, recomputed, density_rows)
    ghost_density = to_neighbours(density_new[export_rows][:, None, :])[0]
    pool_density = jnp.concatenate([density_new, ghost_density], axis=0)
    press_row = (ADIABATIC - 1.0) * pooled[7] / pool_density
    press_matrix = tile_matrix_of(jnp.concatenate([pooled, press_row[None, :]], axis=0))

    def force_step(which, running):
        begin = which * block_size
        targets = lax.dynamic_slice_in_dim(pair_tiles[0], begin, block_size)
        sources = lax.dynamic_slice_in_dim(pair_tiles[1], begin, block_size)
        in_list = begin + jnp.arange(block_size) < used
        return running + force_block(press_matrix, targets, sources, in_list, tile_count)

    forces = lax.fori_loop(
        0, block_count, force_step, jnp.zeros((4, tile_count, TILE), jnp.float32)
    )
    forces = forces.reshape(4, row_count) * active_flag.astype(jnp.float32)[None, :]
    return (density_new, forces[0:3], forces[3])


def solution(mesh):
    in_specs = (
        P(None, ("gx", "gy")),
        P(("gx", "gy")),
        P(("gx", "gy")),
        P(None, ("gx", "gy")),
        P(None, ("gx", "gy")),
        P(None, ("gx", "gy")),
        P(None, ("gx", "gy")),
        P(("gx", "gy")),
    )
    out_specs = (P(("gx", "gy")), P(None, ("gx", "gy")), P(("gx", "gy")))
    return jax.shard_map(
        on_device, mesh=mesh, in_specs=in_specs, out_specs=out_specs, check_vma=False
    )
```

profile of v0, /device:TPU:0, one launch (start us, length us, event | category | flops | bytes accessed | tf_op | source)
XLA Modules:
  0.0 586.7 jit_solution(6157761789098042090)
XLA Ops:
  6.1 7.7 %gather_fusion.2 = f32[2048,10]{1,0:T(8,128)S(1)} fusion(f32[10,8192]{0,1:T(8,128)} %copy.144, s32[2048]{0:T(1024)S(1)} %fusion.79), kind=kCustom, calls=%fused_computation.clone | custom fusion | bytes 172032 | tf_op jit(solution)/shard_map/jit(_take)/gather | solution.py:127
  25.1 11.1 %scatter_custom_fusion = f32[10,8192]{0,1:T(8,128)} fusion(f32[10,8192]{0,1:T(8,128)} %copy.144, s32[2048]{0:T(1024)S(1)} %bitcast.205, f32[10,2048]{0,1:T(8,128)S(1)} %copy.143, pred[2048]{0:T(1024)(128)(4,1)S(1)} %iota_compare_fusion.13, f32[2048,10]{1,0:T(8,128)S(1)} %gather_fusion.2, pred[2048]{0:T(1024)(128)(4,1)S(1)} %compare_and_fusion.4), kind=kCustom, calls=%fused_computation.105 | custom fusion | flops 40960 | bytes 2428928 | tf_op jit(solution)/shard_map/scatter | solution.py:132
  36.2 7.6 %gather_fusion.3 = f32[2048,10]{1,0:T(8,128)S(1)} fusion(f32[10,8192]{0,1:T(8,128)} %scatter_custom_fusion, s32[2048]{0:T(1024)S(1)} %fusion.80), kind=kCustom, calls=%fused_computation.1.clone | custom fusion | bytes 172032 | tf_op jit(solution)/shard_map/jit(_take)/gather | solution.py:127
  49.9 11.1 %scatter_custom_fusion.1 = f32[10,8192]{0,1:T(8,128)} fusion(f32[10,8192]{0,1:T(8,128)} %scatter_custom_fusion, s32[2048]{0:T(1024)S(1)} %bitcast.204, f32[10,2048]{0,1:T(8,128)S(1)} %copy.146, pred[2048]{0:T(1024)(128)(4,1)S(1)} %iota_compare_fusion.12, f32[2048,10]{1,0:T(8,128)S(1)} %gather_fusion.3, pred[2048]{0:T(1024)(128)(4,1)S(1)} %compare_and_fusion.3), kind=kCustom, calls=%fused_computation.103 | custom fusion | flops 40960 | bytes 2428928 | tf_op jit(solution)/shard_map/scatter | solution.py:132
  61.1 7.6 %gather_fusion.4 = f32[2048,10]{1,0:T(8,128)S(1)} fusion(f32[10,8192]{0,1:T(8,128)} %scatter_custom_fusion.1, s32[2048]{0:T(1024)S(1)} %fusion.81), kind=kCustom, calls=%fused_computation.2.clone | custom fusion | bytes 172032 | tf_op jit(solution)/shard_map/jit(_take)/gather | solution.py:127
  74.8 11.1 %scatter_custom_fusion.2 = f32[10,8192]{0,1:T(8,128)} fusion(f32[10,8192]{0,1:T(8,128)} %scatter_custom_fusion.1, s32[2048]{0:T(1024)S(1)} %bitcast.203, f32[10,2048]{0,1:T(8,128)S(1)} %copy.148, pred[2048]{0:T(1024)(128)(4,1)S(1)} %iota_compare_fusion.11, f32[2048,10]{1,0:T(8,128)S(1)} %gather_fusion.4, pred[2048]{0:T(1024)(128)(4,1)S(1)} %compare_and_fusion.2), kind=kCustom, calls=%fused_computation.101 | custom fusion | flops 40960 | bytes 2428928 | tf_op jit(solution)/shard_map/scatter | solution.py:132
  85.9 7.6 %gather_fusion.5 = f32[2048,10]{1,0:T(8,128)S(1)} fusion(f32[10,8192]{0,1:T(8,128)} %scatter_custom_fusion.2, s32[2048]{0:T(1024)S(1)} %fusion.82), kind=kCustom, calls=%fused_computation.3.clone | custom fusion | bytes 172032 | tf_op jit(solution)/shard_map/jit(_take)/gather | solution.py:127
  99.6 11.1 %scatter_custom_fusion.3 = f32[10,8192]{0,1:T(8,128)} fusion(f32[10,8192]{0,1:T(8,128)} %scatter_custom_fusion.2, s32[2048]{0:T(1024)S(1)} %bitcast.202, f32[10,2048]{0,1:T(8,128)S(1)} %copy.150, pred[2048]{0:T(1024)(128)(4,1)S(1)} %iota_compare_fusion.10, f32[2048,10]{1,0:T(8,128)S(1)} %gather_fusion.5, pred[2048]{0:T(1024)(128)(4,1)S(1)} %compare_and_fusion.1), kind=kCustom, calls=%fused_computation.99 | custom fusion | flops 40960 | bytes 2428928 | tf_op jit(solution)/shard_map/scatter | solution.py:132
  110.7 30.1 %gather_fusion = f32[8192,8]{1,0:T(8,128)} fusion(f32[8,8192]{0,1:T(8,128)} %bitcast.173, s32[8192]{0:T(1024)S(1)} %bitcast_clamp_fusion), kind=kCustom, calls=%fused_computation.4 | custom fusion | bytes 557056 | tf_op jit(solution)/shard_map/jit(_take)/gather | solution.py:136
  168.8 53.0 %while.20 = (s32[]{:T(128)}, f32[128,64]{0,1:T(8,128)S(1)}, s32[]{:T(128)}, s32[2,512]{1,0:T(2,128)S(1)}, s32[]{:T(128)}, /*index=5*/f32[256,512]{1,0:T(8,128)S(1)}, s32[]{:T(128)}, s32[]{:T(128)}, s32[]{:T(128)}, s32[]{:T(128)}) while((s32[]{:T(128)}, f32[128,64]{0,1:T(8,128)S(1)}, s32[]{:T(128)}, s32[2,512]{1,0:T(2,128)S(1)}, s32[]{:T(128)}, ...), condition=%wide.region_7.9_spmd, body=%wide.region_4.0_spmd.sunk | while | flops 216862848 | bytes 4630559 | solution.py:152
  221.9 5.6 reshape.442
  227.6 12.7 %slice_reduce_fusion.1 = (f32[8192]{0:T(1024)S(1)}, f32[8192]{0:T(1024)S(1)}, f32[1,8192]{0,1:T(8,128)}, pred[1,8192]{0,1:T(8,128)(4,1)S(1)}) fusion(f32[10,8192]{0,1:T(8,128)} %scatter_custom_fusion.3, f32[1,8192]{0,1:T(8,128)} %reshape.442), kind=kLoop, calls=%fused_computation.97 | loop fusion | flops 196608 | bytes 237568 | tf_op jit(solution)/shard_map/slice | solution.py:155
  241.5 45.5 %gather_fusion.1 = f32[8192]{0:T(1024)S(1)} fusion(f32[8192]{0:T(1024)S(1)} %fusion.75, s32[8192]{0:T(1024)S(1)} %bitcast_clamp_fusion), kind=kCustom, calls=%fused_computation.5 | custom fusion | bytes 98304 | tf_op jit(solution)/shard_map/gather | solution.py:160
  307.1 277.0 %while.21 = (s32[]{:T(128)}, f32[4,128,64]{1,2,0:T(8,128)}, s32[]{:T(128)}, s32[2,512]{1,0:T(2,128)S(1)}, f32[256,576]{1,0:T(8,128)S(1)}, /*index=5*/s32[]{:T(128)}, s32[]{:T(128)}, s32[]{:T(128)}, s32[]{:T(128)}, s32[]{:T(128)}) while((s32[]{:T(128)}, f32[4,128,64]{1,2,0:T(8,128)}, s32[]{:T(128)}, s32[2,512]{1,0:T(2,128)S(1)}, ...), condition=%wide.region_13.15_spmd, body=%wide.region_8.14_spmd.sunk | while | flops 279838848 | bytes 12986679 | solution.py:172
  325.9 9.0 %fusion.134 = (f32[3,64,64]{2,1,0:T(8,128)S(1)}, f32[64,64,64]{2,1,0:T(8,128)}) fusion(f32[64,64,64]{2,1,0:T(8,128)} %multiply_multiply_fusion.22, f32[3,64,64]{2,1,0:T(8,128)S(1)} %copy.182, f32[3,64,64]{2,1,0:T(8,128)S(1)} %copy.183, f32[3,64,64]{2,1,0:T(8,128)S(1)} %copy.190, f32[3,64,64]{2,1,0:T(8,128)S(1)} %copy.191), kind=kLoop, calls=%fused_computation.51.clone.1 | loop fusion | flops 6803456 | bytes 2342912 | tf_op jit(solution)/shard_map/while/body/reduce_sum | solution.py:94
  335.0 4.9 multiply_reduce_fusion.2
  360.5 9.0 %fusion.134 = (f32[3,64,64]{2,1,0:T(8,128)S(1)}, f32[64,64,64]{2,1,0:T(8,128)}) fusion(f32[64,64,64]{2,1,0:T(8,128)} %multiply_multiply_fusion.22, f32[3,64,64]{2,1,0:T(8,128)S(1)} %copy.182, f32[3,64,64]{2,1,0:T(8,128)S(1)} %copy.183, f32[3,64,64]{2,1,0:T(8,128)S(1)} %copy.190, f32[3,64,64]{2,1,0:T(8,128)S(1)} %copy.191), kind=kLoop, calls=%fused_computation.51.clone.1 | loop fusion | flops 6803456 | bytes 2342912 | tf_op jit(solution)/shard_map/while/body/reduce_sum | solution.py:94
  395.1 9.0 %fusion.134 = (f32[3,64,64]{2,1,0:T(8,128)S(1)}, f32[64,64,64]{2,1,0:T(8,128)}) fusion(f32[64,64,64]{2,1,0:T(8,128)} %multiply_multiply_fusion.22, f32[3,64,64]{2,1,0:T(8,128)S(1)} %copy.182, f32[3,64,64]{2,1,0:T(8,128)S(1)} %copy.183, f32[3,64,64]{2,1,0:T(8,128)S(1)} %copy.190, f32[3,64,64]{2,1,0:T(8,128)S(1)} %copy.191), kind=kLoop, calls=%fused_computation.51.clone.1 | loop fusion | flops 6803456 | bytes 2342912 | tf_op jit(solution)/shard_map/while/body/reduce_sum | solution.py:94
  429.8 9.0 %fusion.134 = (f32[3,64,64]{2,1,0:T(8,128)S(1)}, f32[64,64,64]{2,1,0:T(8,128)}) fusion(f32[64,64,64]{2,1,0:T(8,128)} %multiply_multiply_fusion.22, f32[3,64,64]{2,1,0:T(8,128)S(1)} %copy.182, f32[3,64,64]{2,1,0:T(8,128)S(1)} %copy.183, f32[3,64,64]{2,1,0:T(8,128)S(1)} %copy.190, f32[3,64,64]{2,1,0:T(8,128)S(1)} %copy.191), kind=kLoop, calls=%fused_computation.51.clone.1 | loop fusion | flops 6803456 | bytes 2342912 | tf_op jit(solution)/shard_map/while/body/reduce_sum | solution.py:94
  438.9 4.9 multiply_reduce_fusion.2
  464.4 9.0 %fusion.134 = (f32[3,64,64]{2,1,0:T(8,128)S(1)}, f32[64,64,64]{2,1,0:T(8,128)}) fusion(f32[64,64,64]{2,1,0:T(8,128)} %multiply_multiply_fusion.22, f32[3,64,64]{2,1,0:T(8,128)S(1)} %copy.182, f32[3,64,64]{2,1,0:T(8,128)S(1)} %copy.183, f32[3,64,64]{2,1,0:T(8,128)S(1)} %copy.190, f32[3,64,64]{2,1,0:T(8,128)S(1)} %copy.191), kind=kLoop, calls=%fused_computation.51.clone.1 | loop fusion | flops 6803456 | bytes 2342912 | tf_op jit(solution)/shard_map/while/body/reduce_sum | solution.py:94
  499.0 9.0 %fusion.134 = (f32[3,64,64]{2,1,0:T(8,128)S(1)}, f32[64,64,64]{2,1,0:T(8,128)}) fusion(f32[64,64,64]{2,1,0:T(8,128)} %multiply_multiply_fusion.22, f32[3,64,64]{2,1,0:T(8,128)S(1)} %copy.182, f32[3,64,64]{2,1,0:T(8,128)S(1)} %copy.183, f32[3,64,64]{2,1,0:T(8,128)S(1)} %copy.190, f32[3,64,64]{2,1,0:T(8,128)S(1)} %copy.191), kind=kLoop, calls=%fused_computation.51.clone.1 | loop fusion | flops 6803456 | bytes 2342912 | tf_op jit(solution)/shard_map/while/body/reduce_sum | solution.py:94
  533.6 9.0 %fusion.134 = (f32[3,64,64]{2,1,0:T(8,128)S(1)}, f32[64,64,64]{2,1,0:T(8,128)}) fusion(f32[64,64,64]{2,1,0:T(8,128)} %multiply_multiply_fusion.22, f32[3,64,64]{2,1,0:T(8,128)S(1)} %copy.182, f32[3,64,64]{2,1,0:T(8,128)S(1)} %copy.183, f32[3,64,64]{2,1,0:T(8,128)S(1)} %copy.190, f32[3,64,64]{2,1,0:T(8,128)S(1)} %copy.191), kind=kLoop, calls=%fused_computation.51.clone.1 | loop fusion | flops 6803456 | bytes 2342912 | tf_op jit(solution)/shard_map/while/body/reduce_sum | solution.py:94
  568.3 9.0 %fusion.134 = (f32[3,64,64]{2,1,0:T(8,128)S(1)}, f32[64,64,64]{2,1,0:T(8,128)}) fusion(f32[64,64,64]{2,1,0:T(8,128)} %multiply_multiply_fusion.22, f32[3,64,64]{2,1,0:T(8,128)S(1)} %copy.182, f32[3,64,64]{2,1,0:T(8,128)S(1)} %copy.183, f32[3,64,64]{2,1,0:T(8,128)S(1)} %copy.190, f32[3,64,64]{2,1,0:T(8,128)S(1)} %copy.191), kind=kLoop, calls=%fused_computation.51.clone.1 | loop fusion | flops 6803456 | bytes 2342912 | tf_op jit(solution)/shard_map/while/body/reduce_sum | solution.py:94
  (662 shorter events, 331.7 us)
Async XLA Ops:
  14.4 10.4 %collective-permute-start = (f32[10,2048]{1,0:T(8,128)S(1)}, f32[10,2048]{1,0:T(8,128)S(1)}, u32[]{:S(2)}, u32[]{:S(2)}) collective-permute-start(f32[10,2048]{1,0:T(8,128)S(1)} %copy.142), channel_id=1, source_target_pairs={{0,16},{16,0},{4,20},{20,4},{8,24},{24,8},{12,28},{28,12},{1,17},{... | collective-permute-start | bytes 245768 | tf_op jit(solution)/shard_map/ppermute | solution.py:29
  44.6 5.0 collective-permute-start.1
  69.4 5.0 collective-permute-start.2
  94.2 5.0 collective-permute-start.3
  143.6 4.2 collective-permute-start.4
  147.8 8.3 %collective-permute-start.5 = (f32[8,1024]{1,0:T(8,128)S(1)}, f32[8,1024]{1,0:T(8,128)S(1)}, u32[]{:S(2)}, u32[]{:S(2)}) collective-permute-start(f32[8,1024]{1,0:T(8,128)S(1)} %collective-permute-done.4), channel_id=1, source_target_pairs={{0,3},{1,0},{2,1},{3,2},{4,7},{5,4},{6,5},{7,6},{8,11},{9,8},{10,9... | collective-permute-start | bytes 98312 | tf_op jit(solution)/shard_map/ppermute | solution.py:19
  150.3 5.7 collective-permute-start.6
  154.0 9.6 %collective-permute-start.9 = (f32[8,1024]{1,0:T(8,128)S(1)}, f32[8,1024]{1,0:T(8,128)S(1)}, u32[]{:S(2)}, u32[]{:S(2)}) collective-permute-start(f32[8,1024]{1,0:T(8,128)S(1)} %get-tuple-element.172), channel_id=1, source_target_pairs={{0,3},{1,0},{2,1},{3,2},{4,7},{5,4},{6,5},{7,6},{8,11},{9,8},{10,9... | collective-permute-start | bytes 98312 | tf_op jit(solution)/shard_map/ppermute | solution.py:19
  154.6 9.0 %collective-permute-start.10 = (f32[8,1024]{1,0:T(8,128)S(1)}, f32[8,1024]{1,0:T(8,128)S(1)}, u32[]{:S(2)}, u32[]{:S(2)}) collective-permute-start(f32[8,1024]{1,0:T(8,128)S(1)} %get-tuple-element.171), channel_id=1, source_target_pairs={{0,1},{1,2},{2,3},{3,0},{4,5},{5,6},{6,7},{7,4},{8,9},{9,10},{10,1... | collective-permute-start | bytes 98312 | tf_op jit(solution)/shard_map/ppermute | solution.py:19
  156.1 5.1 collective-permute-start.11
  156.1 5.5 collective-permute-start.14
  156.2 6.8 %collective-permute-start.8 = (f32[8,1024]{1,0:T(8,128)S(1)}, f32[8,1024]{1,0:T(8,128)S(1)}, u32[]{:S(2)}, u32[]{:S(2)}) collective-permute-start(f32[8,1024]{1,0:T(8,128)S(1)} %collective-permute-done.7), channel_id=1, source_target_pairs={{0,1},{1,2},{2,3},{3,0},{4,5},{5,6},{6,7},{7,4},{8,9},{9,10},{10,1... | collective-permute-start | bytes 98312 | tf_op jit(solution)/shard_map/ppermute | solution.py:19
  161.2 5.1 collective-permute-start.13
  163.0 4.8 collective-permute-start.15
  290.0 4.7 collective-permute-start.17
  290.7 4.0 collective-permute-start.18
  292.7 9.6 %collective-permute-start.21 = (f32[1,1024]{1,0:T(1,128)S(1)}, f32[1,1024]{1,0:T(1,128)S(1)}, u32[]{:S(2)}, u32[]{:S(2)}) collective-permute-start(f32[1,1024]{1,0:T(1,128)S(1)} %bitcast.208), channel_id=1, source_target_pairs={{0,3},{1,0},{2,1},{3,2},{4,7},{5,4},{6,5},{7,6},{8,11},{9,8},{10,9... | collective-permute-start | bytes 12296 | tf_op jit(solution)/shard_map/ppermute | solution.py:19
  293.0 9.2 %collective-permute-start.22 = (f32[1,1024]{1,0:T(1,128)S(1)}, f32[1,1024]{1,0:T(1,128)S(1)}, u32[]{:S(2)}, u32[]{:S(2)}) collective-permute-start(f32[1,1024]{1,0:T(1,128)S(1)} %bitcast.207), channel_id=1, source_target_pairs={{0,1},{1,2},{2,3},{3,0},{4,5},{5,6},{6,7},{7,4},{8,9},{9,10},{10,1... | collective-permute-start | bytes 12296 | tf_op jit(solution)/shard_map/ppermute | solution.py:19
  294.7 4.8 collective-permute-start.23
  294.7 4.9 collective-permute-start.26
  295.0 5.8 collective-permute-start.20
  299.5 4.8 collective-permute-start.25
  299.6 4.2 collective-permute-start.24
  300.9 4.5 collective-permute-start.27
  (90 other events, 630.6 us)
where the time goes:
time: 595 us; the launch traced here: 587 us
  other arithmetic  285 us (48%)
  local copies, waits for them, and re-layouts  219 us (37%)
  starting transfers between devices  29.5 us (5%)
  waiting for transfers between devices  27.7 us (5%)
  matrix products  21.1 us (4%)
    reduce_sum x8, other arithmetic, force_block(): acceleration = -jnp.sum(weight_pair[None] * offset, axis=3)  71.6 us
    gather x1, local copies, waits for them, and re-layouts, on_device(): ghost_density = to_neighbours(density_new[export_rows][:, None, :])[0]  45.5 us
    scatter x4, other arithmetic, on_device(): state.at[:, slots].set(jnp.where(taken[None, :], incoming, outgoing))  44.5 us
    reduce_sum x8, other arithmetic, force_block(): jnp.sum(weight_pair * jnp.sum(velocity_gap * offset, axis=0), axis=2)  39.3 us
    mul x8, other arithmetic, force_block(): PARTICLE_MASS * (target_press[:, :, None] + source_press[:, None, :])  38.9 us
    reduce_sum x16, other arithmetic, separation(): return (offset, jnp.sum(offset * offset, axis=0))  34.3 us
    add x32, local copies, waits for them, and re-layouts, force_block(): target_press[:, :, None] + source_press[:, None, :]  32.9 us
    gather x2, local copies, waits for them, and re-layouts, on_device(): ghost_out = jnp.moveaxis(jnp.take(fields, export_rows, axis=1), 1, 0)  32.9 us
  transfers between devices with their start and end apart: 28, of which 14 were waited for; matrix products, arithmetic and copies ran while one was open for 2% of the time, Pallas kernels for 0%

commit v1 on v0

v1 whole, which is shorter than its diff:
```python
import math

import jax
import jax.numpy as jnp
from jax import lax
from jax.experimental import pallas as pl
from jax.experimental.pallas import tpu as pltpu
from jax.sharding import PartitionSpec as P

TILE = 64
LANES = 128
UNROLL = 8

PARTICLE_MASS = 1.0 / 512.0
ADIABATIC = 5.0 / 3.0
F32 = jnp.float32
I32 = jnp.int32


def from_behind(value, axis, steps):
    count = lax.axis_size(axis)
    pairs = [(source, (source + steps) % count) for source in range(count)]
    return lax.ppermute(value, axis, pairs)


def from_partner(block, axis, bit):
    count = lax.axis_size(axis)
    route = []
    for low in range(count):
        high = low | 1 << bit
        if high != low and high < count:
            route += [(low, high), (high, low)]
    return lax.ppermute(block, axis, route)


def to_neighbours(low, middle, high, unit):
    low = from_behind(low, "gx", -1)
    high = from_behind(high, "gx", 1)
    down = jnp.concatenate([low[:unit], middle[:unit], high[:unit]], axis=0)
    up = jnp.concatenate([low[2 * unit :], middle[unit:], high[2 * unit :]], axis=0)
    down = from_behind(down, "gy", -1)
    up = from_behind(up, "gy", 1)
    return low, high, down, up


def ghost_place(unit):
    return ((2, 0), (0, unit), (3, 0), (2, unit), (3, unit), (2, 2 * unit), (1, unit), (3, 2 * unit))


def export_place(unit):
    return ((0, 0), (0, unit), (0, 2 * unit), (1, 0), (1, unit), (2, 0), (2, unit), (2, 2 * unit))


def lane_pick(table, index):
    return jnp.take_along_axis(table, index, axis=1, mode="promise_in_bounds")


def spread(row, rows=8):
    return jnp.broadcast_to(row, (rows, LANES))


def iota(shape, axis):
    return lax.broadcasted_iota(I32, shape, axis)


def aligned(value, size=8):
    return pl.multiple_of(value, size)


def gather_fields(field_ref, rows, block_count):
    high = [spread(row >> 7) for row in rows]
    low = [spread(row & 127) for row in rows]
    found = [jnp.zeros((8, LANES), F32) for _ in rows]
    for block in range(block_count):
        table = field_ref[:, LANES * block : LANES * (block + 1)]
        for u in range(len(rows)):
            found[u] = jnp.where(high[u] == block, lane_pick(table, low[u]), found[u])
    return found


def gather_outgoing(field_ref, flag_ref, send_ref, level, index_ref, out_ref):
    row_count = index_ref.shape[0]
    block_count = field_ref.shape[1] // LANES
    for j in range(row_count):
        index_ref[j : j + 1, :] = send_ref[level : level + 1, LANES * j : LANES * (j + 1)]

    def body(step, carry):
        rows = [index_ref[pl.ds(2 * step + u, 1), :] for u in range(2)]
        found = gather_fields(field_ref, rows, block_count)
        for u in range(2):
            out_ref[pl.ds(aligned((2 * step + u) * 8), 8), :] = found[u]
        return carry

    lax.fori_loop(0, row_count // 2, body, 0)
    base = 8 * row_count
    for part in range(row_count // 8):
        index = index_ref[8 * part : 8 * part + 8, :]
        high, low = index >> 7, index & 127
        found = jnp.zeros((8, LANES), F32)
        for block in range(block_count):
            table = spread(flag_ref[block : block + 1, :])
            found = jnp.where(high == block, lane_pick(table, low), found)
        out_ref[base + 8 * part : base + 8 * part + 8, :] = jnp.abs(found)
        out_ref[base + row_count + 8 * part : base + row_count + 8 * part + 8, :] = jnp.where(
            found > 0, 1.0, 0.0
        )


def apply_incoming(field_ref, flag_ref, inverse_ref, level, in_ref, new_field_ref, new_flag_ref, flag_in_ref):
    tile_rows = flag_ref.shape[0]
    in_blocks = flag_in_ref.shape[0]
    base = 8 * in_blocks
    density_in = in_ref[base : base + in_blocks, :]
    flag_in_ref[...] = jnp.where(
        in_ref[base + in_blocks : base + 2 * in_blocks, :] > 0.5, density_in, -density_in
    )
    first = level * tile_rows

    def body(step, carry):
        rows = [2 * step + u for u in range(2)]
        which = [inverse_ref[pl.ds(first + row, 1), :] - 1 for row in rows]
        high = [spread(w >> 7) for w in which]
        low = [spread(w & 127) for w in which]
        found = [field_ref[:, pl.ds(aligned(row * LANES, LANES), LANES)] for row in rows]
        for block in range(in_blocks):
            table = in_ref[8 * block : 8 * block + 8, :]
            for u in range(2):
                found[u] = jnp.where(high[u] == block, lane_pick(table, low[u]), found[u])
        for u in range(2):
            new_field_ref[:, pl.ds(aligned(rows[u] * LANES, LANES), LANES)] = found[u]
        return carry

    lax.fori_loop(0, tile_rows // 2, body, 0)

    for part in range(tile_rows // 8):
        which = inverse_ref[first + 8 * part : first + 8 * part + 8, :] - 1
        high, low = which >> 7, which & 127
        found = flag_ref[8 * part : 8 * part + 8, :]
        for block in range(in_blocks):
            table = spread(flag_in_ref[block : block + 1, :])
            found = jnp.where(high == block, lane_pick(table, low), found)
        new_flag_ref[8 * part : 8 * part + 8, :] = found


def first_kernel(field_ref, flag_ref, send_ref, out_ref, index_ref):
    gather_outgoing(field_ref, flag_ref, send_ref, 0, index_ref, out_ref)


def level_kernel(level, field_ref, flag_ref, inverse_ref, in_ref, send_ref, new_field_ref, new_flag_ref, out_ref, index_ref, flag_in_ref):
    apply_incoming(
        field_ref, flag_ref, inverse_ref, level, in_ref, new_field_ref, new_flag_ref, flag_in_ref
    )
    gather_outgoing(new_field_ref, new_flag_ref, send_ref, level + 1, index_ref, out_ref)


def last_kernel(level, field_ref, flag_ref, inverse_ref, in_ref, export_ref, new_field_ref, new_flag_ref, low_ref, middle_ref, high_ref, flag_in_ref):
    apply_incoming(
        field_ref, flag_ref, inverse_ref, level, in_ref, new_field_ref, new_flag_ref, flag_in_ref
    )
    outs = (low_ref, middle_ref, high_ref)
    blocks = export_ref.shape[1] // LANES
    block_count = field_ref.shape[1] // LANES
    place = export_place(8 * blocks)
    for number in range(8):
        target, start = place[number]

        def body(step, carry, number=number, target=target, start=start):
            rows = [
                export_ref[number : number + 1, pl.ds(aligned((2 * step + u) * LANES, LANES), LANES)]
                for u in range(2)
            ]
            found = gather_fields(new_field_ref, rows, block_count)
            for u in range(2):
                outs[target][pl.ds(aligned(start + (2 * step + u) * 8), 8), :] = found[u]
            return carry

        lax.fori_loop(0, blocks // 2, body, 0)


def inverse_kernel(count_ref, send_ref, inverse_ref):
    levels, slots = send_ref.shape
    tile_rows = inverse_ref.shape[0] // levels
    slot = iota((1, slots), 1)
    for level in range(levels):
        rows = send_ref[level : level + 1, :]
        taken = slot < count_ref[level]
        high = jnp.where(taken, rows >> 7, -1)
        low = rows & 127
        number = slot + 1
        hit = jnp.broadcast_to(high, (tile_rows, slots)) == iota((tile_rows, slots), 0)
        coarse = jnp.where(hit, jnp.broadcast_to((number >> 6).astype(F32), hit.shape), 0.0)
        fine = jnp.where(hit, jnp.broadcast_to((number & 63).astype(F32), hit.shape), 0.0)
        left = jnp.concatenate([coarse, fine], axis=0).astype(jnp.bfloat16)
        right = jnp.where(
            jnp.broadcast_to(low, (LANES, slots)) == iota((LANES, slots), 0), 1.0, 0.0
        ).astype(jnp.bfloat16)
        both = lax.dot_general(left, right, (((1,), (1,)), ((), ())), preferred_element_type=F32)
        total = both[:tile_rows] * 64.0 + both[tile_rows:]
        inverse_ref[level * tile_rows : (level + 1) * tile_rows, :] = total.astype(I32)


def target_kernel(field_ref, flag_ref, compact_ref, rank_ref, order_ref, chunks_ref, stack_ref):
    tile_rows = flag_ref.shape[0]
    groups = tile_rows // 16
    active = flag_ref[...] > 0
    ones = jnp.where(active, 1.0, 0.0).astype(jnp.bfloat16)
    a = iota((LANES, LANES), 0)
    b = iota((LANES, LANES), 1)
    same = (a >> 6) == (b >> 6)
    before = jnp.where(same & (a < b), 1.0, 0.0).astype(jnp.bfloat16)
    whole = jnp.where(same, 1.0, 0.0).astype(jnp.bfloat16)
    rank = jnp.dot(ones, before, preferred_element_type=F32).astype(I32)
    total = jnp.dot(ones, whole, preferred_element_type=F32)
    rank_ref[...] = rank
    chunks_ref[0] = (jnp.max(total).astype(I32) + 15) >> 4
    lane = iota((tile_rows, LANES), 1)
    code = jnp.where(active, lane + 128 * ((lane & 63) - rank), -1)
    for bit in range(6):
        moved = pltpu.roll(code, LANES - (1 << bit), 1)
        take = (moved >= 0) & (((moved >> (7 + bit)) & 1) == 1)
        keep = (code >= 0) & (((code >> (7 + bit)) & 1) == 0)
        code = jnp.where(take, moved, jnp.where(keep, code, -1))
    order_ref[...] = jnp.where(code >= 0, code & 127, lane)
    left_half = iota((8, LANES), 1) < 64
    for group in range(groups):
        for inner in range(16):
            row = group * 16 + inner
            stack_ref[8 * inner : 8 * inner + 8, :] = lane_pick(
                field_ref[:, LANES * row : LANES * (row + 1)], spread(order_ref[row : row + 1, :])
            )
        turned = jnp.transpose(stack_ref[...])
        for half in range(2):
            for chunk in range(4):
                first = half * 64 + chunk * 16
                near, far = turned[first : first + 8], turned[first + 8 : first + 16]
                for section in range(2):
                    if section == 0:
                        mixed = jnp.where(left_half, near, pltpu.roll(far, 64, 1))
                    else:
                        mixed = jnp.where(left_half, pltpu.roll(near, 64, 1), far)
                    place = (((chunk * groups + group) * 2 + section) * 2 + half) * 8
                    compact_ref[place : place + 8, :] = mixed


def expand_targets(compact_ref, chunk, groups, fields, emit):
    lane = iota((8, LANES), 1)
    half_base = jnp.where(lane < 64, 0, 64)
    for inner in range(8):
        for field in fields:
            index = half_base + (inner * 8 + field)
            for group in range(groups):
                for section in range(2):
                    for half in range(2):
                        place = ((group * 2 + section) * 2 + half) * 8
                        start = aligned(chunk * (groups * 32) + place)
                        tile = 2 * (group * 16 + section * 8 + inner) + half
                        emit(field, tile, lane_pick(compact_ref[pl.ds(start, 8), :], index))


def reduce_targets(sum_ref, first, tile_count, chunk, out_ref):
    lane = iota((8, LANES), 1)
    sub = iota((8, LANES), 0)
    left = lane < 64
    for block in range(tile_count // 16):
        near = jnp.zeros((8, LANES), F32)
        far = jnp.zeros((8, LANES), F32)
        for inner in range(16):
            place = first + (block * 16 + inner) * 8
            value = sum_ref[place : place + 8, :]
            here = lane == sub + inner * 8
            near_sum = jnp.sum(jnp.where(left, value, 0.0), axis=1, keepdims=True)
            far_sum = jnp.sum(jnp.where(left, 0.0, value), axis=1, keepdims=True)
            near = jnp.where(here, near_sum, near)
            far = jnp.where(here, far_sum, far)
        blocks = tile_count // 16
        out_ref[pl.ds((chunk * 2) * blocks + block, 1), :] = jnp.sum(near, axis=0, keepdims=True)
        out_ref[pl.ds((chunk * 2 + 1) * blocks + block, 1), :] = jnp.sum(far, axis=0, keepdims=True)


def place_results(red_ref, blocks, part, rank):
    row = iota((8, LANES), 0)
    half = iota((8, LANES), 1) >> 6
    index = (2 * row + half) * 8 + (rank & 7)
    which = rank >> 3
    found = jnp.zeros((8, LANES), F32)
    for section in range(8):
        table = spread(red_ref[section * blocks + part : section * blocks + part + 1, :])
        found = jnp.where(which == section, lane_pick(table, index), found)
    return found


def density_kernel(count_ref, chunks_ref, target_ref, source_ref, compact_ref, rank_ref, field_ref, flag_ref, low_ref, high_ref, down_ref, up_ref, export_ref,
                   density_ref, low_out, middle_out, high_out, pool_ref,
                   expanded_ref, sum_ref, red_ref, height_ref):
    tile_rows = flag_ref.shape[0]
    tile_count = 2 * tile_rows
    groups = tile_rows // 16
    region = (tile_count + 1) * 8
    left = iota((8, LANES), 1) < 64

    def write_doubled(row, value):
        other = pltpu.roll(value, 64, 1)
        pool_ref[pl.ds(aligned(row * 16), 8), :] = jnp.where(left, value, other)
        pool_ref[pl.ds(aligned(row * 16 + 8), 8), :] = jnp.where(left, other, value)

    for row in range(tile_rows):
        write_doubled(row, field_ref[:, LANES * row : LANES * (row + 1)])
        height_ref[row : row + 1, :] = field_ref[6:7, LANES * row : LANES * (row + 1)]
    ghosts = (low_ref, high_ref, down_ref, up_ref)
    unit = low_ref.shape[0] // 3
    place = ghost_place(unit)
    for number in range(8):
        which, start = place[number]
        for block in range(unit // 8):
            write_doubled(
                tile_rows + number * (unit // 8) + block,
                ghosts[which][start + 8 * block : start + 8 * block + 8, :],
            )

    def one_chunk(chunk, carry):
        order = {0: 0, 1: 1, 2: 2, 6: 3}

        def emit(field, tile, value):
            if field == 6:
                value = 1.0 / value
            first = order[field] * region + tile * 8
            expanded_ref[first : first + 8, :] = value

        expand_targets(compact_ref, chunk, groups, (0, 1, 2, 6), emit)
        for tile in range(tile_count):
            sum_ref[8 * tile : 8 * tile + 8, :] = jnp.zeros((8, LANES), F32)

        def step(number, inner_carry):
            results = []
            for u in range(UNROLL):
                target = aligned(target_ref[number * UNROLL + u])
                source = source_ref[number * UNROLL + u]

                def at(field, target=target):
                    return expanded_ref[pl.ds(aligned(target + field * region), 8), :]

                def source_row(field, source=source):
                    return pool_ref[pl.ds(source + field, 1), :]

                square = None
                for axis in range(3):
                    gap = at(axis) - source_row(axis)
                    gap = gap - jnp.floor(gap + 0.5)
                    square = gap * gap if square is None else square + gap * gap
                safe = jnp.maximum(square, 1.2e-38)
                ratio = safe * lax.rsqrt(safe) * at(3)
                outer = jnp.maximum(2.0 - ratio, 0.0)
                inner = jnp.maximum(1.0 - ratio, 0.0)
                results.append((target, 0.25 * (outer * outer * outer) - inner * inner * inner))
            for target, value in results:
                sum_ref[pl.ds(target, 8), :] += value
            return inner_carry

        lax.fori_loop(0, (count_ref[0] + UNROLL - 1) // UNROLL, step, 0)
        reduce_targets(sum_ref, 0, tile_count, chunk, red_ref)
        return carry

    lax.fori_loop(0, chunks_ref[0], one_chunk, 0)

    for part in range(tile_rows // 8):
        rank = rank_ref[8 * part : 8 * part + 8, :]
        found = place_results(red_ref, tile_count // 16, part, rank)
        height = height_ref[8 * part : 8 * part + 8, :]
        flag = flag_ref[8 * part : 8 * part + 8, :]
        norm = PARTICLE_MASS / (math.pi * height * height * height)
        density_ref[8 * part : 8 * part + 8, :] = jnp.where(
            flag > 0, norm * (1.0 + found), jnp.abs(flag)
        )
    outs = (low_out, middle_out, high_out)
    blocks = unit // 8
    place = export_place(blocks)
    for block in range(blocks):
        index = export_ref[:, LANES * block : LANES * (block + 1)]
        high, low = index >> 7, index & 127
        found = jnp.zeros((8, LANES), F32)
        for row in range(tile_rows):
            found = jnp.where(high == row, lane_pick(spread(density_ref[row : row + 1, :]), low), found)
        for number in range(8):
            which, start = place[number]
            outs[which][start + block : start + block + 1, :] = found[number : number + 1, :]


def force_kernel(count_ref, chunks_ref, target_ref, source_ref, compact_ref, rank_ref, order_ref, field_ref, flag_ref, density_ref, pool_ref, low_ref, high_ref, down_ref, up_ref,
                 accel_ref, heat_ref,
                 first_ref, second_ref, expanded_ref, sum_ref, red_ref, energy_ref, press_ref, press_compact_ref):
    tile_rows = flag_ref.shape[0]
    tile_count = 2 * tile_rows
    groups = tile_rows // 16
    region = (tile_count + 1) * 8
    left = iota((8, LANES), 1) < 64
    sub = iota((8, LANES), 0)
    slope_norm = 0.5 * PARTICLE_MASS / math.pi

    def derived(height):
        inverse = 1.0 / height
        square = inverse * inverse
        return inverse, slope_norm * (square * square * inverse)

    def sources(row, density_row):
        wide = spread(density_row)
        other = pltpu.roll(wide, 64, 1)
        for half in range(2):
            doubled = jnp.where(left, wide, other) if half == 0 else jnp.where(left, other, wide)
            start = aligned(row * 16 + half * 8)
            value = pool_ref[pl.ds(start, 8), :]
            inverse, norm = derived(value)
            first_ref[pl.ds(start, 8), :] = jnp.where(
                sub == 7, (ADIABATIC - 1.0) * value / doubled, jnp.where(sub == 6, inverse, value)
            )
            second_ref[pl.ds(start, 8), :] = jnp.where(
                sub == 6, norm, -0.75 * pltpu.roll(value, 1, 0)
            )

    for row in range(tile_rows):
        sources(row, density_ref[row : row + 1, :])
        energy_ref[row : row + 1, :] = field_ref[7:8, LANES * row : LANES * (row + 1)]
    ghosts = (low_ref, high_ref, down_ref, up_ref)
    unit = low_ref.shape[0] // 3
    place = ghost_place(unit)
    for number in range(8):
        which, start = place[number]
        for block in range(unit):
            sources(tile_rows + number * unit + block, ghosts[which][start + block : start + block + 1, :])

    for part in range(tile_rows // 8):
        rows = slice(8 * part, 8 * part + 8)
        press = (ADIABATIC - 1.0) * energy_ref[rows, :] / density_ref[rows, :]
        press_ref[rows, :] = lane_pick(press, order_ref[rows, :])
    press_ref[tile_rows:, :] = jnp.zeros((LANES - tile_rows, LANES), F32)
    turned = jnp.transpose(press_ref[...])
    for half in range(2):
        for chunk in range(4):
            first = half * 64 + chunk * 16
            near, far = turned[first : first + 8], turned[first + 8 : first + 16]
            place_at = (chunk * 2 + half) * 8
            press_compact_ref[place_at : place_at + 8, :] = jnp.where(left, near, pltpu.roll(far, 64, 1))

    half_base = jnp.where(left, 0, 64)

    def one_chunk(chunk, carry):
        def emit(field, tile, value):
            first = field * region + tile * 8
            if field == 6:
                inverse, norm = derived(value)
                expanded_ref[first : first + 8, :] = inverse
                expanded_ref[2 * region + first : 2 * region + first + 8, :] = norm
                expanded_ref[3 * region + first : 3 * region + first + 8, :] = -0.75 * value
            else:
                expanded_ref[first : first + 8, :] = value

        expand_targets(compact_ref, chunk, groups, range(7), emit)
        for row in range(tile_rows):
            for half in range(2):
                start = aligned(chunk * 16 + half * 8)
                first = 7 * region + (2 * row + half) * 8
                expanded_ref[first : first + 8, :] = lane_pick(
                    press_compact_ref[pl.ds(start, 8), :], half_base + row
                )
        for quantity in range(4):
            for tile in range(tile_count):
                first = quantity * region + 8 * tile
                sum_ref[first : first + 8, :] = jnp.zeros((8, LANES), F32)

        def step(number, inner_carry):
            results = []
            for u in range(UNROLL):
                target = aligned(target_ref[number * UNROLL + u])
                source = source_ref[number * UNROLL + u]

                def at(field, target=target):
                    return expanded_ref[pl.ds(aligned(target + field * region), 8), :]

                def source_row(field, source=source):
                    return first_ref[pl.ds(source + field, 1), :]

                def source_more(field, source=source):
                    return second_ref[pl.ds(source + field, 1), :]

                gaps = []
                square = None
                approach = None
                for axis in range(3):
                    gap = at(axis) - source_row(axis)
                    gap = gap - jnp.floor(gap + 0.5)
                    gaps.append(gap)
                    square = gap * gap if square is None else square + gap * gap
                    part = (at(3 + axis) - source_row(3 + axis)) * gap
                    approach = part if approach is None else approach + part
                safe = jnp.maximum(square, 1.2e-38)
                inverse_distance = lax.rsqrt(safe)
                distance = safe * inverse_distance

                def slope(inverse_height, norm, scaled_height):
                    ratio = distance * inverse_height
                    outer = jnp.maximum(2.0 - ratio, 0.0)
                    far = (outer * outer) * (inverse_distance * scaled_height)
                    return norm * jnp.where(ratio < 1.0, 2.25 * ratio - 3.0, far)

                total = slope(at(6), at(8), at(9)) + slope(
                    source_row(6), source_more(6), source_more(7)
                )
                weight = (at(7) + source_row(7)) * total
                results.append((target, [weight * gap for gap in gaps] + [weight * approach]))
            for target, values in results:
                for quantity in range(4):
                    sum_ref[pl.ds(aligned(target + quantity * region), 8), :] += values[quantity]
            return inner_carry

        lax.fori_loop(0, (count_ref[0] + UNROLL - 1) // UNROLL, step, 0)
        for quantity in range(4):
            reduce_targets(sum_ref, quantity * region, tile_count, chunk + 4 * quantity, red_ref)
        return carry

    lax.fori_loop(0, chunks_ref[0], one_chunk, 0)
    blocks = tile_count // 16
    for part in range(tile_rows // 8):
        rank = rank_ref[8 * part : 8 * part + 8, :]
        flag = flag_ref[8 * part : 8 * part + 8, :]
        for quantity in range(4):
            found = place_results(red_ref.at[pl.ds(quantity * 8 * blocks, 8 * blocks)], blocks, part, rank)
            if quantity == 3:
                heat_ref[8 * part : 8 * part + 8, :] = jnp.where(flag > 0, 0.5 * found, 0.0)
            else:
                found = jnp.where(flag > 0, -found, 0.0)
                for row in range(8):
                    at = LANES * (8 * part + row)
                    accel_ref[quantity : quantity + 1, at : at + LANES] = found[row : row + 1, :]


def call(kernel, outs, scratch, operands, scalars=0, scalar_outs=()):
    smem = pl.BlockSpec(memory_space=pltpu.SMEM)
    vmem = pl.BlockSpec(memory_space=pltpu.VMEM)
    return pl.pallas_call(
        kernel,
        out_shape=[jax.ShapeDtypeStruct(shape, dtype) for shape, dtype in outs],
        in_specs=[smem if i < scalars else vmem for i in range(len(operands))],
        out_specs=[smem if i in scalar_outs else vmem for i in range(len(outs))],
        scratch_shapes=[pltpu.VMEM(shape, dtype) for shape, dtype in scratch],
        compiler_params=pltpu.CompilerParams(vmem_limit_bytes=40 * 2**20),
    )(*operands)


def on_device(
    particles, old_density, active, send_rows, send_count, export_rows, pair_tiles, pair_count
):
    row_count = particles.shape[1]
    levels, slots = send_rows.shape
    ghosts = export_rows.shape[1]
    pair_total = pair_tiles.shape[1]
    tile_rows = row_count // LANES
    tile_count = 2 * tile_rows
    in_blocks = slots // LANES
    out_rows = 10 * in_blocks
    unit = 8 * (ghosts // LANES)
    dense_unit = ghosts // LANES
    bits_x = lax.axis_size("gx").bit_length() - 1
    bits_y = lax.axis_size("gy").bit_length() - 1

    flag = jnp.where(active == 1, old_density, -old_density).reshape(tile_rows, LANES)
    used = jnp.arange(pair_total) < pair_count[0]
    targets = jnp.where(used, pair_tiles[0], tile_count) * 8
    sources = pair_tiles[1] * 8
    state_shapes = [((8, row_count), F32), ((tile_rows, LANES), F32)]
    index_scratch = ((in_blocks, LANES), I32)
    flag_scratch = ((in_blocks, LANES), F32)

    fields = particles
    (outgoing,) = call(
        first_kernel, [((out_rows, LANES), F32)], [index_scratch], [fields, flag, send_rows]
    )
    (inverse,) = call(
        inverse_kernel,
        [((levels * tile_rows, LANES), I32)],
        [],
        [send_count[:, 0], send_rows],
        scalars=1,
    )
    for level in range(4):
        if level < 2:
            incoming = from_partner(outgoing, "gx", bits_x - 1 - level)
        else:
            incoming = from_partner(outgoing, "gy", bits_y + 1 - level)
        if level < 3:
            fields, flag, outgoing = call(
                lambda *refs, level=level: level_kernel(level, *refs),
                state_shapes + [((out_rows, LANES), F32)],
                [index_scratch, flag_scratch],
                [fields, flag, inverse, incoming, send_rows],
            )
        else:
            fields, flag, low, middle, high = call(
                lambda *refs, level=level: last_kernel(level, *refs),
                state_shapes
                + [((3 * unit, LANES), F32), ((2 * unit, LANES), F32), ((3 * unit, LANES), F32)],
                [flag_scratch],
                [fields, flag, inverse, incoming, export_rows],
            )
    low, high, down, up = to_neighbours(low, middle, high, unit)
    compact, rank, order, chunks = call(
        target_kernel,
        [
            ((4 * tile_count * 4, LANES), F32),
            ((tile_rows, LANES), I32),
            ((tile_rows, LANES), I32),
            ((1,), I32),
        ],
        [((LANES, LANES), F32)],
        [fields, flag],
        scalar_outs=(3,),
    )
    region = (tile_count + 1) * 8
    density, low_d, middle_d, high_d, pool = call(
        density_kernel,
        [
            ((tile_rows, LANES), F32),
            ((3 * dense_unit, LANES), F32),
            ((2 * dense_unit, LANES), F32),
            ((3 * dense_unit, LANES), F32),
            ((2 * (tile_rows + 8 * dense_unit) * 8, LANES), F32),
        ],
        [
            ((4 * region, LANES), F32),
            ((region, LANES), F32),
            ((8 * (tile_count // 16), LANES), F32),
            ((tile_rows, LANES), F32),
        ],
        [
            pair_count, chunks, targets, sources,
            compact, rank, fields, flag, low, high, down, up, export_rows,
        ],
        scalars=4,
    )
    low_d, high_d, down_d, up_d = to_neighbours(low_d, middle_d, high_d, dense_unit)
    pool_shape = ((2 * (tile_rows + 8 * dense_unit) * 8, LANES), F32)
    accel, heat = call(
        force_kernel,
        [((3, row_count), F32), ((tile_rows, LANES), F32)],
        [
            pool_shape,
            pool_shape,
            ((10 * region, LANES), F32),
            ((4 * region, LANES), F32),
            ((32 * (tile_count // 16), LANES), F32),
            ((tile_rows, LANES), F32),
            ((LANES, LANES), F32),
            ((64, LANES), F32),
        ],
        [
            pair_count, chunks, targets, sources,
            compact, rank, order, fields, flag, density, pool, low_d, high_d, down_d, up_d,
        ],
        scalars=4,
    )
    return (density.reshape(row_count), accel, heat.reshape(row_count))


def solution(mesh):
    in_specs = (
        P(None, ("gx", "gy")),
        P(("gx", "gy")),
        P(("gx", "gy")),
        P(None, ("gx", "gy")),
        P(None, ("gx", "gy")),
        P(None, ("gx", "gy")),
        P(None, ("gx", "gy")),
        P(("gx", "gy")),
    )
    out_specs = (P(("gx", "gy")), P(None, ("gx", "gy")), P(("gx", "gy")))
    return jax.shard_map(
        on_device, mesh=mesh, in_specs=in_specs, out_specs=out_specs, check_vma=False
    )
```

time: 595 us -> 111 us (0.19); the launches traced: 587 us -> 111 us
  other arithmetic: 285 us -> 0.82 us
  local copies, waits for them, and re-layouts: 219 us -> 0.99 us
  Pallas kernels: 0 us -> 64 us
  matrix products: 21.1 us -> 0 us
  starting transfers between devices: 29.5 us -> 14.4 us
    reduce_sum x40 -> x0, other arithmetic: 165 us -> none  [the longest x8 71.6 us: force_block(): acceleration = -jnp.sum(weight_pair[None] * offset, axis=3)]
    gather x7 -> x0, local copies, waits for them, and re-layouts: 109 us -> none  [the longest x1 45.5 us: on_device(): ghost_density = to_neighbours(density_new[export_rows][:, None, :])[0]]
    pallas_call x0 -> x9, Pallas kernels: none -> 64 us  [call(): pl.pallas_call(kernel, out_shape=[jax.ShapeDtypeStruct(shape, dtype) for...]
    mul x42 -> x2, other arithmetic: 45.3 us -> 0.01 us  [the longest x1 0.01 us: on_device(): sources = pair_tiles[1] * 8]
    scatter x4 -> x0, other arithmetic: 44.5 us -> none  [on_device(): state.at[:, slots].set(jnp.where(taken[None, :], incoming, outgoing))]
    add x32 -> x0, local copies, waits for them, and re-layouts: 32.9 us -> none  [force_block(): target_press[:, :, None] + source_press[:, None, :]]
    div x16 -> x0, local copies, waits for them, and re-layouts: 23.1 us -> none  [kernel_slope(): q = jnp.sqrt(dist_sq) / smooth]
    dot_general x48 -> x0, matrix products: 21.1 us -> none  [the longest x32 16.7 us: select_tiles(): jnp.dot(onehot, tile_matrix, precision=lax.Precision.HIGHEST, preferred_e...]
  transfers between devices with their start and end apart: 28 -> 12, of which waited for: 14 -> 12; matrix products, arithmetic and copies ran while one was open for 2% -> 0% of each run, Pallas kernels for 0% -> 2%
where the time goes in v1:
time: 111 us
  Pallas kernels  64 us (58%)
  waiting for transfers between devices  29.2 us (26%)
  starting transfers between devices  14.4 us (13%)
  between operations  1.43 us (1%)
    pallas_call x9, Pallas kernels, call(): pl.pallas_call(kernel, out_shape=[jax.ShapeDtypeStruct(shape, dtype) for...  64 us
    ppermute x8, waiting for transfers between devices, from_behind(): return lax.ppermute(value, axis, pairs)  17.8 us
    ppermute x4, waiting for transfers between devices, from_partner(): return lax.ppermute(block, axis, route)  11.3 us
    ppermute x4, starting transfers between devices, from_partner(): return lax.ppermute(block, axis, route)  8.4 us
    ppermute x8, starting transfers between devices, from_behind(): return lax.ppermute(value, axis, pairs)  5.96 us
  transfers between devices with their start and end apart: 12, of which 12 were waited for; matrix products, arithmetic and copies ran while one was open for 0% of the time, Pallas kernels for 2%

profile of v1, /device:TPU:0, one launch (start us, length us, event | category | flops | bytes accessed | tf_op | source)
XLA Modules:
  0.0 110.8 jit_solution(13260605703130214016)
XLA Ops:
  2.4 1.9 %shard_map.104 = f32[160,128]{1,0:T(8,128)S(1)} custom-call(f32[8,8192]{1,0:T(8,128)S(1)} %copy-done, f32[64,128]{1,0:T(8,128)S(1)} %fusion.flag_ref.refs_1_, s32[4,2048]{1,0:T(4,128)S(1)} %copy-done.2), custom_call_target="tpu_custom_call" | custom-call | tf_op jit(solution)/shard_map/pallas_call | solution.py:538
  4.3 4.1 %collective-permute-start = (f32[160,128]{1,0:T(8,128)S(1)}, f32[160,128]{1,0:T(8,128)S(1)}, u32[]{:S(2)}, u32[]{:S(2)}) collective-permute-start(f32[160,128]{1,0:T(8,128)S(1)} %shard_map.104), channel_id=1, source_target_pairs={{0,16},{16,0},{4,20},{20,4},{8,24},{24,8},{12,28},{28,12},{1,17},{... | collective-permute-start | bytes 245768 | tf_op jit(solution)/shard_map/ppermute | solution.py:33
  8.4 1.4 %shard_map.103.refs_2_ = s32[256,128]{1,0:T(8,128)S(1)} custom-call(s32[4]{0:T(128)S(1)} %bitcast.12, s32[4,2048]{1,0:T(4,128)S(1)} %copy-done.2), custom_call_target="tpu_custom_call" | custom-call | tf_op jit(solution)/shard_map/pallas_call | solution.py:538
  9.8 2.8 %collective-permute-done.refs_3_ = f32[160,128]{1,0:T(8,128)S(1)} collective-permute-done((f32[160,128]{1,0:T(8,128)S(1)}, f32[160,128]{1,0:T(8,128)S(1)}, u32[]{:S(2)}, u32[]{:S(2)}) %collective-permute-start) | collective-permute-done | bytes 81952 | tf_op jit(solution)/shard_map/ppermute | solution.py:33
  12.6 5.7 %shard_map.105 = (f32[8,8192]{1,0:T(8,128)S(1)}, f32[64,128]{1,0:T(8,128)S(1)}, f32[160,128]{1,0:T(8,128)S(1)}) custom-call(f32[8,8192]{1,0:T(8,128)S(1)} %copy-done.1, f32[64,128]{1,0:T(8,128)S(1)} %fusion.flag_ref.refs_1_, s32[256,128]{1,0:T(8,128)S(1)} %shard_map.103.refs_2_, f32[160,128]{1,0:T(8,128)S(1)} %collective-permute-done.refs_3_, ...), custom_call_target="tpu_custom_call" | custom-call | tf_op jit(solution)/shard_map/pallas_call | solution.py:538
  19.1 3.7 %collective-permute-done.1.refs_3_ = f32[160,128]{1,0:T(8,128)S(1)} collective-permute-done((f32[160,128]{1,0:T(8,128)S(1)}, f32[160,128]{1,0:T(8,128)S(1)}, u32[]{:S(2)}, u32[]{:S(2)}) %collective-permute-start.1) | collective-permute-done | bytes 81952 | tf_op jit(solution)/shard_map/ppermute | solution.py:33
  22.9 5.7 %shard_map.106 = (f32[8,8192]{1,0:T(8,128)S(1)}, f32[64,128]{1,0:T(8,128)S(1)}, f32[160,128]{1,0:T(8,128)S(1)}) custom-call(f32[8,8192]{1,0:T(8,128)S(1)} %get-tuple-element.28.refs_0_, f32[64,128]{1,0:T(8,128)S(1)} %get-tuple-element.29.refs_1_, s32[256,128]{1,0:T(8,128)S(1)} %shard_map.103.refs_2_, f32[160,128]{1,0:T(8,128)S(1)} %collective-permute-done.1.refs_3_, ...), custom_call_target="tpu_custom_call" | custom-call | tf_op jit(solution)/shard_map/pallas_call | solution.py:538
  28.6 1.8 %collective-permute-start.2 = (f32[160,128]{1,0:T(8,128)S(1)}, f32[160,128]{1,0:T(8,128)S(1)}, u32[]{:S(2)}, u32[]{:S(2)}) collective-permute-start(f32[160,128]{1,0:T(8,128)S(1)} %get-tuple-element.33), channel_id=1, source_target_pairs={{0,2},{2,0},{1,3},{3,1},{4,6},{6,4},{5,7},{7,5},{8,10},{10,8},{9,1... | collective-permute-start | bytes 245768 | tf_op jit(solution)/shard_map/ppermute | solution.py:33
  30.4 2.7 %collective-permute-done.2.refs_3_ = f32[160,128]{1,0:T(8,128)S(1)} collective-permute-done((f32[160,128]{1,0:T(8,128)S(1)}, f32[160,128]{1,0:T(8,128)S(1)}, u32[]{:S(2)}, u32[]{:S(2)}) %collective-permute-start.2) | collective-permute-done | bytes 81952 | tf_op jit(solution)/shard_map/ppermute | solution.py:33
  33.1 5.7 %shard_map.107 = (f32[8,8192]{1,0:T(8,128)S(1)}, f32[64,128]{1,0:T(8,128)S(1)}, f32[160,128]{1,0:T(8,128)S(1)}) custom-call(f32[8,8192]{1,0:T(8,128)S(1)} %get-tuple-element.31.refs_0_, f32[64,128]{1,0:T(8,128)S(1)} %get-tuple-element.32.refs_1_, s32[256,128]{1,0:T(8,128)S(1)} %shard_map.103.refs_2_, f32[160,128]{1,0:T(8,128)S(1)} %collective-permute-done.2.refs_3_, ...), custom_call_target="tpu_custom_call" | custom-call | tf_op jit(solution)/shard_map/pallas_call | solution.py:538
  38.8 1.7 %collective-permute-start.3 = (f32[160,128]{1,0:T(8,128)S(1)}, f32[160,128]{1,0:T(8,128)S(1)}, u32[]{:S(2)}, u32[]{:S(2)}) collective-permute-start(f32[160,128]{1,0:T(8,128)S(1)} %get-tuple-element.36), channel_id=1, source_target_pairs={{0,1},{1,0},{2,3},{3,2},{4,5},{5,4},{6,7},{7,6},{8,9},{9,8},{10,11... | collective-permute-start | bytes 245768 | tf_op jit(solution)/shard_map/ppermute | solution.py:33
  41.2 2.1 %collective-permute-done.3.refs_3_ = f32[160,128]{1,0:T(8,128)S(1)} collective-permute-done((f32[160,128]{1,0:T(8,128)S(1)}, f32[160,128]{1,0:T(8,128)S(1)}, u32[]{:S(2)}, u32[]{:S(2)}) %collective-permute-start.3) | collective-permute-done | bytes 81952 | tf_op jit(solution)/shard_map/ppermute | solution.py:33
  43.3 10.6 %shard_map.108 = (f32[8,8192]{1,0:T(8,128)S(1)}, f32[64,128]{1,0:T(8,128)S(1)}, f32[192,128]{1,0:T(8,128)S(1)}, f32[128,128]{1,0:T(8,128)S(1)}, f32[192,128]{1,0:T(8,128)S(1)}) custom-call(f32[8,8192]{1,0:T(8,128)S(1)} %get-tuple-element.34.refs_0_, f32[64,128]{1,0:T(8,128)S(1)} %get-tuple-element.35.refs_1_, s32[256,128]{1,0:T(8,128)S(1)} %shard_map.103.refs_2_, ...), custom_call_target="tpu_custom_call" | custom-call | tf_op jit(solution)/shard_map/pallas_call | solution.py:538
  54.6 2.5 %collective-permute-done.4.low_ref = f32[192,128]{1,0:T(8,128)S(1)} collective-permute-done((f32[192,128]{1,0:T(8,128)S(1)}, f32[192,128]{1,0:T(8,128)S(1)}, u32[]{:S(2)}, u32[]{:S(2)}) %collective-permute-start.4) | collective-permute-done | bytes 98336 | tf_op jit(solution)/shard_map/ppermute | solution.py:23
  57.0 3.9 %collective-permute-done.5.high_ref = f32[192,128]{1,0:T(8,128)S(1)} collective-permute-done((f32[192,128]{1,0:T(8,128)S(1)}, f32[192,128]{1,0:T(8,128)S(1)}, u32[]{:S(2)}, u32[]{:S(2)}) %collective-permute-start.5) | collective-permute-done | bytes 98336 | tf_op jit(solution)/shard_map/ppermute | solution.py:23
  60.9 2.8 %collective-permute-start.6 = (f32[192,128]{1,0:T(8,128)S(1)}, f32[192,128]{1,0:T(8,128)S(1)}, u32[]{:S(2)}, u32[]{:S(2)}) collective-permute-start(f32[192,128]{1,0:T(8,128)S(1)} %pad_maximum_fusion), channel_id=1, source_target_pairs={{0,3},{1,0},{2,1},{3,2},{4,7},{5,4},{6,5},{7,6},{8,11},{9,8},{10,9... | collective-permute-start | bytes 294920 | tf_op jit(solution)/shard_map/ppermute | solution.py:23
  63.8 1.0 shard_map.109
  64.8 1.1 %collective-permute-done.6.down_ref = f32[192,128]{1,0:T(8,128)S(1)} collective-permute-done((f32[192,128]{1,0:T(8,128)S(1)}, f32[192,128]{1,0:T(8,128)S(1)}, u32[]{:S(2)}, u32[]{:S(2)}) %collective-permute-start.6) | collective-permute-done | bytes 98336 | tf_op jit(solution)/shard_map/ppermute | solution.py:23
  65.9 3.4 %collective-permute-done.7.up_ref = f32[192,128]{1,0:T(8,128)S(1)} collective-permute-done((f32[192,128]{1,0:T(8,128)S(1)}, f32[192,128]{1,0:T(8,128)S(1)}, u32[]{:S(2)}, u32[]{:S(2)}) %collective-permute-start.7) | collective-permute-done | bytes 98336 | tf_op jit(solution)/shard_map/ppermute | solution.py:23
  69.3 11.7 %shard_map.110 = (f32[64,128]{1,0:T(8,128)}, f32[24,128]{1,0:T(8,128)S(1)}, f32[16,128]{1,0:T(8,128)S(1)}, f32[24,128]{1,0:T(8,128)S(1)}, f32[2048,128]{1,0:T(8,128)S(1)}) custom-call(s32[1]{0:T(128)} %copy.11.count_ref, s32[1]{0:T(128)} %get-tuple-element.39.chunks_ref, s32[512]{0:T(512)S(1)} %select_multiply_fusion.target_ref, s32[512]{0:T(512)S(1)} %bitcast.10, ...), custom_call_target="tpu_custom_call" | custom-call | tf_op jit(solution)/shard_map/pallas_call | solution.py:538
  82.4 3.5 %collective-permute-done.9.high_ref = f32[24,128]{1,0:T(8,128)S(1)} collective-permute-done((f32[24,128]{1,0:T(8,128)S(1)}, f32[24,128]{1,0:T(8,128)S(1)}, u32[]{:S(2)}, u32[]{:S(2)}) %collective-permute-start.9) | collective-permute-done | bytes 12320 | tf_op jit(solution)/shard_map/ppermute | solution.py:23
  86.0 2.0 %collective-permute-start.11 = (f32[24,128]{1,0:T(8,128)S(1)}, f32[24,128]{1,0:T(8,128)S(1)}, u32[]{:S(2)}, u32[]{:S(2)}) collective-permute-start(f32[24,128]{1,0:T(8,128)S(1)} %pad_maximum_fusion.3), channel_id=1, source_target_pairs={{0,1},{1,2},{2,3},{3,0},{4,5},{5,6},{6,7},{7,4},{8,9},{9,10},{10,1... | collective-permute-start | bytes 36872 | tf_op jit(solution)/shard_map/ppermute | solution.py:23
  88.0 1.7 %collective-permute-done.10.down_ref = f32[24,128]{1,0:T(8,128)S(1)} collective-permute-done((f32[24,128]{1,0:T(8,128)S(1)}, f32[24,128]{1,0:T(8,128)S(1)}, u32[]{:S(2)}, u32[]{:S(2)}) %collective-permute-start.10) | collective-permute-done | bytes 12320 | tf_op jit(solution)/shard_map/ppermute | solution.py:23
  90.6 20.2 %shard_map.111 = (f32[3,8192]{1,0:T(4,128)}, f32[64,128]{1,0:T(8,128)}) custom-call(s32[1]{0:T(128)} %copy.11.count_ref, s32[1]{0:T(128)} %get-tuple-element.39.chunks_ref, s32[512]{0:T(512)S(1)} %select_multiply_fusion.target_ref, s32[512]{0:T(512)S(1)} %bitcast.11, f32[2048,128]{1,0:T(8,128)S(1)} %get-tuple-element.40.compact_ref, ...), custom_call_target="tpu_custom_call" | custom-call | tf_op jit(solution)/shard_map/pallas_call | solution.py:538
  (36 shorter events, 5.6 us)
Async XLA Ops:
  0.6 0.8 copy-start.2
  1.4 1.0 copy-start
  2.4 10.2 %copy-start.1 = (f32[8,8192]{1,0:T(8,128)S(1)}, f32[8,8192]{1,0:T(8,128)}, u32[]{:S(2)}) copy-start(f32[8,8192]{1,0:T(8,128)} %refs_0_.1) | copy-start | bytes 786436
  4.3 4.1 %copy-start.5 = (s32[4,1]{0,1:T(1,128)S(1)}, s32[4,1]{0,1:T(1,128)}, u32[]{:S(2)}) copy-start(s32[4,1]{0,1:T(1,128)} %param.12) | copy-start | bytes 52
  4.3 8.3 %collective-permute-start = (f32[160,128]{1,0:T(8,128)S(1)}, f32[160,128]{1,0:T(8,128)S(1)}, u32[]{:S(2)}, u32[]{:S(2)}) collective-permute-start(f32[160,128]{1,0:T(8,128)S(1)} %shard_map.104), channel_id=1, source_target_pairs={{0,16},{16,0},{4,20},{20,4},{8,24},{24,8},{12,28},{28,12},{1,17},{... | collective-permute-start | bytes 245768 | tf_op jit(solution)/shard_map/ppermute | solution.py:33
  18.4 4.5 %collective-permute-start.1 = (f32[160,128]{1,0:T(8,128)S(1)}, f32[160,128]{1,0:T(8,128)S(1)}, u32[]{:S(2)}, u32[]{:S(2)}) collective-permute-start(f32[160,128]{1,0:T(8,128)S(1)} %get-tuple-element.30), channel_id=1, source_target_pairs={{0,8},{8,0},{4,12},{12,4},{16,24},{24,16},{20,28},{28,20},{1,9},{9... | collective-permute-start | bytes 245768 | tf_op jit(solution)/shard_map/ppermute | solution.py:33
  28.6 4.5 %collective-permute-start.2 = (f32[160,128]{1,0:T(8,128)S(1)}, f32[160,128]{1,0:T(8,128)S(1)}, u32[]{:S(2)}, u32[]{:S(2)}) collective-permute-start(f32[160,128]{1,0:T(8,128)S(1)} %get-tuple-element.33), channel_id=1, source_target_pairs={{0,2},{2,0},{1,3},{3,1},{4,6},{6,4},{5,7},{7,5},{8,10},{10,8},{9,1... | collective-permute-start | bytes 245768 | tf_op jit(solution)/shard_map/ppermute | solution.py:33
  33.1 7.5 %copy-start.6 = (s32[2,512]{1,0:T(2,128)S(1)}, s32[2,512]{1,0:T(2,128)}, u32[]{:S(2)}) copy-start(s32[2,512]{1,0:T(2,128)} %param.14) | copy-start | bytes 12292
  33.1 10.2 %copy-start.3 = (s32[8,1024]{1,0:T(8,128)S(1)}, s32[8,1024]{1,0:T(8,128)}, u32[]{:S(2)}) copy-start(s32[8,1024]{1,0:T(8,128)} %export_ref.1) | copy-start | bytes 98308
  38.8 4.5 %collective-permute-start.3 = (f32[160,128]{1,0:T(8,128)S(1)}, f32[160,128]{1,0:T(8,128)S(1)}, u32[]{:S(2)}, u32[]{:S(2)}) collective-permute-start(f32[160,128]{1,0:T(8,128)S(1)} %get-tuple-element.36), channel_id=1, source_target_pairs={{0,1},{1,0},{2,3},{3,2},{4,5},{5,4},{6,7},{7,6},{8,9},{9,8},{10,11... | collective-permute-start | bytes 245768 | tf_op jit(solution)/shard_map/ppermute | solution.py:33
  54.0 3.0 %collective-permute-start.4 = (f32[192,128]{1,0:T(8,128)S(1)}, f32[192,128]{1,0:T(8,128)S(1)}, u32[]{:S(2)}, u32[]{:S(2)}) collective-permute-start(f32[192,128]{1,0:T(8,128)S(1)} %get-tuple-element.42), channel_id=1, source_target_pairs={{0,28},{4,0},{8,4},{12,8},{16,12},{20,16},{24,20},{28,24},{1,29},{... | collective-permute-start | bytes 294920 | tf_op jit(solution)/shard_map/ppermute | solution.py:23
  54.1 6.8 %collective-permute-start.5 = (f32[192,128]{1,0:T(8,128)S(1)}, f32[192,128]{1,0:T(8,128)S(1)}, u32[]{:S(2)}, u32[]{:S(2)}) collective-permute-start(f32[192,128]{1,0:T(8,128)S(1)} %get-tuple-element.43), channel_id=1, source_target_pairs={{0,4},{4,8},{8,12},{12,16},{16,20},{20,24},{24,28},{28,0},{1,5},{5... | collective-permute-start | bytes 294920 | tf_op jit(solution)/shard_map/ppermute | solution.py:23
  60.9 5.0 %collective-permute-start.6 = (f32[192,128]{1,0:T(8,128)S(1)}, f32[192,128]{1,0:T(8,128)S(1)}, u32[]{:S(2)}, u32[]{:S(2)}) collective-permute-start(f32[192,128]{1,0:T(8,128)S(1)} %pad_maximum_fusion), channel_id=1, source_target_pairs={{0,3},{1,0},{2,1},{3,2},{4,7},{5,4},{6,5},{7,6},{8,11},{9,8},{10,9... | collective-permute-start | bytes 294920 | tf_op jit(solution)/shard_map/ppermute | solution.py:23
  63.7 5.6 %collective-permute-start.7 = (f32[192,128]{1,0:T(8,128)S(1)}, f32[192,128]{1,0:T(8,128)S(1)}, u32[]{:S(2)}, u32[]{:S(2)}) collective-permute-start(f32[192,128]{1,0:T(8,128)S(1)} %pad_maximum_fusion.1), channel_id=1, source_target_pairs={{0,1},{1,2},{2,3},{3,0},{4,5},{5,6},{6,7},{7,4},{8,9},{9,10},{10,1... | collective-permute-start | bytes 294920 | tf_op jit(solution)/shard_map/ppermute | solution.py:23
  81.0 1.4 %collective-permute-start.8 = (f32[24,128]{1,0:T(8,128)S(1)}, f32[24,128]{1,0:T(8,128)S(1)}, u32[]{:S(2)}, u32[]{:S(2)}) collective-permute-start(f32[24,128]{1,0:T(8,128)S(1)} %get-tuple-element.48), channel_id=1, source_target_pairs={{0,28},{4,0},{8,4},{12,8},{16,12},{20,16},{24,20},{28,24},{1,29},{... | collective-permute-start | bytes 36872 | tf_op jit(solution)/shard_map/ppermute | solution.py:23
  81.0 4.9 %collective-permute-start.9 = (f32[24,128]{1,0:T(8,128)S(1)}, f32[24,128]{1,0:T(8,128)S(1)}, u32[]{:S(2)}, u32[]{:S(2)}) collective-permute-start(f32[24,128]{1,0:T(8,128)S(1)} %get-tuple-element.49), channel_id=1, source_target_pairs={{0,4},{4,8},{8,12},{12,16},{16,20},{20,24},{24,28},{28,0},{1,5},{5... | collective-permute-start | bytes 36872 | tf_op jit(solution)/shard_map/ppermute | solution.py:23
  85.9 4.7 %copy-start.4 = (f32[64,128]{1,0:T(8,128)S(1)}, f32[64,128]{1,0:T(8,128)}, u32[]{:S(2)}) copy-start(f32[64,128]{1,0:T(8,128)} %get-tuple-element.45.density_ref) | copy-start | bytes 98308
  85.9 3.7 %collective-permute-start.10 = (f32[24,128]{1,0:T(8,128)S(1)}, f32[24,128]{1,0:T(8,128)S(1)}, u32[]{:S(2)}, u32[]{:S(2)}) collective-permute-start(f32[24,128]{1,0:T(8,128)S(1)} %pad_maximum_fusion.2), channel_id=1, source_target_pairs={{0,3},{1,0},{2,1},{3,2},{4,7},{5,4},{6,5},{7,6},{8,11},{9,8},{10,9... | collective-permute-start | bytes 36872 | tf_op jit(solution)/shard_map/ppermute | solution.py:23
  86.0 4.6 %collective-permute-start.11 = (f32[24,128]{1,0:T(8,128)S(1)}, f32[24,128]{1,0:T(8,128)S(1)}, u32[]{:S(2)}, u32[]{:S(2)}) collective-permute-start(f32[24,128]{1,0:T(8,128)S(1)} %pad_maximum_fusion.3), channel_id=1, source_target_pairs={{0,1},{1,2},{2,3},{3,0},{4,5},{5,6},{6,7},{7,4},{8,9},{9,10},{10,1... | collective-permute-start | bytes 36872 | tf_op jit(solution)/shard_map/ppermute | solution.py:23

commit v2 on v0

v2 whole, which is shorter than its diff:
```python
import math

import jax
import jax.numpy as jnp
from jax import lax
from jax.experimental import pallas as pl
from jax.experimental.pallas import tpu as pltpu
from jax.sharding import PartitionSpec as P

TILE = 64
LANES = 128
UNROLL = 8

PARTICLE_MASS = 1.0 / 512.0
ADIABATIC = 5.0 / 3.0
F32 = jnp.float32
I32 = jnp.int32


def from_behind(value, axis, steps):
    count = lax.axis_size(axis)
    pairs = [(source, (source + steps) % count) for source in range(count)]
    return lax.ppermute(value, axis, pairs)


def from_partner(block, axis, bit):
    count = lax.axis_size(axis)
    route = []
    for low in range(count):
        high = low | 1 << bit
        if high != low and high < count:
            route += [(low, high), (high, low)]
    return lax.ppermute(block, axis, route)


def along_x(low, high):
    return from_behind(low, "gx", -1), from_behind(high, "gx", 1)


def along_y(low, middle, high, unit):
    down = jnp.concatenate([low[:unit], middle[:unit], high[:unit]], axis=0)
    up = jnp.concatenate([low[2 * unit :], middle[unit:], high[2 * unit :]], axis=0)
    return from_behind(down, "gy", -1), from_behind(up, "gy", 1)


def ghost_place(unit):
    return ((2, 0), (0, unit), (3, 0), (2, unit), (3, unit), (2, 2 * unit), (1, unit), (3, 2 * unit))


def export_place(unit):
    return ((0, 0), (0, unit), (0, 2 * unit), (1, 0), (1, unit), (2, 0), (2, unit), (2, 2 * unit))


def lane_pick(table, index):
    return jnp.take_along_axis(table, index, axis=1, mode="promise_in_bounds")


def spread(row, rows=8):
    return jnp.broadcast_to(row, (rows, row.shape[1]))


def iota(shape, axis):
    return lax.broadcasted_iota(I32, shape, axis)


def aligned(value, size=8):
    return pl.multiple_of(value, size)


def pick_fields(tables, row, start):
    high, low = spread(row >> 7), spread(row & 127)
    found = start
    for block, table in enumerate(tables):
        found = jnp.where(high == block, lane_pick(table, low), found)
    return found


def pick_rows(table_refs, index, starts):
    high, low = index >> 7, index & 127
    found = list(starts)
    for block in range(table_refs[0].shape[0]):
        here = high == block
        for n, ref in enumerate(table_refs):
            found[n] = jnp.where(here, lane_pick(spread(ref[block : block + 1, :]), low), found[n])
    return found


def lane_blocks(ref):
    return [ref[:, LANES * b : LANES * (b + 1)] for b in range(ref.shape[1] // LANES)]


def row_blocks(ref, count):
    return [ref[8 * b : 8 * b + 8, :] for b in range(count)]


def stage_index(send_ref, level, index_ref):
    for j in range(index_ref.shape[0]):
        index_ref[j : j + 1, :] = send_ref[level : level + 1, LANES * j : LANES * (j + 1)]


def gather_outgoing(field_ref, flag_ref, index_ref, out_ref, inverse_ref=None, pick_ref=None):
    count = index_ref.shape[0]

    def body(step, carry):
        found = pick_fields(
            lane_blocks(field_ref), index_ref[pl.ds(step, 1), :], jnp.zeros((8, LANES), F32)
        )
        out_ref[pl.ds(aligned(step * 8), 8), :] = found
        return carry

    lax.fori_loop(0, count, body, 0, unroll=True)
    zero = jnp.zeros((8, LANES), F32)
    for part in range(count // 8):
        rows = slice(8 * part, 8 * part + 8)
        refs = [flag_ref] if inverse_ref is None else [flag_ref, inverse_ref]
        found = pick_rows(refs, index_ref[rows, :], [zero] * len(refs))
        first = 8 * count + 8 * part
        out_ref[first : first + 8, :] = jnp.abs(found[0])
        out_ref[first + count : first + count + 8, :] = jnp.where(found[0] > 0, 1.0, 0.0)
        if pick_ref is not None:
            pick_ref[rows, :] = found[1].astype(I32)


def apply_incoming(field_ref, flag_ref, inverse_ref, in_ref, new_field_ref, new_flag_ref, flag_in_ref):
    tile_rows = flag_ref.shape[0]
    count = flag_in_ref.shape[0]
    base = 8 * count
    density_in = in_ref[base : base + count, :]
    flag_in_ref[...] = jnp.where(in_ref[base + count : base + 2 * count, :] > 0.5, density_in, -density_in)

    def body(row, carry):
        where = pl.ds(aligned(row * LANES, LANES), LANES)
        slot = inverse_ref[pl.ds(row, 1), :].astype(I32) - 1
        new_field_ref[:, where] = pick_fields(row_blocks(in_ref, count), slot, field_ref[:, where])
        return carry

    lax.fori_loop(0, tile_rows, body, 0, unroll=16)
    for part in range(tile_rows // 8):
        rows = slice(8 * part, 8 * part + 8)
        slot = inverse_ref[rows, :].astype(I32) - 1
        new_flag_ref[rows, :] = pick_rows([flag_in_ref], slot, [flag_ref[rows, :]])[0]


def first_kernel(particle_ref, flag_ref, send_in_ref, field_ref, out_ref, send_ref, index_ref):
    stage_index(send_in_ref, 0, index_ref)
    gather_outgoing(particle_ref, flag_ref, index_ref, out_ref)
    field_ref[...] = particle_ref[...]
    send_ref[...] = send_in_ref[...]


def inverse_kernel(count_ref, send_ref, *inverse_refs):
    slots = send_ref.shape[1]
    slot = iota((1, slots), 1)
    for level, inverse_ref in enumerate(inverse_refs):
        tile_rows = inverse_ref.shape[0]
        rows = send_ref[level : level + 1, :]
        taken = slot < count_ref[level]
        high = jnp.where(taken, rows >> 7, -1)
        low = rows & 127
        number = slot + 1
        hit = spread(high, tile_rows) == iota((tile_rows, slots), 0)
        coarse = jnp.where(hit, spread((number >> 6).astype(F32), tile_rows), 0.0)
        fine = jnp.where(hit, spread((number & 63).astype(F32), tile_rows), 0.0)
        left = jnp.concatenate([coarse, fine], axis=0).astype(jnp.bfloat16)
        right = jnp.where(spread(low, LANES) == iota((LANES, slots), 0), 1.0, 0.0).astype(jnp.bfloat16)
        both = lax.dot_general(left, right, (((1,), (1,)), ((), ())), preferred_element_type=F32)
        inverse_ref[...] = both[:tile_rows] * 64.0 + both[tile_rows:]


def ahead_first_kernel(field_ref, flag_ref, inverse_ref, send_ref, partial_ref, pick_ref, index_ref):
    stage_index(send_ref, 1, index_ref)
    gather_outgoing(field_ref, flag_ref, index_ref, partial_ref, inverse_ref, pick_ref)


def ahead_kernel(level, field_ref, flag_ref, before_ref, in_ref, inverse_ref, send_ref, new_field_ref, new_flag_ref, partial_ref, pick_ref, index_ref, flag_in_ref):
    apply_incoming(field_ref, flag_ref, before_ref, in_ref, new_field_ref, new_flag_ref, flag_in_ref)
    stage_index(send_ref, level + 1, index_ref)
    gather_outgoing(new_field_ref, new_flag_ref, index_ref, partial_ref, inverse_ref, pick_ref)


def fix_kernel(partial_ref, pick_ref, in_ref, out_ref):
    count = pick_ref.shape[0]

    def body(step, carry):
        where = pl.ds(aligned(step * 8), 8)
        slot = pick_ref[pl.ds(step, 1), :] - 1
        out_ref[where, :] = pick_fields(row_blocks(in_ref, count), slot, partial_ref[where, :])
        return carry

    lax.fori_loop(0, count, body, 0, unroll=True)
    base = 8 * count
    for part in range(count // 8):
        slot = pick_ref[8 * part : 8 * part + 8, :] - 1
        tables = [in_ref.at[pl.ds(base, count)], in_ref.at[pl.ds(base + count, count)]]
        places = [slice(base + n * count + 8 * part, base + n * count + 8 * part + 8) for n in range(2)]
        found = pick_rows(tables, slot, [partial_ref[place, :] for place in places])
        for place, value in zip(places, found):
            out_ref[place, :] = value


def ahead_export_kernel(field_ref, flag_ref, before_ref, in_ref, inverse_ref, send_ref, last_ref, export_ref, new_field_ref, new_flag_ref, partial_ref, pick_ref, export_pick_ref, export_index_ref, index_ref, flag_in_ref):
    ahead_kernel(1, field_ref, flag_ref, before_ref, in_ref, inverse_ref, send_ref, new_field_ref, new_flag_ref, partial_ref, pick_ref, index_ref, flag_in_ref)
    zero = jnp.zeros((8, LANES), F32)
    blocks = export_ref.shape[1] // LANES
    for block in range(blocks):
        index = export_ref[:, LANES * block : LANES * (block + 1)]
        export_pick_ref[8 * block : 8 * block + 8, :] = pick_rows([last_ref], index, [zero])[0].astype(I32)
        for number in range(8):
            at = number * blocks + block
            export_index_ref[at : at + 1, :] = index[number : number + 1, :]


def ahead_last_kernel(field_ref, flag_ref, before_ref, in_ref, export_index_ref, new_field_ref, new_flag_ref, *rest):
    outs, flag_in_ref = rest[:3], rest[3]
    apply_incoming(field_ref, flag_ref, before_ref, in_ref, new_field_ref, new_flag_ref, flag_in_ref)
    blocks = export_index_ref.shape[0] // 8
    for target, (first, count) in enumerate(((0, 3), (3, 2), (5, 3))):

        def body(step, carry, target=target, first=first):
            row = export_index_ref[pl.ds(first * blocks + step, 1), :]
            outs[target][pl.ds(aligned(step * 8), 8), :] = pick_fields(
                lane_blocks(new_field_ref), row, jnp.zeros((8, LANES), F32)
            )
            return carry

        lax.fori_loop(0, count * blocks, body, 0, unroll=8)


def fix_last_kernel(low_ref, middle_ref, high_ref, pick_ref, in_ref, *outs):
    parts = (low_ref, middle_ref, high_ref)
    blocks = pick_ref.shape[0] // 8
    count = in_ref.shape[0] // 10
    for number, (target, start) in enumerate(export_place(8 * blocks)):
        for block in range(blocks):
            slot = pick_ref[8 * block + number : 8 * block + number + 1, :] - 1
            rows = slice(start + 8 * block, start + 8 * block + 8)
            outs[target][rows, :] = pick_fields(row_blocks(in_ref, count), slot, parts[target][rows, :])


EXPANDED = 9
SLOPE_NORM = 0.5 * PARTICLE_MASS / math.pi


def derived(height):
    inverse = 1.0 / height
    square = inverse * inverse
    return inverse, SLOPE_NORM * (square * square * inverse)


def expand_targets(compact_ref, chunk, base, expanded_ref):
    groups = compact_ref.shape[0] // (4 * 32)
    region = (groups * 32 + 1) * 8
    half_base = jnp.where(iota((8, LANES), 1) < 64, 0, 64)
    for inner in range(8):
        for field in range(7):
            index = half_base + (inner * 8 + field)
            for group in range(groups):
                for section in range(2):
                    for half in range(2):
                        place = ((group * 2 + section) * 2 + half) * 8
                        start = aligned(chunk * (groups * 32) + place)
                        tile = 2 * (group * 16 + section * 8 + inner) + half
                        value = lane_pick(compact_ref[pl.ds(start, 8), :], index)
                        first = base + field * region + tile * 8
                        if field == 6:
                            inverse, norm = derived(value)
                            expanded_ref[pl.ds(aligned(first), 8), :] = inverse
                            expanded_ref[pl.ds(aligned(first + region), 8), :] = norm
                            expanded_ref[pl.ds(aligned(first + 2 * region), 8), :] = -0.75 * value
                        else:
                            expanded_ref[pl.ds(aligned(first), 8), :] = value


def target_kernel(count_ref, field_ref, flag_ref, inverse_ref, in_ref, pair_ref,
                  new_field_ref, new_flag_ref, compact_ref, rank_ref, order_ref, list_ref, length_ref, expanded_ref,
                  flag_in_ref, stack_ref):
    apply_incoming(field_ref, flag_ref, inverse_ref, in_ref, new_field_ref, new_flag_ref, flag_in_ref)
    tile_rows = flag_ref.shape[0]
    groups = tile_rows // 16
    tile_count = 2 * tile_rows
    region = (tile_count + 1) * 8
    active = new_flag_ref[...] > 0
    ones = jnp.where(active, 1.0, 0.0).astype(jnp.bfloat16)
    a = iota((LANES, LANES), 0)
    b = iota((LANES, LANES), 1)
    same = (a >> 6) == (b >> 6)
    before = jnp.where(same & (a < b), 1.0, 0.0).astype(jnp.bfloat16)
    whole = jnp.where(same, 1.0, 0.0).astype(jnp.bfloat16)
    rank = jnp.dot(ones, before, preferred_element_type=F32).astype(I32)
    total = jnp.dot(ones, whole, preferred_element_type=F32)
    rank_ref[...] = rank
    lane = iota((tile_rows, LANES), 1)
    code = jnp.where(active, lane + 128 * ((lane & 63) - rank), -1)
    for bit in range(6):
        moved = pltpu.roll(code, LANES - (1 << bit), 1)
        take = (moved >= 0) & (((moved >> (7 + bit)) & 1) == 1)
        keep = (code >= 0) & (((code >> (7 + bit)) & 1) == 0)
        code = jnp.where(take, moved, jnp.where(keep, code, -1))
    order_ref[...] = jnp.where(code >= 0, code & 127, lane)
    left_half = iota((8, LANES), 1) < 64
    for group in range(groups):
        for inner in range(16):
            row = group * 16 + inner
            stack_ref[8 * inner : 8 * inner + 8, :] = lane_pick(
                new_field_ref[:, LANES * row : LANES * (row + 1)], spread(order_ref[row : row + 1, :])
            )
        turned = jnp.transpose(stack_ref[...])
        for half in range(2):
            for chunk in range(4):
                first = half * 64 + chunk * 16
                near, far = turned[first : first + 8], turned[first + 8 : first + 16]
                for section in range(2):
                    if section == 0:
                        mixed = jnp.where(left_half, near, pltpu.roll(far, 64, 1))
                    else:
                        mixed = jnp.where(left_half, pltpu.roll(near, 64, 1), far)
                    place = (((chunk * groups + group) * 2 + section) * 2 + half) * 8
                    compact_ref[place : place + 8, :] = mixed

    pairs = pair_ref.shape[1]
    slots = list_ref.shape[1]
    target, source = pair_ref[0:1, :], pair_ref[1:2, :]
    folded = jnp.where((lane & 63) == iota((tile_rows, LANES), 0), total, 0.0)
    totals = spread(jnp.sum(folded, axis=0, keepdims=True))
    place = spread((target & 1) * 64 + (target >> 1))
    need = jnp.concatenate(
        [lane_pick(totals, place[:, LANES * q : LANES * (q + 1)]) for q in range(pairs // LANES)], axis=1
    )
    sub = iota((8, pairs), 0)
    is_ghost = spread(source) >= tile_count
    member = (
        (iota((8, pairs), 1) < count_ref[0])
        & (need > (16 * (sub & 3)).astype(F32))
        & (is_ghost == (sub >= 4))
    )
    member_value = jnp.where(member, 1.0, 0.0)
    earlier = jnp.where(iota((pairs, pairs), 0) < iota((pairs, pairs), 1), 1.0, 0.0).astype(jnp.bfloat16)
    position = jnp.dot(member_value.astype(jnp.bfloat16), earlier, preferred_element_type=F32).astype(I32)
    length = jnp.broadcast_to(jnp.sum(member_value, axis=1, keepdims=True), (8, LANES)).astype(I32)
    length_ref[...] = length
    own_steps = ((length + (UNROLL - 1)) // UNROLL) * UNROLL
    base = jnp.where(iota((8, LANES), 0) >= 4, pltpu.roll(own_steps, 4, 0), 0)
    position = position + jnp.concatenate([base] * (pairs // LANES), axis=1)
    position = jnp.where(member, position, -1)
    local = jnp.where(source >= tile_count, source - tile_count, source)
    values = jnp.where(
        sub == 0, spread(target + 1), jnp.where(sub == 1, spread(local + 1), 0)
    ).astype(F32).astype(jnp.bfloat16)

    def make_list(chunk):
        row = jnp.maximum(position[chunk : chunk + 1, :], position[chunk + 4 : chunk + 5, :])
        hit = jnp.where(spread(row, slots) == iota((slots, pairs), 0), 1.0, 0.0).astype(jnp.bfloat16)
        found = lax.dot_general(
            values, hit, (((1,), (1,)), ((), ())), preferred_element_type=F32
        ).astype(I32)
        list_ref[chunk : chunk + 1, :] = jnp.where(found[0:1] > 0, found[0:1] - 1, tile_count) * 8
        list_ref[4 + chunk : 5 + chunk, :] = jnp.maximum(found[1:2] - 1, 0) * 8

    make_list(0)
    make_list(1)

    @pl.when(jnp.max(total) > 32.0)
    def _():
        make_list(2)
        make_list(3)

    def one_chunk(chunk, carry):
        expand_targets(compact_ref, chunk, aligned(chunk * (EXPANDED * region)), expanded_ref)
        return carry

    lax.fori_loop(0, 2, one_chunk, 0)


def reduce_targets(sum_ref, first, tile_count, section, out_ref):
    lane = iota((8, LANES), 1)
    sub = iota((8, LANES), 0)
    left = lane < 64
    blocks = tile_count // 16
    for block in range(blocks):
        near = jnp.zeros((8, LANES), F32)
        far = jnp.zeros((8, LANES), F32)
        for inner in range(16):
            place = first + (block * 16 + inner) * 8
            value = sum_ref[place : place + 8, :]
            here = lane == sub + inner * 8
            near_sum = jnp.sum(jnp.where(left, value, 0.0), axis=1, keepdims=True)
            far_sum = jnp.sum(jnp.where(left, 0.0, value), axis=1, keepdims=True)
            near = jnp.where(here, near_sum, near)
            far = jnp.where(here, far_sum, far)
        out_ref[pl.ds((section * 2) * blocks + block, 1), :] = jnp.sum(near, axis=0, keepdims=True)
        out_ref[pl.ds((section * 2 + 1) * blocks + block, 1), :] = jnp.sum(far, axis=0, keepdims=True)


def place_results(red_ref, blocks, part, rank):
    row = iota((8, LANES), 0)
    half = iota((8, LANES), 1) >> 6
    index = (2 * row + half) * 8 + (rank & 7)
    which = rank >> 3
    found = jnp.zeros((8, LANES), F32)
    for section in range(8):
        table = spread(red_ref[section * blocks + part : section * blocks + part + 1, :])
        found = jnp.where(which == section, lane_pick(table, index), found)
    return found


def clear(sum_ref, first, rows):
    for at in range(0, rows, 8):
        sum_ref[first + at : first + at + 8, :] = jnp.zeros((8, LANES), F32)


def steps_of(length):
    return (length + (UNROLL - 1)) // UNROLL


def span(length_ref, chunk, ghost):
    own = steps_of(length_ref[chunk, 0])
    if not ghost:
        return 0, own
    return own, own + steps_of(length_ref[chunk + 4, 0])


def double_into(pool_ref, row, value):
    left = iota((8, LANES), 1) < 64
    other = pltpu.roll(value, 64, 1)
    pool_ref[16 * row : 16 * row + 8, :] = jnp.where(left, value, other)
    pool_ref[16 * row + 8 : 16 * row + 16, :] = jnp.where(left, other, value)


def density_pairs(list_ref, length_ref, chunk, ghost, expanded_ref, base, region, pool_ref, sum_ref, sum_base):
    def step(number, carry):
        results = []
        for u in range(UNROLL):
            target = list_ref[chunk, number * UNROLL + u]
            source = list_ref[chunk + 4, number * UNROLL + u]

            def at(field, target=target):
                return expanded_ref[pl.ds(aligned(target + (base + field * region)), 8), :]

            square = None
            for axis in range(3):
                gap = at(axis) - pool_ref[pl.ds(source + axis, 1), :]
                gap = gap - jnp.floor(gap + 0.5)
                square = gap * gap if square is None else square + gap * gap
            safe = jnp.maximum(square, 1.2e-38)
            ratio = safe * lax.rsqrt(safe) * at(6)
            outer = jnp.maximum(2.0 - ratio, 0.0)
            inner = jnp.maximum(1.0 - ratio, 0.0)
            results.append((target, 0.25 * (outer * outer * outer) - inner * inner * inner))
        for target, value in results:
            sum_ref[pl.ds(aligned(target + sum_base), 8), :] += value
        return carry

    first, last = span(length_ref, chunk, ghost)
    lax.fori_loop(first, last, step, 0)


def density_own_kernel(list_ref, length_ref, field_ref, expanded_ref, pool_ref, sum_ref):
    tile_rows = field_ref.shape[1] // LANES
    region = (2 * tile_rows + 1) * 8
    for row in range(tile_rows):
        double_into(pool_ref, row, field_ref[:, LANES * row : LANES * (row + 1)])
    clear(sum_ref, 0, 2 * region)
    for chunk in range(2):
        density_pairs(
            list_ref, length_ref, chunk, False, expanded_ref, chunk * EXPANDED * region, region,
            pool_ref, sum_ref, chunk * region,
        )


def density_kernel(list_ref, length_ref, compact_ref, expanded_ref, own_pool_ref, own_sum_ref, rank_ref, field_ref, flag_ref, low_ref, high_ref, down_ref, up_ref, export_ref,
                   density_ref, low_out, middle_out, high_out, pool_ref,
                   sum_ref, red_ref, height_ref, spare_ref):
    tile_rows = flag_ref.shape[0]
    tile_count = 2 * tile_rows
    region = (tile_count + 1) * 8
    ghosts = (low_ref, high_ref, down_ref, up_ref)
    unit = low_ref.shape[0] // 3
    blocks = unit // 8
    for number, (which, start) in enumerate(ghost_place(unit)):
        for block in range(blocks):
            first = start + 8 * block
            double_into(pool_ref, number * blocks + block, ghosts[which][first : first + 8, :])
    sum_ref[...] = own_sum_ref[...]
    for chunk in range(2):
        density_pairs(
            list_ref, length_ref, chunk, True, expanded_ref, chunk * EXPANDED * region, region,
            pool_ref, sum_ref, chunk * region,
        )
        reduce_targets(sum_ref, chunk * region, tile_count, chunk, red_ref)
    for row in range(4 * (tile_count // 16), 8 * (tile_count // 16), 8):
        red_ref[row : row + 8, :] = jnp.zeros((8, LANES), F32)

    def rare_chunk(chunk, carry):
        @pl.when(length_ref[chunk, 0] + length_ref[chunk + 4, 0] > 0)
        def _():
            expand_targets(compact_ref, chunk, 0, spare_ref)
            clear(sum_ref, 0, region)
            density_pairs(list_ref, length_ref, chunk, False, spare_ref, 0, region, own_pool_ref, sum_ref, 0)
            density_pairs(list_ref, length_ref, chunk, True, spare_ref, 0, region, pool_ref, sum_ref, 0)
            reduce_targets(sum_ref, 0, tile_count, chunk, red_ref)

        return carry

    lax.fori_loop(2, 4, rare_chunk, 0)
    for row in range(tile_rows):
        height_ref[row : row + 1, :] = field_ref[6:7, LANES * row : LANES * (row + 1)]
    for part in range(tile_rows // 8):
        rows = slice(8 * part, 8 * part + 8)
        found = place_results(red_ref, tile_count // 16, part, rank_ref[rows, :])
        height = height_ref[rows, :]
        flag = flag_ref[rows, :]
        norm = PARTICLE_MASS / (math.pi * height * height * height)
        density_ref[rows, :] = jnp.where(flag > 0, norm * (1.0 + found), jnp.abs(flag))
    outs = (low_out, middle_out, high_out)
    zero = jnp.zeros((8, LANES), F32)
    for block in range(blocks):
        index = export_ref[:, LANES * block : LANES * (block + 1)]
        found = pick_rows([density_ref], index, [zero])[0]
        for number, (which, start) in enumerate(export_place(blocks)):
            outs[which][start + block : start + block + 1, :] = found[number : number + 1, :]


def source_tables(pool_ref, tile, first_ref, second_ref, density=None):
    sub = iota((8, LANES), 0)
    rows = slice(8 * tile, 8 * tile + 8)
    value = pool_ref[rows, :]
    inverse, norm = derived(value)
    press = (ADIABATIC - 1.0) * value
    if density is not None:
        press = press / density
    first_ref[rows, :] = jnp.where(sub == 7, press, jnp.where(sub == 6, inverse, value))
    second_ref[rows, :] = jnp.where(sub == 6, norm, -0.75 * pltpu.roll(value, 1, 0))


def doubled_halves(row):
    left = iota((8, LANES), 1) < 64
    wide = spread(row)
    other = pltpu.roll(wide, 64, 1)
    return jnp.where(left, wide, other), jnp.where(left, other, wide)


def force_pairs(list_ref, length_ref, chunk, ghost, expanded_ref, base, region, press_ref, press_base, first_ref, second_ref, sum_ref):
    def step(number, carry):
        results = []
        for u in range(UNROLL):
            target = list_ref[chunk, number * UNROLL + u]
            source = list_ref[chunk + 4, number * UNROLL + u]

            def at(field, target=target):
                return expanded_ref[pl.ds(aligned(target + (base + field * region)), 8), :]

            def source_row(field, source=source):
                return first_ref[pl.ds(source + field, 1), :]

            def source_more(field, source=source):
                return second_ref[pl.ds(source + field, 1), :]

            gaps = []
            square = None
            approach = None
            for axis in range(3):
                gap = at(axis) - source_row(axis)
                gap = gap - jnp.floor(gap + 0.5)
                gaps.append(gap)
                square = gap * gap if square is None else square + gap * gap
                part = (at(3 + axis) - source_row(3 + axis)) * gap
                approach = part if approach is None else approach + part
            safe = jnp.maximum(square, 1.2e-38)
            inverse_distance = lax.rsqrt(safe)
            distance = safe * inverse_distance

            def slope(inverse_height, norm, scaled_height):
                ratio = distance * inverse_height
                outer = jnp.maximum(2.0 - ratio, 0.0)
                far = (outer * outer) * (inverse_distance * scaled_height)
                return norm * jnp.where(ratio < 1.0, 2.25 * ratio - 3.0, far)

            total = slope(at(6), at(7), at(8)) + slope(source_row(6), source_more(6), source_more(7))
            press = press_ref[pl.ds(aligned(target + press_base), 8), :] + source_row(7)
            weight = press * total
            results.append((target, [weight * gap for gap in gaps] + [weight * approach]))
        for target, values in results:
            for quantity in range(4):
                sum_ref[pl.ds(aligned(target + quantity * region), 8), :] += values[quantity]
        return carry

    first, last = span(length_ref, chunk, ghost)
    lax.fori_loop(first, last, step, 0)


def expand_press(press_compact_ref, chunk, tile_rows, press_ref, base):
    half_base = jnp.where(iota((8, LANES), 1) < 64, 0, 64)
    for row in range(tile_rows):
        for half in range(2):
            start = aligned(chunk * 16 + half * 8)
            first = base + (2 * row + half) * 8
            press_ref[first : first + 8, :] = lane_pick(
                press_compact_ref[pl.ds(start, 8), :], half_base + row
            )


def force_own_kernel(list_ref, length_ref, density_ref, field_ref, order_ref, expanded_ref, pool_ref,
                     first_ref, second_ref, press_compact_ref, press_ref, sum_ref,
                     energy_ref, ordered_ref):
    tile_rows = density_ref.shape[0]
    tile_count = 2 * tile_rows
    region = (tile_count + 1) * 8
    left = iota((8, LANES), 1) < 64
    for row in range(tile_rows):
        near, far = doubled_halves(density_ref[row : row + 1, :])
        source_tables(pool_ref, 2 * row, first_ref, second_ref, near)
        source_tables(pool_ref, 2 * row + 1, first_ref, second_ref, far)
        energy_ref[row : row + 1, :] = field_ref[7:8, LANES * row : LANES * (row + 1)]
    for part in range(tile_rows // 8):
        rows = slice(8 * part, 8 * part + 8)
        press = (ADIABATIC - 1.0) * energy_ref[rows, :] / density_ref[rows, :]
        ordered_ref[rows, :] = lane_pick(press, order_ref[rows, :])
    ordered_ref[tile_rows:, :] = jnp.zeros((LANES - tile_rows, LANES), F32)
    turned = jnp.transpose(ordered_ref[...])
    for half in range(2):
        for chunk in range(4):
            first = half * 64 + chunk * 16
            near, far = turned[first : first + 8], turned[first + 8 : first + 16]
            place_at = (chunk * 2 + half) * 8
            press_compact_ref[place_at : place_at + 8, :] = jnp.where(left, near, pltpu.roll(far, 64, 1))
    for chunk in range(2):
        expand_press(press_compact_ref, chunk, tile_rows, press_ref, chunk * region)
    clear(sum_ref, 0, 4 * region)
    force_pairs(
        list_ref, length_ref, 0, False, expanded_ref, 0, region, press_ref, 0, first_ref, second_ref, sum_ref
    )


def force_own_more_kernel(list_ref, length_ref, expanded_ref, press_ref, own_first_ref, own_second_ref, pool_ref,
                          sum_ref, first_ref, second_ref):
    region = sum_ref.shape[0] // 4
    for tile in range(pool_ref.shape[0] // 8):
        source_tables(pool_ref, tile, first_ref, second_ref)
    clear(sum_ref, 0, 4 * region)
    force_pairs(
        list_ref, length_ref, 1, False, expanded_ref, EXPANDED * region, region, press_ref, region,
        own_first_ref, own_second_ref, sum_ref,
    )


def force_kernel(list_ref, length_ref, compact_ref, expanded_ref, press_compact_ref, press_ref, rank_ref, flag_ref, own_first_ref, own_second_ref, half_ref, second_ref, zero_sum_ref, one_sum_ref, low_ref, high_ref, down_ref, up_ref,
                 accel_ref, heat_ref,
                 first_ref, sum_ref, red_ref, spare_ref, spare_press_ref):
    tile_rows = flag_ref.shape[0]
    tile_count = 2 * tile_rows
    region = (tile_count + 1) * 8
    blocks = tile_count // 16
    is_press = iota((8, LANES), 0) == 7
    ghosts = (low_ref, high_ref, down_ref, up_ref)
    unit = low_ref.shape[0] // 3
    for number, (which, start) in enumerate(ghost_place(unit)):
        for block in range(unit):
            row = number * unit + block
            for half, density in enumerate(doubled_halves(ghosts[which][start + block : start + block + 1, :])):
                rows = slice(16 * row + 8 * half, 16 * row + 8 * half + 8)
                value = half_ref[rows, :]
                first_ref[rows, :] = jnp.where(is_press, value / density, value)
    for chunk in range(2):
        sum_ref[...] = (zero_sum_ref if chunk == 0 else one_sum_ref)[...]
        force_pairs(
            list_ref, length_ref, chunk, True, expanded_ref, chunk * EXPANDED * region, region,
            press_ref, chunk * region, first_ref, second_ref, sum_ref,
        )
        for quantity in range(4):
            reduce_targets(sum_ref, quantity * region, tile_count, chunk + 4 * quantity, red_ref)
    for quantity in range(4):
        for row in range(4 * blocks, 8 * blocks, 8):
            at = quantity * 8 * blocks + row
            red_ref[at : at + 8, :] = jnp.zeros((8, LANES), F32)

    def rare_chunk(chunk, carry):
        @pl.when(length_ref[chunk, 0] + length_ref[chunk + 4, 0] > 0)
        def _():
            expand_targets(compact_ref, chunk, 0, spare_ref)
            expand_press(press_compact_ref, chunk, tile_rows, spare_press_ref, 0)
            clear(sum_ref, 0, 4 * region)
            force_pairs(
                list_ref, length_ref, chunk, False, spare_ref, 0, region, spare_press_ref, 0,
                own_first_ref, own_second_ref, sum_ref,
            )
            force_pairs(
                list_ref, length_ref, chunk, True, spare_ref, 0, region, spare_press_ref, 0,
                first_ref, second_ref, sum_ref,
            )
            for quantity in range(4):
                reduce_targets(sum_ref, quantity * region, tile_count, chunk + 4 * quantity, red_ref)

        return carry

    lax.fori_loop(2, 4, rare_chunk, 0)
    for part in range(tile_rows // 8):
        rank = rank_ref[8 * part : 8 * part + 8, :]
        flag = flag_ref[8 * part : 8 * part + 8, :]
        for quantity in range(4):
            found = place_results(red_ref.at[pl.ds(quantity * 8 * blocks, 8 * blocks)], blocks, part, rank)
            if quantity == 3:
                heat_ref[8 * part : 8 * part + 8, :] = jnp.where(flag > 0, 0.5 * found, 0.0)
            else:
                found = jnp.where(flag > 0, -found, 0.0)
                for row in range(8):
                    at = LANES * (8 * part + row)
                    accel_ref[quantity : quantity + 1, at : at + LANES] = found[row : row + 1, :]


def call(kernel, outs, scratch, operands, scalars=0):
    smem = pl.BlockSpec(memory_space=pltpu.SMEM)
    vmem = pl.BlockSpec(memory_space=pltpu.VMEM)
    return pl.pallas_call(
        kernel,
        out_shape=[jax.ShapeDtypeStruct(shape, dtype) for shape, dtype in outs],
        in_specs=[smem if i < scalars else vmem for i in range(len(operands))],
        out_specs=[vmem] * len(outs),
        scratch_shapes=[pltpu.VMEM(shape, dtype) for shape, dtype in scratch],
        compiler_params=pltpu.CompilerParams(vmem_limit_bytes=24 * 2**20),
    )(*operands)


def on_device(
    particles, old_density, active, send_rows, send_count, export_rows, pair_tiles, pair_count
):
    row_count = particles.shape[1]
    levels, slots = send_rows.shape
    ghosts = export_rows.shape[1]
    pair_total = pair_tiles.shape[1]
    tile_rows = row_count // LANES
    tile_count = 2 * tile_rows
    in_blocks = slots // LANES
    unit = 8 * (ghosts // LANES)
    dense_unit = ghosts // LANES
    region = (tile_count + 1) * 8
    list_slots = -(-(pair_total + 2 * UNROLL) // LANES) * LANES
    bits_x = lax.axis_size("gx").bit_length() - 1
    bits_y = lax.axis_size("gy").bit_length() - 1

    row = ((tile_rows, LANES), F32)
    whole = ((8, row_count), F32)
    offered = ((10 * in_blocks, LANES), F32)
    picked = ((in_blocks, LANES), I32)
    index_scratch = ((in_blocks, LANES), I32)
    flag_scratch = ((in_blocks, LANES), F32)
    exported = [((3 * unit, LANES), F32), ((2 * unit, LANES), F32), ((3 * unit, LANES), F32)]

    def swap(block, level):
        if level < 2:
            return from_partner(block, "gx", bits_x - 1 - level)
        return from_partner(block, "gy", bits_y + 1 - level)

    flag = jnp.where(active == 1, old_density, -old_density).reshape(tile_rows, LANES)
    fields, outgoing, send_rows = call(
        first_kernel,
        [whole, offered, (send_rows.shape, I32)],
        [index_scratch],
        [particles, flag, send_rows],
    )
    incoming = swap(outgoing, 0)
    inverse = call(inverse_kernel, [row] * levels, [], [send_count[:, 0], send_rows], scalars=1)
    partial, pick = call(
        ahead_first_kernel, [offered, picked], [index_scratch], [fields, flag, inverse[0], send_rows]
    )
    (outgoing,) = call(fix_kernel, [offered], [], [partial, pick, incoming])
    before = incoming
    incoming = swap(outgoing, 1)
    fields, flag, partial, pick, export_pick, export_index = call(
        ahead_export_kernel,
        [whole, row, offered, picked, ((8 * dense_unit, LANES), I32), ((8 * dense_unit, LANES), I32)],
        [index_scratch, flag_scratch],
        [fields, flag, inverse[0], before, inverse[1], send_rows, inverse[3], export_rows],
    )
    (outgoing,) = call(fix_kernel, [offered], [], [partial, pick, incoming])
    before = incoming
    incoming = swap(outgoing, 2)
    fields, flag, partial, pick = call(
        lambda *refs: ahead_kernel(2, *refs),
        [whole, row, offered, picked],
        [index_scratch, flag_scratch],
        [fields, flag, inverse[1], before, inverse[2], send_rows],
    )
    (outgoing,) = call(fix_kernel, [offered], [], [partial, pick, incoming])
    before = incoming
    incoming = swap(outgoing, 3)
    fields, flag, low, middle, high = call(
        ahead_last_kernel,
        [whole, row] + exported,
        [flag_scratch],
        [fields, flag, inverse[2], before, export_index],
    )
    low, middle, high = call(
        fix_last_kernel, exported, [], [low, middle, high, export_pick, incoming]
    )
    low, high = along_x(low, high)
    fields, flag, compact, rank, order, lists, lengths, expanded = call(
        target_kernel,
        [
            whole,
            row,
            ((8 * tile_rows, LANES), F32),
            ((tile_rows, LANES), I32),
            ((tile_rows, LANES), I32),
            ((8, list_slots), I32),
            ((8, LANES), I32),
            ((2 * EXPANDED * region, LANES), F32),
        ],
        [flag_scratch, ((LANES, LANES), F32)],
        [pair_count, fields, flag, inverse[3], incoming, pair_tiles],
        scalars=1,
    )
    low, high, lengths = lax.optimization_barrier((low, high, lengths))
    down, up = along_y(low, middle, high, unit)
    pool_shape = ((tile_count * 8, LANES), F32)
    ghost_pool_shape = ((2 * 8 * dense_unit * 8, LANES), F32)
    own_pool, own_sum = call(
        density_own_kernel,
        [pool_shape, ((2 * region, LANES), F32)],
        [],
        [lists, lengths, fields, expanded],
        scalars=2,
    )
    density, low_d, middle_d, high_d, ghost_pool = call(
        density_kernel,
        [
            row,
            ((3 * dense_unit, LANES), F32),
            ((2 * dense_unit, LANES), F32),
            ((3 * dense_unit, LANES), F32),
            ghost_pool_shape,
        ],
        [
            ((2 * region, LANES), F32),
            ((8 * (tile_count // 16), LANES), F32),
            row,
            ((EXPANDED * region, LANES), F32),
        ],
        [
            lists, lengths, compact, expanded, own_pool, own_sum,
            rank, fields, flag, low, high, down, up, export_rows,
        ],
        scalars=2,
    )
    low_d, high_d = along_x(low_d, high_d)
    sums = ((4 * region, LANES), F32)
    own_first, own_second, press_compact, press, zero_sum = call(
        force_own_kernel,
        [pool_shape, pool_shape, ((64, LANES), F32), ((2 * region, LANES), F32), sums],
        [row, ((LANES, LANES), F32)],
        [lists, lengths, density, fields, order, expanded, own_pool],
        scalars=2,
    )
    low_d, high_d, press = lax.optimization_barrier((low_d, high_d, press))
    down_d, up_d = along_y(low_d, middle_d, high_d, dense_unit)
    one_sum, ghost_first, ghost_second = call(
        force_own_more_kernel,
        [sums, ghost_pool_shape, ghost_pool_shape],
        [],
        [lists, lengths, expanded, press, own_first, own_second, ghost_pool],
        scalars=2,
    )
    accel, heat = call(
        force_kernel,
        [((3, row_count), F32), row],
        [
            ghost_pool_shape,
            sums,
            ((32 * (tile_count // 16), LANES), F32),
            ((EXPANDED * region, LANES), F32),
            ((region, LANES), F32),
        ],
        [
            lists, lengths, compact, expanded, press_compact, press, rank, flag,
            own_first, own_second, ghost_first, ghost_second, zero_sum, one_sum,
            low_d, high_d, down_d, up_d,
        ],
        scalars=2,
    )
    return (density.reshape(row_count), accel, heat.reshape(row_count))


def solution(mesh):
    in_specs = (
        P(None, ("gx", "gy")),
        P(("gx", "gy")),
        P(("gx", "gy")),
        P(None, ("gx", "gy")),
        P(None, ("gx", "gy")),
        P(None, ("gx", "gy")),
        P(None, ("gx", "gy")),
        P(("gx", "gy")),
    )
    out_specs = (P(("gx", "gy")), P(None, ("gx", "gy")), P(("gx", "gy")))
    return jax.shard_map(
        on_device, mesh=mesh, in_specs=in_specs, out_specs=out_specs, check_vma=False
    )
```

time: 595 us -> 77.7 us (0.13); the launches traced: 587 us -> 76.9 us
  other arithmetic: 285 us -> 0.81 us
  local copies, waits for them, and re-layouts: 219 us -> 3.91 us
  Pallas kernels: 0 us -> 52.1 us
  waiting for transfers between devices: 27.7 us -> 4.08 us
  matrix products: 21.1 us -> 0 us
  starting transfers between devices: 29.5 us -> 14.5 us
    reduce_sum x40 -> x0, other arithmetic: 165 us -> none  [the longest x8 71.6 us: force_block(): acceleration = -jnp.sum(weight_pair[None] * offset, axis=3)]
    gather x7 -> x0, local copies, waits for them, and re-layouts: 109 us -> none  [the longest x1 45.5 us: on_device(): ghost_density = to_neighbours(density_new[export_rows][:, None, :])[0]]
    pallas_call x0 -> x16, Pallas kernels: none -> 52.1 us  [call(): pl.pallas_call(kernel, out_shape=[jax.ShapeDtypeStruct(shape, dtype) for...]
    mul x42 -> x0, other arithmetic: 45.3 us -> none  [the longest x8 38.9 us: force_block(): PARTICLE_MASS * (target_press[:, :, None] + source_press[:, None, :])]
    scatter x4 -> x0, other arithmetic: 44.5 us -> none  [on_device(): state.at[:, slots].set(jnp.where(taken[None, :], incoming, outgoing))]
    add x32 -> x0, local copies, waits for them, and re-layouts: 32.9 us -> none  [force_block(): target_press[:, :, None] + source_press[:, None, :]]
    div x16 -> x0, local copies, waits for them, and re-layouts: 23.1 us -> none  [kernel_slope(): q = jnp.sqrt(dist_sq) / smooth]
    dot_general x48 -> x0, matrix products: 21.1 us -> none  [the longest x32 16.7 us: select_tiles(): jnp.dot(onehot, tile_matrix, precision=lax.Precision.HIGHEST, preferred_e...]
  transfers between devices with their start and end apart: 28 -> 12, of which waited for: 14 -> 4; matrix products, arithmetic and copies ran while one was open for 2% -> 0% of each run, Pallas kernels for 0% -> 43%
where the time goes in v2:
time: 77.7 us; the launch traced here: 76.9 us
  Pallas kernels  52.1 us (67%)
  starting transfers between devices  14.5 us (19%)
  waiting for transfers between devices  4.08 us (5%)
  local copies, waits for them, and re-layouts  3.91 us (5%)
  between operations  1.46 us (2%)
  other arithmetic  0.81 us (1%)
    pallas_call x16, Pallas kernels, call(): pl.pallas_call(kernel, out_shape=[jax.ShapeDtypeStruct(shape, dtype) for...  52.1 us
    ppermute x4, starting transfers between devices, from_partner(): return lax.ppermute(block, axis, route)  8.25 us
    ppermute x8, starting transfers between devices, from_behind(): return lax.ppermute(value, axis, pairs)  6.28 us
    unnamed x14, local copies, waits for them, and re-layouts  3.88 us
    ppermute x8, waiting for transfers between devices, from_behind(): return lax.ppermute(value, axis, pairs)  3.42 us
  transfers between devices with their start and end apart: 12, of which 4 were waited for; matrix products, arithmetic and copies ran while one was open for 0% of the time, Pallas kernels for 43%

profile of v2, /device:TPU:0, one launch (start us, length us, event | category | flops | bytes accessed | tf_op | source)
XLA Modules:
  0.0 76.9 jit_solution(14194733691672378495)
XLA Ops:
  0.6 0.8 %fusion.flag_ref = f32[64,128]{1,0:T(8,128)S(1)} fusion(f32[8192]{0:T(1024)} %param.9, s32[8192]{0:T(1024)} %param.10), kind=kLoop, calls=%fused_computation.3 | loop fusion | flops 24576 | bytes 98304 | tf_op jit(solution)/shard_map/reshape | solution.py:753
  1.4 0.9 %copy-done = f32[8,8192]{1,0:T(8,128)S(1)} copy-done((f32[8,8192]{1,0:T(8,128)S(1)}, f32[8,8192]{1,0:T(8,128)}, u32[]{:S(2)}) %copy-start) | copy-done | bytes 262168
  3.1 1.3 %shard_map.103 = (f32[8,8192]{1,0:T(8,128)S(1)}, f32[160,128]{1,0:T(8,128)S(1)}, s32[4,2048]{1,0:T(4,128)S(1)}) custom-call(f32[8,8192]{1,0:T(8,128)S(1)} %copy-done, f32[64,128]{1,0:T(8,128)S(1)} %fusion.flag_ref, s32[4,2048]{1,0:T(4,128)S(1)} %copy-done.4), custom_call_target="tpu_custom_call" | custom-call | tf_op jit(solution)/shard_map/pallas_call | solution.py:713
  4.5 4.1 %collective-permute-start = (f32[160,128]{1,0:T(8,128)S(1)}, f32[160,128]{1,0:T(8,128)S(1)}, u32[]{:S(2)}, u32[]{:S(2)}) collective-permute-start(f32[160,128]{1,0:T(8,128)S(1)} %get-tuple-element.64), channel_id=1, source_target_pairs={{0,16},{16,0},{4,20},{20,4},{8,24},{24,8},{12,28},{28,12},{1,17},{... | collective-permute-start | bytes 245768 | tf_op jit(solution)/shard_map/ppermute | solution.py:33
  9.2 1.4 %shard_map.104 = (f32[64,128]{1,0:T(8,128)S(1)}, f32[64,128]{1,0:T(8,128)S(1)}, f32[64,128]{1,0:T(8,128)S(1)}, f32[64,128]{1,0:T(8,128)S(1)}) custom-call(s32[4]{0:T(128)S(1)} %bitcast.6, s32[4,2048]{1,0:T(4,128)S(1)} %get-tuple-element.62.send_ref.refs_5_), custom_call_target="tpu_custom_call" | custom-call | tf_op jit(solution)/shard_map/pallas_call | solution.py:713
  10.7 1.5 %shard_map.106 = (f32[160,128]{1,0:T(8,128)S(1)}, s32[16,128]{1,0:T(8,128)S(1)}) custom-call(f32[8,8192]{1,0:T(8,128)S(1)} %get-tuple-element.61.field_ref, f32[64,128]{1,0:T(8,128)S(1)} %fusion.flag_ref, f32[64,128]{1,0:T(8,128)S(1)} %get-tuple-element.63.before_ref.inverse_ref, s32[4,2048]{1,0:T(4,128)S(1)} %get-tuple-element.62.send_ref.refs_5_), custom_call_target="tpu_custom_call" | custom-call | tf_op jit(solution)/shard_map/pallas_call | solution.py:713
  13.2 1.0 %collective-permute-start.1 = (f32[160,128]{1,0:T(8,128)S(1)}, f32[160,128]{1,0:T(8,128)S(1)}, u32[]{:S(2)}, u32[]{:S(2)}) collective-permute-start(f32[160,128]{1,0:T(8,128)S(1)} %shard_map.107), channel_id=1, source_target_pairs={{0,8},{8,0},{4,12},{12,4},{16,24},{24,16},{20,28},{28,20},{1,9},{9... | collective-permute-start | bytes 245768 | tf_op jit(solution)/shard_map/ppermute | solution.py:33
  15.0 3.8 %shard_map.105 = (f32[8,8192]{1,0:T(8,128)S(1)}, f32[64,128]{1,0:T(8,128)S(1)}, f32[160,128]{1,0:T(8,128)S(1)}, s32[16,128]{1,0:T(8,128)S(1)}, s32[64,128]{1,0:T(8,128)S(1)}, /*index=5*/s32[64,128]{1,0:T(8,128)S(1)}) custom-call(f32[8,8192]{1,0:T(8,128)S(1)} %get-tuple-element.61.field_ref, f32[64,128]{1,0:T(8,128)S(1)} %fusion.flag_ref, ...), custom_call_target="tpu_custom_call" | custom-call | tf_op jit(solution)/shard_map/pallas_call | solution.py:713
  19.3 1.6 %collective-permute-start.2 = (f32[160,128]{1,0:T(8,128)S(1)}, f32[160,128]{1,0:T(8,128)S(1)}, u32[]{:S(2)}, u32[]{:S(2)}) collective-permute-start(f32[160,128]{1,0:T(8,128)S(1)} %shard_map.109), channel_id=1, source_target_pairs={{0,2},{2,0},{1,3},{3,1},{4,6},{6,4},{5,7},{7,5},{8,10},{10,8},{9,1... | collective-permute-start | bytes 245768 | tf_op jit(solution)/shard_map/ppermute | solution.py:33
  20.8 3.2 %shard_map.108 = (f32[8,8192]{1,0:T(8,128)S(1)}, f32[64,128]{1,0:T(8,128)S(1)}, f32[160,128]{1,0:T(8,128)S(1)}, s32[16,128]{1,0:T(8,128)S(1)}) custom-call(f32[8,8192]{1,0:T(8,128)S(1)} %get-tuple-element.67.refs_0_, f32[64,128]{1,0:T(8,128)S(1)} %get-tuple-element.68.refs_1_, f32[64,128]{1,0:T(8,128)S(1)} %get-tuple-element.65.inverse_ref.refs_2_, ...), custom_call_target="tpu_custom_call" | custom-call | tf_op jit(solution)/shard_map/pallas_call | solution.py:713
  24.5 1.6 %collective-permute-start.3 = (f32[160,128]{1,0:T(8,128)S(1)}, f32[160,128]{1,0:T(8,128)S(1)}, u32[]{:S(2)}, u32[]{:S(2)}) collective-permute-start(f32[160,128]{1,0:T(8,128)S(1)} %shard_map.111), channel_id=1, source_target_pairs={{0,1},{1,0},{2,3},{3,2},{4,5},{5,4},{6,7},{7,6},{8,9},{9,8},{10,11... | collective-permute-start | bytes 245768 | tf_op jit(solution)/shard_map/ppermute | solution.py:33
  26.7 6.9 %shard_map.110 = (f32[8,8192]{1,0:T(8,128)S(1)}, f32[64,128]{1,0:T(8,128)S(1)}, f32[192,128]{1,0:T(8,128)S(1)}, f32[128,128]{1,0:T(8,128)S(1)}, f32[192,128]{1,0:T(8,128)S(1)}) custom-call(f32[8,8192]{1,0:T(8,128)S(1)} %get-tuple-element.72.field_ref, f32[64,128]{1,0:T(8,128)S(1)} %get-tuple-element.73.flag_ref, ...), custom_call_target="tpu_custom_call" | custom-call | tf_op jit(solution)/shard_map/pallas_call | solution.py:713
  33.7 1.4 %shard_map.113 = (f32[192,128]{1,0:T(8,128)S(1)}, f32[128,128]{1,0:T(8,128)S(1)}, f32[192,128]{1,0:T(8,128)S(1)}) custom-call(f32[192,128]{1,0:T(8,128)S(1)} %get-tuple-element.82.low_ref, f32[128,128]{1,0:T(8,128)S(1)} %get-tuple-element.83.middle_ref, f32[192,128]{1,0:T(8,128)S(1)} %get-tuple-element.84.high_ref, ...), custom_call_target="tpu_custom_call" | custom-call | tf_op jit(solution)/shard_map/pallas_call | solution.py:713
  35.0 1.6 %collective-permute-start.4 = (f32[192,128]{1,0:T(8,128)S(1)}, f32[192,128]{1,0:T(8,128)S(1)}, u32[]{:S(2)}, u32[]{:S(2)}) collective-permute-start(f32[192,128]{1,0:T(8,128)S(1)} %get-tuple-element.86), channel_id=1, source_target_pairs={{0,28},{4,0},{8,4},{12,8},{16,12},{20,16},{24,20},{28,24},{1,29},{... | collective-permute-start | bytes 294920 | tf_op jit(solution)/shard_map/ppermute | solution.py:23
  36.6 5.4 %shard_map.112 = (f32[8,8192]{1,0:T(8,128)S(1)}, f32[64,128]{1,0:T(8,128)S(1)}, f32[512,128]{1,0:T(8,128)S(1)}, s32[64,128]{1,0:T(8,128)S(1)}, s32[64,128]{1,0:T...) custom-call(s32[1]{0:T(128)S(6)} %copy.11.count_ref, ...), custom_call_target="tpu_custom_call" | custom-call | tf_op jit(solution)/shard_map/pallas_call | solution.py:713
  43.1 1.5 %collective-permute-start.7 = (f32[192,128]{1,0:T(8,128)S(1)}, f32[192,128]{1,0:T(8,128)S(1)}, u32[]{:S(2)}, u32[]{:S(2)}) collective-permute-start(f32[192,128]{1,0:T(8,128)S(1)} %pad_maximum_fusion.1), channel_id=1, source_target_pairs={{0,1},{1,2},{2,3},{3,0},{4,5},{5,6},{6,7},{7,4},{8,9},{9,10},{10,1... | collective-permute-start | bytes 294920 | tf_op jit(solution)/shard_map/ppermute | solution.py:23
  44.6 3.8 %shard_map.114 = (f32[1024,128]{1,0:T(8,128)S(1)}, f32[2064,128]{1,0:T(8,128)S(1)}) custom-call(s32[8,640]{1,0:T(8,128)S(1)} %get-tuple-element.81.list_ref, s32[8,128]{1,0:T(8,128)S(1)} %get-tuple-element.89.length_ref, f32[8,8192]{1,0:T(8,128)S(1)} %get-tuple-element.92.field_ref, f32[18576,128]{1,0:T(8,128)S(1)} %get-tuple-element.91.expanded_ref), custom_call_target="tpu_custom_call" | custom-call | tf_op jit(solution)/shard_map/pallas_call | solution.py:713
  48.4 1.3 %collective-permute-done.7.up_ref = f32[192,128]{1,0:T(8,128)S(1)} collective-permute-done((f32[192,128]{1,0:T(8,128)S(1)}, f32[192,128]{1,0:T(8,128)S(1)}, u32[]{:S(2)}, u32[]{:S(2)}) %collective-permute-start.7) | collective-permute-done | bytes 98336 | tf_op jit(solution)/shard_map/ppermute | solution.py:23
  49.7 5.7 %shard_map.115 = (f32[64,128]{1,0:T(8,128)}, f32[24,128]{1,0:T(8,128)S(1)}, f32[16,128]{1,0:T(8,128)S(1)}, f32[24,128]{1,0:T(8,128)S(1)}, f32[1024,128]{1,0:T(8,128)S(1)}) custom-call(s32[8,640]{1,0:T(8,128)S(1)} %get-tuple-element.81.list_ref, s32[8,128]{1,0:T(8,128)S(1)} %get-tuple-element.89.length_ref, f32[512,128]{1,0:T(8,128)S(1)} %get-tuple-element.90.compact_ref, ...), custom_call_target="tpu_custom_call" | custom-call | tf_op jit(solution)/shard_map/pallas_call | solution.py:713
  56.7 5.0 %shard_map.116 = (f32[1024,128]{1,0:T(8,128)S(1)}, f32[1024,128]{1,0:T(8,128)S(1)}, f32[64,128]{1,0:T(8,128)S(1)}, f32[2064,128]{1,0:T(8,128)S(1)}, f32[4128,128]{1,0:T(8,128)S(1)}) custom-call(s32[8,640]{1,0:T(8,128)S(1)} %get-tuple-element.81.list_ref, s32[8,128]{1,0:T(8,128)S(1)} %get-tuple-element.89.length_ref, f32[64,128]{1,0:T(8,128)S(1)} %copy-done.3, ...), custom_call_target="tpu_custom_call" | custom-call | tf_op jit(solution)/shard_map/pallas_call | solution.py:713
  61.7 1.5 %collective-permute-start.10 = (f32[24,128]{1,0:T(8,128)S(1)}, f32[24,128]{1,0:T(8,128)S(1)}, u32[]{:S(2)}, u32[]{:S(2)}) collective-permute-start(f32[24,128]{1,0:T(8,128)S(1)} %pad_maximum_fusion.2), channel_id=1, source_target_pairs={{0,3},{1,0},{2,1},{3,2},{4,7},{5,4},{6,5},{7,6},{8,11},{9,8},{10,9... | collective-permute-start | bytes 36872 | tf_op jit(solution)/shard_map/ppermute | solution.py:23
  63.8 2.3 %shard_map.117 = (f32[4128,128]{1,0:T(8,128)S(1)}, f32[1024,128]{1,0:T(8,128)S(1)}, f32[1024,128]{1,0:T(8,128)S(1)}) custom-call(s32[8,640]{1,0:T(8,128)S(1)} %get-tuple-element.81.list_ref, s32[8,128]{1,0:T(8,128)S(1)} %get-tuple-element.89.length_ref, f32[18576,128]{1,0:T(8,128)S(1)} %get-tuple-element.91.expanded_ref, ...), custom_call_target="tpu_custom_call" | custom-call | tf_op jit(solution)/shard_map/pallas_call | solution.py:713
  66.2 1.7 %collective-permute-done.11.up_ref = f32[24,128]{1,0:T(8,128)S(1)} collective-permute-done((f32[24,128]{1,0:T(8,128)S(1)}, f32[24,128]{1,0:T(8,128)S(1)}, u32[]{:S(2)}, u32[]{:S(2)}) %collective-permute-start.11) | collective-permute-done | bytes 12320 | tf_op jit(solution)/shard_map/ppermute | solution.py:23
  67.9 9.0 %shard_map.118 = (f32[3,8192]{1,0:T(4,128)}, f32[64,128]{1,0:T(8,128)}) custom-call(s32[8,640]{1,0:T(8,128)S(1)} %get-tuple-element.81.list_ref, s32[8,128]{1,0:T(8,128)S(1)} %get-tuple-element.89.length_ref, f32[512,128]{1,0:T(8,128)S(1)} %get-tuple-element.90.compact_ref, f32[18576,128]{1,0:T(8,128)S(1)} %get-tuple-element.91.expanded_ref, ...), custom_call_target="tpu_custom_call" | custom-call | tf_op jit(solution)/shard_map/pallas_call | solution.py:713
  (40 shorter events, 7.1 us)
Async XLA Ops:
  0.6 36.0 %copy-start.5 = (s32[2,512]{1,0:T(2,128)S(1)}, s32[2,512]{1,0:T(2,128)}, u32[]{:S(2)}) copy-start(s32[2,512]{1,0:T(2,128)} %pair_ref.1) | copy-start | bytes 12292
  1.4 0.9 %copy-start = (f32[8,8192]{1,0:T(8,128)S(1)}, f32[8,8192]{1,0:T(8,128)}, u32[]{:S(2)}) copy-start(f32[8,8192]{1,0:T(8,128)} %particle_ref.1) | copy-start | bytes 786436
  2.4 0.8 copy-start.4
  4.5 8.3 %collective-permute-start = (f32[160,128]{1,0:T(8,128)S(1)}, f32[160,128]{1,0:T(8,128)S(1)}, u32[]{:S(2)}, u32[]{:S(2)}) collective-permute-start(f32[160,128]{1,0:T(8,128)S(1)} %get-tuple-element.64), channel_id=1, source_target_pairs={{0,16},{16,0},{4,20},{20,4},{8,24},{24,8},{12,28},{28,12},{1,17},{... | collective-permute-start | bytes 245768 | tf_op jit(solution)/shard_map/ppermute | solution.py:33
  8.6 0.7 copy-start.6
  13.2 5.6 %collective-permute-start.1 = (f32[160,128]{1,0:T(8,128)S(1)}, f32[160,128]{1,0:T(8,128)S(1)}, u32[]{:S(2)}, u32[]{:S(2)}) collective-permute-start(f32[160,128]{1,0:T(8,128)S(1)} %shard_map.107), channel_id=1, source_target_pairs={{0,8},{8,0},{4,12},{12,4},{16,24},{24,16},{20,28},{28,20},{1,9},{9... | collective-permute-start | bytes 245768 | tf_op jit(solution)/shard_map/ppermute | solution.py:33
  14.2 0.8 copy-start.1
  19.3 4.8 %collective-permute-start.2 = (f32[160,128]{1,0:T(8,128)S(1)}, f32[160,128]{1,0:T(8,128)S(1)}, u32[]{:S(2)}, u32[]{:S(2)}) collective-permute-start(f32[160,128]{1,0:T(8,128)S(1)} %shard_map.109), channel_id=1, source_target_pairs={{0,2},{2,0},{1,3},{3,1},{4,6},{6,4},{5,7},{7,5},{8,10},{10,8},{9,1... | collective-permute-start | bytes 245768 | tf_op jit(solution)/shard_map/ppermute | solution.py:33
  24.5 9.1 %collective-permute-start.3 = (f32[160,128]{1,0:T(8,128)S(1)}, f32[160,128]{1,0:T(8,128)S(1)}, u32[]{:S(2)}, u32[]{:S(2)}) collective-permute-start(f32[160,128]{1,0:T(8,128)S(1)} %shard_map.111), channel_id=1, source_target_pairs={{0,1},{1,0},{2,3},{3,2},{4,5},{5,4},{6,7},{7,6},{8,9},{9,8},{10,11... | collective-permute-start | bytes 245768 | tf_op jit(solution)/shard_map/ppermute | solution.py:33
  35.0 7.0 %collective-permute-start.4 = (f32[192,128]{1,0:T(8,128)S(1)}, f32[192,128]{1,0:T(8,128)S(1)}, u32[]{:S(2)}, u32[]{:S(2)}) collective-permute-start(f32[192,128]{1,0:T(8,128)S(1)} %get-tuple-element.86), channel_id=1, source_target_pairs={{0,28},{4,0},{8,4},{12,8},{16,12},{20,16},{24,20},{28,24},{1,29},{... | collective-permute-start | bytes 294920 | tf_op jit(solution)/shard_map/ppermute | solution.py:23
  36.6 5.8 %collective-permute-start.5 = (f32[192,128]{1,0:T(8,128)S(1)}, f32[192,128]{1,0:T(8,128)S(1)}, u32[]{:S(2)}, u32[]{:S(2)}) collective-permute-start(f32[192,128]{1,0:T(8,128)S(1)} %get-tuple-element.87), channel_id=1, source_target_pairs={{0,4},{4,8},{8,12},{12,16},{16,20},{20,24},{24,28},{28,0},{1,5},{5... | collective-permute-start | bytes 294920 | tf_op jit(solution)/shard_map/ppermute | solution.py:23
  42.5 5.9 %collective-permute-start.6 = (f32[192,128]{1,0:T(8,128)S(1)}, f32[192,128]{1,0:T(8,128)S(1)}, u32[]{:S(2)}, u32[]{:S(2)}) collective-permute-start(f32[192,128]{1,0:T(8,128)S(1)} %pad_maximum_fusion), channel_id=1, source_target_pairs={{0,3},{1,0},{2,1},{3,2},{4,7},{5,4},{6,5},{7,6},{8,11},{9,8},{10,9... | collective-permute-start | bytes 294920 | tf_op jit(solution)/shard_map/ppermute | solution.py:23
  43.1 6.6 %collective-permute-start.7 = (f32[192,128]{1,0:T(8,128)S(1)}, f32[192,128]{1,0:T(8,128)S(1)}, u32[]{:S(2)}, u32[]{:S(2)}) collective-permute-start(f32[192,128]{1,0:T(8,128)S(1)} %pad_maximum_fusion.1), channel_id=1, source_target_pairs={{0,1},{1,2},{2,3},{3,0},{4,5},{5,6},{6,7},{7,4},{8,9},{9,10},{10,1... | collective-permute-start | bytes 294920 | tf_op jit(solution)/shard_map/ppermute | solution.py:23
  44.6 5.1 %copy-start.2 = (s32[8,1024]{1,0:T(8,128)S(1)}, s32[8,1024]{1,0:T(8,128)}, u32[]{:S(2)}) copy-start(s32[8,1024]{1,0:T(8,128)} %export_ref.3) | copy-start | bytes 98308
  55.4 6.3 %collective-permute-start.8 = (f32[24,128]{1,0:T(8,128)S(1)}, f32[24,128]{1,0:T(8,128)S(1)}, u32[]{:S(2)}, u32[]{:S(2)}) collective-permute-start(f32[24,128]{1,0:T(8,128)S(1)} %get-tuple-element.103), channel_id=1, source_target_pairs={{0,28},{4,0},{8,4},{12,8},{16,12},{20,16},{24,20},{28,24},{1,29},{... | collective-permute-start | bytes 36872 | tf_op jit(solution)/shard_map/ppermute | solution.py:23
  55.5 6.2 %collective-permute-start.9 = (f32[24,128]{1,0:T(8,128)S(1)}, f32[24,128]{1,0:T(8,128)S(1)}, u32[]{:S(2)}, u32[]{:S(2)}) collective-permute-start(f32[24,128]{1,0:T(8,128)S(1)} %get-tuple-element.104), channel_id=1, source_target_pairs={{0,4},{4,8},{8,12},{12,16},{16,20},{20,24},{24,28},{28,0},{1,5},{5... | collective-permute-start | bytes 36872 | tf_op jit(solution)/shard_map/ppermute | solution.py:23
  55.9 0.8 copy-start.3
  61.7 4.4 %collective-permute-start.10 = (f32[24,128]{1,0:T(8,128)S(1)}, f32[24,128]{1,0:T(8,128)S(1)}, u32[]{:S(2)}, u32[]{:S(2)}) collective-permute-start(f32[24,128]{1,0:T(8,128)S(1)} %pad_maximum_fusion.2), channel_id=1, source_target_pairs={{0,3},{1,0},{2,1},{3,2},{4,7},{5,4},{6,5},{7,6},{8,11},{9,8},{10,9... | collective-permute-start | bytes 36872 | tf_op jit(solution)/shard_map/ppermute | solution.py:23
  63.3 4.6 %collective-permute-start.11 = (f32[24,128]{1,0:T(8,128)S(1)}, f32[24,128]{1,0:T(8,128)S(1)}, u32[]{:S(2)}, u32[]{:S(2)}) collective-permute-start(f32[24,128]{1,0:T(8,128)S(1)} %pad_maximum_fusion.3), channel_id=1, source_target_pairs={{0,1},{1,2},{2,3},{3,0},{4,5},{5,6},{6,7},{7,4},{8,9},{9,10},{10,1... | collective-permute-start | bytes 36872 | tf_op jit(solution)/shard_map/ppermute | solution.py:23

commit v3 on v2

--- a/solution.py
+++ b/solution.py
@@ -34,7 +34,15 @@
 
 
 def along_x(low, high):
-    return from_behind(low, "gx", -1), from_behind(high, "gx", 1)
+    count = lax.axis_size("gx")
+    if count % 2:
+        return from_behind(low, "gx", -1), from_behind(high, "gx", 1)
+    even = lax.axis_index("gx") % 2 == 0
+    first = [(i, i ^ 1) for i in range(count)]
+    second = [(i, (i + 1) % count if i % 2 else (i - 1) % count) for i in range(count)]
+    after = lax.ppermute(jnp.where(even, high, low), "gx", first)
+    before = lax.ppermute(jnp.where(even, low, high), "gx", second)
+    return jnp.where(even, after, before), jnp.where(even, before, after)
 
 
 def along_y(low, middle, high, unit):
@@ -198,61 +206,55 @@
             out_ref[place, :] = value
 
 
-def ahead_export_kernel(field_ref, flag_ref, before_ref, in_ref, inverse_ref, send_ref, last_ref, export_ref, new_field_ref, new_flag_ref, partial_ref, pick_ref, export_pick_ref, export_index_ref, index_ref, flag_in_ref):
-    ahead_kernel(1, field_ref, flag_ref, before_ref, in_ref, inverse_ref, send_ref, new_field_ref, new_flag_ref, partial_ref, pick_ref, index_ref, flag_in_ref)
-    zero = jnp.zeros((8, LANES), F32)
+def apply_kernel(field_ref, flag_ref, inverse_ref, in_ref, new_field_ref, new_flag_ref, flag_in_ref):
+    apply_incoming(field_ref, flag_ref, inverse_ref, in_ref, new_field_ref, new_flag_ref, flag_in_ref)
+
+
+def gather_exports(field_ref, index_ref, first, count, out_ref):
+    def body(step, carry):
+        row = index_ref[pl.ds(first + step, 1), :]
+        out_ref[pl.ds(aligned(step * 8), 8), :] = pick_fields(
+            lane_blocks(field_ref), row, jnp.zeros((8, LANES), F32)
+        )
+        return carry
+
+    lax.fori_loop(0, count, body, 0, unroll=8)
+
+
+def last_kernel(field_ref, flag_ref, inverse_ref, in_ref, export_ref, new_field_ref, new_flag_ref, low_ref, high_ref, index_ref, flag_in_ref):
     blocks = export_ref.shape[1] // LANES
-    for block in range(blocks):
-        index = export_ref[:, LANES * block : LANES * (block + 1)]
-        export_pick_ref[8 * block : 8 * block + 8, :] = pick_rows([last_ref], index, [zero])[0].astype(I32)
-        for number in range(8):
+    for number in range(8):
+        for block in range(blocks):
             at = number * blocks + block
-            export_index_ref[at : at + 1, :] = index[number : number + 1, :]
-
-
-def ahead_last_kernel(field_ref, flag_ref, before_ref, in_ref, export_index_ref, new_field_ref, new_flag_ref, *rest):
-    outs, flag_in_ref = rest[:3], rest[3]
-    apply_incoming(field_ref, flag_ref, before_ref, in_ref, new_field_ref, new_flag_ref, flag_in_ref)
-    blocks = export_index_ref.shape[0] // 8
-    for target, (first, count) in enumerate(((0, 3), (3, 2), (5, 3))):
-
-        def body(step, carry, target=target, first=first):
-            row = export_index_ref[pl.ds(first * blocks + step, 1), :]
-            outs[target][pl.ds(aligned(step * 8), 8), :] = pick_fields(
-                lane_blocks(new_field_ref), row, jnp.zeros((8, LANES), F32)
-            )
-            return carry
-
-        lax.fori_loop(0, count * blocks, body, 0, unroll=8)
-
-
-def fix_last_kernel(low_ref, middle_ref, high_ref, pick_ref, in_ref, *outs):
-    parts = (low_ref, middle_ref, high_ref)
-    blocks = pick_ref.shape[0] // 8
-    count = in_ref.shape[0] // 10
-    for number, (target, start) in enumerate(export_place(8 * blocks)):
-        for block in range(blocks):
-            slot = pick_ref[8 * block + number : 8 * block + number + 1, :] - 1
-            rows = slice(start + 8 * block, start + 8 * block + 8)
-            outs[target][rows, :] = pick_fields(row_blocks(in_ref, count), slot, parts[target][rows, :])
-
-
-EXPANDED = 9
-SLOPE_NORM = 0.5 * PARTICLE_MASS / math.pi
+            index_ref[at : at + 1, :] = export_ref[number : number + 1, LANES * block : LANES * (block + 1)]
+    apply_incoming(field_ref, flag_ref, inverse_ref, in_ref, new_field_ref, new_flag_ref, flag_in_ref)
+    gather_exports(new_field_ref, index_ref, 0, 3 * blocks, low_ref)
+    gather_exports(new_field_ref, index_ref, 5 * blocks, 3 * blocks, high_ref)
+
+
+def middle_kernel(field_ref, index_ref, out_ref):
+    blocks = index_ref.shape[0] // 8
+    gather_exports(field_ref, index_ref, 3 * blocks, 2 * blocks, out_ref)
+
+
+EXPANDED = 8
+NEAR_FIELDS = (0, 1, 2, 6)
+SPEED_FIELDS = (3, 4, 5)
+SLOPE_NORM = 0.375 * PARTICLE_MASS / math.pi
 
 
 def derived(height):
     inverse = 1.0 / height
     square = inverse * inverse
-    return inverse, SLOPE_NORM * (square * square * inverse)
-
-
-def expand_targets(compact_ref, chunk, base, expanded_ref):
+    return inverse, SLOPE_NORM * (square * square)
+
+
+def expand_targets(compact_ref, chunk, base, expanded_ref, fields=range(7), shift=0):
     groups = compact_ref.shape[0] // (4 * 32)
     region = (groups * 32 + 1) * 8
     half_base = jnp.where(iota((8, LANES), 1) < 64, 0, 64)
     for inner in range(8):
-        for field in range(7):
+        for field in fields:
             index = half_base + (inner * 8 + field)
             for group in range(groups):
                 for section in range(2):
@@ -261,25 +263,23 @@
                         start = aligned(chunk * (groups * 32) + place)
                         tile = 2 * (group * 16 + section * 8 + inner) + half
                         value = lane_pick(compact_ref[pl.ds(start, 8), :], index)
-                        first = base + field * region + tile * 8
+                        first = base + (field - shift) * region + tile * 8
                         if field == 6:
                             inverse, norm = derived(value)
                             expanded_ref[pl.ds(aligned(first), 8), :] = inverse
                             expanded_ref[pl.ds(aligned(first + region), 8), :] = norm
-                            expanded_ref[pl.ds(aligned(first + 2 * region), 8), :] = -0.75 * value
                         else:
                             expanded_ref[pl.ds(aligned(first), 8), :] = value
 
 
-def target_kernel(count_ref, field_ref, flag_ref, inverse_ref, in_ref, pair_ref,
-                  new_field_ref, new_flag_ref, compact_ref, rank_ref, order_ref, list_ref, length_ref, expanded_ref,
-                  flag_in_ref, stack_ref):
-    apply_incoming(field_ref, flag_ref, inverse_ref, in_ref, new_field_ref, new_flag_ref, flag_in_ref)
+def target_kernel(count_ref, field_ref, flag_ref, pair_ref,
+                  compact_ref, rank_ref, order_ref, list_ref, length_ref, expanded_ref,
+                  stack_ref):
     tile_rows = flag_ref.shape[0]
     groups = tile_rows // 16
     tile_count = 2 * tile_rows
     region = (tile_count + 1) * 8
-    active = new_flag_ref[...] > 0
+    active = flag_ref[...] > 0
     ones = jnp.where(active, 1.0, 0.0).astype(jnp.bfloat16)
     a = iota((LANES, LANES), 0)
     b = iota((LANES, LANES), 1)
@@ -302,7 +302,7 @@
         for inner in range(16):
             row = group * 16 + inner
             stack_ref[8 * inner : 8 * inner + 8, :] = lane_pick(
-                new_field_ref[:, LANES * row : LANES * (row + 1)], spread(order_ref[row : row + 1, :])
+                field_ref[:, LANES * row : LANES * (row + 1)], spread(order_ref[row : row + 1, :])
             )
         turned = jnp.transpose(stack_ref[...])
         for half in range(2):
@@ -365,30 +365,20 @@
         make_list(3)
 
     def one_chunk(chunk, carry):
-        expand_targets(compact_ref, chunk, aligned(chunk * (EXPANDED * region)), expanded_ref)
+        expand_targets(compact_ref, chunk, aligned(chunk * (EXPANDED * region)), expanded_ref, NEAR_FIELDS)
         return carry
 
     lax.fori_loop(0, 2, one_chunk, 0)
 
 
 def reduce_targets(sum_ref, first, tile_count, section, out_ref):
-    lane = iota((8, LANES), 1)
-    sub = iota((8, LANES), 0)
-    left = lane < 64
     blocks = tile_count // 16
     for block in range(blocks):
-        near = jnp.zeros((8, LANES), F32)
-        far = jnp.zeros((8, LANES), F32)
-        for inner in range(16):
-            place = first + (block * 16 + inner) * 8
-            value = sum_ref[place : place + 8, :]
-            here = lane == sub + inner * 8
-            near_sum = jnp.sum(jnp.where(left, value, 0.0), axis=1, keepdims=True)
-            far_sum = jnp.sum(jnp.where(left, 0.0, value), axis=1, keepdims=True)
-            near = jnp.where(here, near_sum, near)
-            far = jnp.where(here, far_sum, far)
-        out_ref[pl.ds((section * 2) * blocks + block, 1), :] = jnp.sum(near, axis=0, keepdims=True)
-        out_ref[pl.ds((section * 2 + 1) * blocks + block, 1), :] = jnp.sum(far, axis=0, keepdims=True)
+        start = first + block * LANES
+        turned = jnp.transpose(sum_ref[start : start + LANES, :])
+        for half in range(2):
+            total = jnp.sum(turned[64 * half : 64 * half + 64], axis=0, keepdims=True)
+            out_ref[pl.ds((section * 2 + half) * blocks + block, 1), :] = total
 
 
 def place_results(red_ref, blocks, part, rank):
@@ -438,7 +428,7 @@
 
             square = None
             for axis in range(3):
-                gap = at(axis) - pool_ref[pl.ds(source + axis, 1), :]
+                gap = at(axis) - pool_ref[pl.ds(source + axis, 8, stride=0), :]
                 gap = gap - jnp.floor(gap + 0.5)
                 square = gap * gap if square is None else square + gap * gap
             safe = jnp.maximum(square, 1.2e-38)
@@ -454,7 +444,7 @@
     lax.fori_loop(first, last, step, 0)
 
 
-def density_own_kernel(list_ref, length_ref, field_ref, expanded_ref, pool_ref, sum_ref):
+def density_own_kernel(list_ref, length_ref, field_ref, expanded_ref, compact_ref, pool_ref, sum_ref, speed_ref):
     tile_rows = field_ref.shape[1] // LANES
     region = (2 * tile_rows + 1) * 8
     for row in range(tile_rows):
@@ -466,10 +456,16 @@
             pool_ref, sum_ref, chunk * region,
         )
 
+    def one_chunk(chunk, carry):
+        expand_targets(compact_ref, chunk, aligned(chunk * (3 * region)), speed_ref, SPEED_FIELDS, 3)
+        return carry
+
+    lax.fori_loop(0, 2, one_chunk, 0)
+
 
 def density_kernel(list_ref, length_ref, compact_ref, expanded_ref, own_pool_ref, own_sum_ref, rank_ref, field_ref, flag_ref, low_ref, high_ref, down_ref, up_ref, export_ref,
-                   density_ref, low_out, middle_out, high_out, pool_ref,
-                   sum_ref, red_ref, height_ref, spare_ref):
+                   density_ref, low_out, middle_out, high_out, pool_ref, sum_ref, result_ref,
+                   red_ref, height_ref, spare_ref):
     tile_rows = flag_ref.shape[0]
     tile_count = 2 * tile_rows
     region = (tile_count + 1) * 8
@@ -480,7 +476,6 @@
         for block in range(blocks):
             first = start + 8 * block
             double_into(pool_ref, number * blocks + block, ghosts[which][first : first + 8, :])
-    sum_ref[...] = own_sum_ref[...]
     for chunk in range(2):
         density_pairs(
             list_ref, length_ref, chunk, True, expanded_ref, chunk * EXPANDED * region, region,
@@ -511,6 +506,7 @@
         flag = flag_ref[rows, :]
         norm = PARTICLE_MASS / (math.pi * height * height * height)
         density_ref[rows, :] = jnp.where(flag > 0, norm * (1.0 + found), jnp.abs(flag))
+        result_ref[rows, :] = density_ref[rows, :]
     outs = (low_out, middle_out, high_out)
     zero = jnp.zeros((8, LANES), F32)
     for block in range(blocks):
@@ -529,7 +525,7 @@
     if density is not None:
         press = press / density
     first_ref[rows, :] = jnp.where(sub == 7, press, jnp.where(sub == 6, inverse, value))
-    second_ref[rows, :] = jnp.where(sub == 6, norm, -0.75 * pltpu.roll(value, 1, 0))
+    second_ref[rows, :] = norm
 
 
 def doubled_halves(row):
@@ -539,7 +535,7 @@
     return jnp.where(left, wide, other), jnp.where(left, other, wide)
 
 
-def force_pairs(list_ref, length_ref, chunk, ghost, expanded_ref, base, region, press_ref, press_base, first_ref, second_ref, sum_ref):
+def force_pairs(list_ref, length_ref, chunk, ghost, expanded_ref, base, speed_ref, speed_base, region, press_ref, press_base, first_ref, second_ref, sum_ref):
     def step(number, carry):
         results = []
         for u in range(UNROLL):
@@ -549,11 +545,14 @@
             def at(field, target=target):
                 return expanded_ref[pl.ds(aligned(target + (base + field * region)), 8), :]
 
+            def speed(axis, target=target):
+                return speed_ref[pl.ds(aligned(target + (speed_base + axis * region)), 8), :]
+
             def source_row(field, source=source):
-                return first_ref[pl.ds(source + field, 1), :]
+                return first_ref[pl.ds(source + field, 8, stride=0), :]
 
             def source_more(field, source=source):
-                return second_ref[pl.ds(source + field, 1), :]
+                return second_ref[pl.ds(source + field, 8, stride=0), :]
 
             gaps = []
             square = None
@@ -563,21 +562,22 @@
                 gap = gap - jnp.floor(gap + 0.5)
                 gaps.append(gap)
                 square = gap * gap if square is None else square + gap * gap
-                part = (at(3 + axis) - source_row(3 + axis)) * gap
+                part = (speed(axis) - source_row(3 + axis)) * gap
                 approach = part if approach is None else approach + part
             safe = jnp.maximum(square, 1.2e-38)
             inverse_distance = lax.rsqrt(safe)
             distance = safe * inverse_distance
 
-            def slope(inverse_height, norm, scaled_height):
+            def slope(inverse_height, norm):
                 ratio = distance * inverse_height
-                outer = jnp.maximum(2.0 - ratio, 0.0)
-                far = (outer * outer) * (inverse_distance * scaled_height)
-                return norm * jnp.where(ratio < 1.0, 2.25 * ratio - 3.0, far)
-
-            total = slope(at(6), at(7), at(8)) + slope(source_row(6), source_more(6), source_more(7))
+                outer = 2.0 - ratio
+                inner = jnp.maximum(outer - ratio, 0.0)
+                outer = jnp.maximum(outer, 0.0)
+                return norm * (inner * inner - outer * outer)
+
+            total = slope(at(6), at(7)) + slope(source_row(6), source_more(6))
             press = press_ref[pl.ds(aligned(target + press_base), 8), :] + source_row(7)
-            weight = press * total
+            weight = press * (total * inverse_distance)
             results.append((target, [weight * gap for gap in gaps] + [weight * approach]))
         for target, values in results:
             for quantity in range(4):
@@ -599,7 +599,7 @@
             )
 
 
-def force_own_kernel(list_ref, length_ref, density_ref, field_ref, order_ref, expanded_ref, pool_ref,
+def force_own_kernel(list_ref, length_ref, density_ref, field_ref, order_ref, expanded_ref, speed_ref, pool_ref,
                      first_ref, second_ref, press_compact_ref, press_ref, sum_ref,
                      energy_ref, ordered_ref):
     tile_rows = density_ref.shape[0]
@@ -627,24 +627,24 @@
         expand_press(press_compact_ref, chunk, tile_rows, press_ref, chunk * region)
     clear(sum_ref, 0, 4 * region)
     force_pairs(
-        list_ref, length_ref, 0, False, expanded_ref, 0, region, press_ref, 0, first_ref, second_ref, sum_ref
-    )
-
-
-def force_own_more_kernel(list_ref, length_ref, expanded_ref, press_ref, own_first_ref, own_second_ref, pool_ref,
+        list_ref, length_ref, 0, False, expanded_ref, 0, speed_ref, 0, region, press_ref, 0, first_ref, second_ref, sum_ref,
+    )
+
+
+def force_own_more_kernel(list_ref, length_ref, expanded_ref, speed_ref, press_ref, own_first_ref, own_second_ref, pool_ref,
                           sum_ref, first_ref, second_ref):
     region = sum_ref.shape[0] // 4
     for tile in range(pool_ref.shape[0] // 8):
         source_tables(pool_ref, tile, first_ref, second_ref)
     clear(sum_ref, 0, 4 * region)
     force_pairs(
-        list_ref, length_ref, 1, False, expanded_ref, EXPANDED * region, region, press_ref, region,
+        list_ref, length_ref, 1, False, expanded_ref, EXPANDED * region, speed_ref, 3 * region, region, press_ref, region,
         own_first_ref, own_second_ref, sum_ref,
     )
 
 
-def force_kernel(list_ref, length_ref, compact_ref, expanded_ref, press_compact_ref, press_ref, rank_ref, flag_ref, own_first_ref, own_second_ref, half_ref, second_ref, zero_sum_ref, one_sum_ref, low_ref, high_ref, down_ref, up_ref,
-                 accel_ref, heat_ref,
+def force_kernel(list_ref, length_ref, compact_ref, expanded_ref, speed_ref, press_compact_ref, press_ref, rank_ref, flag_ref, own_first_ref, own_second_ref, half_ref, second_ref, zero_sum_ref, one_sum_ref, low_ref, high_ref, down_ref, up_ref,
+                 accel_ref, heat_ref, first_sum_ref, second_sum_ref,
                  first_ref, sum_ref, red_ref, spare_ref, spare_press_ref):
     tile_rows = flag_ref.shape[0]
     tile_count = 2 * tile_rows
@@ -661,13 +661,14 @@
                 value = half_ref[rows, :]
                 first_ref[rows, :] = jnp.where(is_press, value / density, value)
     for chunk in range(2):
-        sum_ref[...] = (zero_sum_ref if chunk == 0 else one_sum_ref)[...]
+        chunk_sum_ref = first_sum_ref if chunk == 0 else second_sum_ref
         force_pairs(
-            list_ref, length_ref, chunk, True, expanded_ref, chunk * EXPANDED * region, region,
-            press_ref, chunk * region, first_ref, second_ref, sum_ref,
+            list_ref, length_ref, chunk, True, expanded_ref, chunk * EXPANDED * region,
+            speed_ref, chunk * 3 * region, region,
+            press_ref, chunk * region, first_ref, second_ref, chunk_sum_ref,
         )
         for quantity in range(4):
-            reduce_targets(sum_ref, quantity * region, tile_count, chunk + 4 * quantity, red_ref)
+            reduce_targets(chunk_sum_ref, quantity * region, tile_count, chunk + 4 * quantity, red_ref)
     for quantity in range(4):
         for row in range(4 * blocks, 8 * blocks, 8):
             at = quantity * 8 * blocks + row
@@ -680,11 +681,11 @@
             expand_press(press_compact_ref, chunk, tile_rows, spare_press_ref, 0)
             clear(sum_ref, 0, 4 * region)
             force_pairs(
-                list_ref, length_ref, chunk, False, spare_ref, 0, region, spare_press_ref, 0,
+                list_ref, length_ref, chunk, False, spare_ref, 0, spare_ref, 3 * region, region, spare_press_ref, 0,
                 own_first_ref, own_second_ref, sum_ref,
             )
             force_pairs(
-                list_ref, length_ref, chunk, True, spare_ref, 0, region, spare_press_ref, 0,
+                list_ref, length_ref, chunk, True, spare_ref, 0, spare_ref, 3 * region, region, spare_press_ref, 0,
                 first_ref, second_ref, sum_ref,
             )
             for quantity in range(4):
@@ -707,7 +708,7 @@
                     accel_ref[quantity : quantity + 1, at : at + LANES] = found[row : row + 1, :]
 
 
-def call(kernel, outs, scratch, operands, scalars=0):
+def call(kernel, outs, scratch, operands, scalars=0, aliases=None):
     smem = pl.BlockSpec(memory_space=pltpu.SMEM)
     vmem = pl.BlockSpec(memory_space=pltpu.VMEM)
     return pl.pallas_call(
@@ -716,6 +717,7 @@
         in_specs=[smem if i < scalars else vmem for i in range(len(operands))],
         out_specs=[vmem] * len(outs),
         scratch_shapes=[pltpu.VMEM(shape, dtype) for shape, dtype in scratch],
+        input_output_aliases=aliases or {},
         compiler_params=pltpu.CompilerParams(vmem_limit_bytes=24 * 2**20),
     )(*operands)
 
@@ -765,39 +767,40 @@
     (outgoing,) = call(fix_kernel, [offered], [], [partial, pick, incoming])
     before = incoming
     incoming = swap(outgoing, 1)
-    fields, flag, partial, pick, export_pick, export_index = call(
-        ahead_export_kernel,
-        [whole, row, offered, picked, ((8 * dense_unit, LANES), I32), ((8 * dense_unit, LANES), I32)],
-        [index_scratch, flag_scratch],
-        [fields, flag, inverse[0], before, inverse[1], send_rows, inverse[3], export_rows],
+    ahead = [whole, row, offered, picked]
+    ahead_scratch = [index_scratch, flag_scratch]
+    fields, flag, partial, pick = call(
+        lambda *refs: ahead_kernel(1, *refs),
+        ahead,
+        ahead_scratch,
+        [fields, flag, inverse[0], before, inverse[1], send_rows],
     )
     (outgoing,) = call(fix_kernel, [offered], [], [partial, pick, incoming])
     before = incoming
     incoming = swap(outgoing, 2)
     fields, flag, partial, pick = call(
         lambda *refs: ahead_kernel(2, *refs),
-        [whole, row, offered, picked],
-        [index_scratch, flag_scratch],
+        ahead,
+        ahead_scratch,
         [fields, flag, inverse[1], before, inverse[2], send_rows],
     )
     (outgoing,) = call(fix_kernel, [offered], [], [partial, pick, incoming])
     before = incoming
     incoming = swap(outgoing, 3)
-    fields, flag, low, middle, high = call(
-        ahead_last_kernel,
-        [whole, row] + exported,
+    fields, flag = call(
+        apply_kernel, [whole, row], [flag_scratch], [fields, flag, inverse[2], before]
+    )
+    fields, flag, low, high, export_index = call(
+        last_kernel,
+        [whole, row, exported[0], exported[2], ((8 * dense_unit, LANES), I32)],
         [flag_scratch],
-        [fields, flag, inverse[2], before, export_index],
-    )
-    low, middle, high = call(
-        fix_last_kernel, exported, [], [low, middle, high, export_pick, incoming]
+        [fields, flag, inverse[3], incoming, export_rows],
     )
     low, high = along_x(low, high)
-    fields, flag, compact, rank, order, lists, lengths, expanded = call(
+    (middle,) = call(middle_kernel, [exported[1]], [], [fields, export_index])
+    compact, rank, order, lists, lengths, expanded = call(
         target_kernel,
         [
-            whole,
-            row,
             ((8 * tile_rows, LANES), F32),
             ((tile_rows, LANES), I32),
             ((tile_rows, LANES), I32),
@@ -805,22 +808,22 @@
             ((8, LANES), I32),
             ((2 * EXPANDED * region, LANES), F32),
         ],
-        [flag_scratch, ((LANES, LANES), F32)],
-        [pair_count, fields, flag, inverse[3], incoming, pair_tiles],
+        [((LANES, LANES), F32)],
+        [pair_count, fields, flag, pair_tiles],
         scalars=1,
     )
     low, high, lengths = lax.optimization_barrier((low, high, lengths))
     down, up = along_y(low, middle, high, unit)
     pool_shape = ((tile_count * 8, LANES), F32)
     ghost_pool_shape = ((2 * 8 * dense_unit * 8, LANES), F32)
-    own_pool, own_sum = call(
+    own_pool, own_sum, speed = call(
         density_own_kernel,
-        [pool_shape, ((2 * region, LANES), F32)],
+        [pool_shape, ((2 * region, LANES), F32), ((6 * region, LANES), F32)],
         [],
-        [lists, lengths, fields, expanded],
+        [lists, lengths, fields, expanded, compact],
         scalars=2,
     )
-    density, low_d, middle_d, high_d, ghost_pool = call(
+    density, low_d, middle_d, high_d, ghost_pool, _, density_out = call(
         density_kernel,
         [
             row,
@@ -828,9 +831,10 @@
             ((2 * dense_unit, LANES), F32),
             ((3 * dense_unit, LANES), F32),
             ghost_pool_shape,
+            ((2 * region, LANES), F32),
+            row,
         ],
         [
-            ((2 * region, LANES), F32),
             ((8 * (tile_count // 16), LANES), F32),
             row,
             ((EXPANDED * region, LANES), F32),
@@ -840,6 +844,7 @@
             rank, fields, flag, low, high, down, up, export_rows,
         ],
         scalars=2,
+        aliases={5: 5},
     )
     low_d, high_d = along_x(low_d, high_d)
     sums = ((4 * region, LANES), F32)
@@ -847,7 +852,7 @@
         force_own_kernel,
         [pool_shape, pool_shape, ((64, LANES), F32), ((2 * region, LANES), F32), sums],
         [row, ((LANES, LANES), F32)],
-        [lists, lengths, density, fields, order, expanded, own_pool],
+        [lists, lengths, density, fields, order, expanded, speed, own_pool],
         scalars=2,
     )
     low_d, high_d, press = lax.optimization_barrier((low_d, high_d, press))
@@ -856,12 +861,12 @@
         force_own_more_kernel,
         [sums, ghost_pool_shape, ghost_pool_shape],
         [],
-        [lists, lengths, expanded, press, own_first, own_second, ghost_pool],
+        [lists, lengths, expanded, speed, press, own_first, own_second, ghost_pool],
         scalars=2,
     )
-    accel, heat = call(
+    accel, heat, _, _ = call(
         force_kernel,
-        [((3, row_count), F32), row],
+        [((3, row_count), F32), row, sums, sums],
         [
             ghost_pool_shape,
             sums,
@@ -870,13 +875,14 @@
             ((region, LANES), F32),
         ],
         [
-            lists, lengths, compact, expanded, press_compact, press, rank, flag,
+            lists, lengths, compact, expanded, speed, press_compact, press, rank, flag,
             own_first, own_second, ghost_first, ghost_second, zero_sum, one_sum,
             low_d, high_d, down_d, up_d,
         ],
         scalars=2,
-    )
-    return (density.reshape(row_count), accel, heat.reshape(row_count))
+        aliases={13: 2, 14: 3},
+    )
+    return (density_out.reshape(row_count), accel, heat.reshape(row_count))
 
 
 def solution(mesh):

time: 77.7 us -> 72.2 us (0.929); the launches traced: 76.9 us -> 72.6 us
  Pallas kernels: 52.1 us -> 48.3 us
  local copies, waits for them, and re-layouts: 3.91 us -> 2.4 us
  waiting for transfers between devices: 4.08 us -> 5.47 us
    pallas_call x16 -> x17, Pallas kernels: 52.1 us -> 48.3 us  [call(): pl.pallas_call(kernel, out_shape=[jax.ShapeDtypeStruct(shape, dtype) for...]
    ppermute x0 -> x4, waiting for transfers between devices: none -> 2.18 us  [the longest x2 2.17 us: along_x(): before = lax.ppermute(jnp.where(even, low, high), 'gx', second)]
    ppermute x8 -> x4, starting transfers between devices: 6.28 us -> 4.5 us  [from_behind(): return lax.ppermute(value, axis, pairs)]
    ppermute x8 -> x4, waiting for transfers between devices: 3.42 us -> 1.89 us  [from_behind(): return lax.ppermute(value, axis, pairs)]
    unnamed x14 -> x10, local copies, waits for them, and re-layouts: 3.88 us -> 2.37 us
    ppermute x0 -> x4, starting transfers between devices: none -> 1.07 us  [the longest x2 0.72 us: along_x(): before = lax.ppermute(jnp.where(even, low, high), 'gx', second)]
  transfers between devices with their start and end apart: 12 -> 12, of which waited for: 4 -> 7; matrix products, arithmetic and copies ran while one was open for 0% -> 0% of each run, Pallas kernels for 43% -> 38%
where the time goes in v3:
time: 72.2 us; the launch traced here: 72.6 us
  Pallas kernels  48.3 us (67%)
  starting transfers between devices  14 us (19%)
  waiting for transfers between devices  5.47 us (8%)
  local copies, waits for them, and re-layouts  2.4 us (3%)
  between operations  1.48 us (2%)
  other arithmetic  0.85 us (1%)
    pallas_call x17, Pallas kernels, call(): pl.pallas_call(kernel, out_shape=[jax.ShapeDtypeStruct(shape, dtype) for...  48.3 us
    ppermute x4, starting transfers between devices, from_partner(): return lax.ppermute(block, axis, route)  8.43 us
    ppermute x4, starting transfers between devices, from_behind(): return lax.ppermute(value, axis, pairs)  4.5 us
    unnamed x10, local copies, waits for them, and re-layouts  2.37 us
    ppermute x2, waiting for transfers between devices, along_x(): before = lax.ppermute(jnp.where(even, low, high), 'gx', second)  2.17 us
    ppermute x4, waiting for transfers between devices, from_behind(): return lax.ppermute(value, axis, pairs)  1.89 us
  transfers between devices with their start and end apart: 12, of which 7 were waited for; matrix products, arithmetic and copies ran while one was open for 0% of the time, Pallas kernels for 38%

profile of v3, /device:TPU:0, one launch (start us, length us, event | category | flops | bytes accessed | tf_op | source)
XLA Modules:
  0.0 72.6 jit_solution(17795786887452506795)
XLA Ops:
  0.6 0.8 %fusion.flag_ref.refs_1_ = f32[64,128]{1,0:T(8,128)S(1)} fusion(f32[8192]{0:T(1024)} %param.9, s32[8192]{0:T(1024)} %param.10), kind=kLoop, calls=%fused_computation.7 | loop fusion | flops 24576 | bytes 98304 | tf_op jit(solution)/shard_map/reshape | solution.py:755
  1.4 0.9 %copy-done = f32[8,8192]{1,0:T(8,128)S(1)} copy-done((f32[8,8192]{1,0:T(8,128)S(1)}, f32[8,8192]{1,0:T(8,128)}, u32[]{:S(2)}) %copy-start) | copy-done | bytes 262168
  3.1 1.3 %shard_map.103 = (f32[8,8192]{1,0:T(8,128)S(1)}, f32[160,128]{1,0:T(8,128)S(1)}, s32[4,2048]{1,0:T(4,128)S(1)}) custom-call(f32[8,8192]{1,0:T(8,128)S(1)} %copy-done, f32[64,128]{1,0:T(8,128)S(1)} %fusion.flag_ref.refs_1_, s32[4,2048]{1,0:T(4,128)S(1)} %copy-done.2), custom_call_target="tpu_custom_call" | custom-call | tf_op jit(solution)/shard_map/pallas_call | solution.py:714
  4.5 4.1 %collective-permute-start = (f32[160,128]{1,0:T(8,128)S(1)}, f32[160,128]{1,0:T(8,128)S(1)}, u32[]{:S(2)}, u32[]{:S(2)}) collective-permute-start(f32[160,128]{1,0:T(8,128)S(1)} %get-tuple-element.61), channel_id=1, source_target_pairs={{0,16},{16,0},{4,20},{20,4},{8,24},{24,8},{12,28},{28,12},{1,17},{... | collective-permute-start | bytes 245768 | tf_op jit(solution)/shard_map/ppermute | solution.py:33
  9.2 1.4 %shard_map.104 = (f32[64,128]{1,0:T(8,128)S(1)}, f32[64,128]{1,0:T(8,128)S(1)}, f32[64,128]{1,0:T(8,128)S(1)}, f32[64,128]{1,0:T(8,128)S(1)}) custom-call(s32[4]{0:T(128)S(1)} %bitcast.5, s32[4,2048]{1,0:T(4,128)S(1)} %get-tuple-element.59.send_ref.refs_5_), custom_call_target="tpu_custom_call" | custom-call | tf_op jit(solution)/shard_map/pallas_call | solution.py:714
  10.7 1.5 %shard_map.106 = (f32[160,128]{1,0:T(8,128)S(1)}, s32[16,128]{1,0:T(8,128)S(1)}) custom-call(f32[8,8192]{1,0:T(8,128)S(1)} %get-tuple-element.58.refs_0_.field_ref, f32[64,128]{1,0:T(8,128)S(1)} %fusion.flag_ref.refs_1_, f32[64,128]{1,0:T(8,128)S(1)} %get-tuple-element.60.refs_2_.inverse_ref, s32[4,2048]{1,0:T(4,128)S(1)} %get-tuple-element.59.send_ref.refs_5_), custom_call_target="tpu_custom_call" | custom-call | tf_op jit(solution)/shard_map/pallas_call | solution.py:714
  13.2 1.0 %collective-permute-start.1 = (f32[160,128]{1,0:T(8,128)S(1)}, f32[160,128]{1,0:T(8,128)S(1)}, u32[]{:S(2)}, u32[]{:S(2)}) collective-permute-start(f32[160,128]{1,0:T(8,128)S(1)} %shard_map.107), channel_id=1, source_target_pairs={{0,8},{8,0},{4,12},{12,4},{16,24},{24,16},{20,28},{28,20},{1,9},{9... | collective-permute-start | bytes 245768 | tf_op jit(solution)/shard_map/ppermute | solution.py:33
  14.3 3.2 %shard_map.105 = (f32[8,8192]{1,0:T(8,128)S(1)}, f32[64,128]{1,0:T(8,128)S(1)}, f32[160,128]{1,0:T(8,128)S(1)}, s32[16,128]{1,0:T(8,128)S(1)}) custom-call(f32[8,8192]{1,0:T(8,128)S(1)} %get-tuple-element.58.refs_0_.field_ref, f32[64,128]{1,0:T(8,128)S(1)} %fusion.flag_ref.refs_1_, f32[64,128]{1,0:T(8,128)S(1)} %get-tuple-element.60.refs_2_.inverse_ref, ...), custom_call_target="tpu_custom_call" | custom-call | tf_op jit(solution)/shard_map/pallas_call | solution.py:714
  18.2 1.8 %collective-permute-start.2 = (f32[160,128]{1,0:T(8,128)S(1)}, f32[160,128]{1,0:T(8,128)S(1)}, u32[]{:S(2)}, u32[]{:S(2)}) collective-permute-start(f32[160,128]{1,0:T(8,128)S(1)} %shard_map.109), channel_id=1, source_target_pairs={{0,2},{2,0},{1,3},{3,1},{4,6},{6,4},{5,7},{7,5},{8,10},{10,8},{9,1... | collective-permute-start | bytes 245768 | tf_op jit(solution)/shard_map/ppermute | solution.py:33
  20.0 3.2 %shard_map.108 = (f32[8,8192]{1,0:T(8,128)S(1)}, f32[64,128]{1,0:T(8,128)S(1)}, f32[160,128]{1,0:T(8,128)S(1)}, s32[16,128]{1,0:T(8,128)S(1)}) custom-call(f32[8,8192]{1,0:T(8,128)S(1)} %get-tuple-element.63.refs_0_, f32[64,128]{1,0:T(8,128)S(1)} %get-tuple-element.64.refs_1_, f32[64,128]{1,0:T(8,128)S(1)} %get-tuple-element.62.refs_4_.refs_2_, ...), custom_call_target="tpu_custom_call" | custom-call | tf_op jit(solution)/shard_map/pallas_call | solution.py:714
  23.7 1.6 %collective-permute-start.3 = (f32[160,128]{1,0:T(8,128)S(1)}, f32[160,128]{1,0:T(8,128)S(1)}, u32[]{:S(2)}, u32[]{:S(2)}) collective-permute-start(f32[160,128]{1,0:T(8,128)S(1)} %shard_map.111), channel_id=1, source_target_pairs={{0,1},{1,0},{2,3},{3,2},{4,5},{5,4},{6,7},{7,6},{8,9},{9,8},{10,11... | collective-permute-start | bytes 245768 | tf_op jit(solution)/shard_map/ppermute | solution.py:33
  25.9 1.8 %shard_map.110 = (f32[8,8192]{1,0:T(8,128)S(1)}, f32[64,128]{1,0:T(8,128)S(1)}) custom-call(f32[8,8192]{1,0:T(8,128)S(1)} %get-tuple-element.68.field_ref, f32[64,128]{1,0:T(8,128)S(1)} %get-tuple-element.69.flag_ref, f32[64,128]{1,0:T(8,128)S(1)} %get-tuple-element.67.refs_4_.inverse_ref, f32[160,128]{1,0:T(8,128)S(1)} %collective-permute-done.2.in_ref), custom_call_target="tpu_custom_call" | custom-call | tf_op jit(solution)/shard_map/pallas_call | solution.py:714
  28.2 5.6 %shard_map.112 = (f32[8,8192]{1,0:T(8,128)S(1)}, f32[64,128]{1,0:T(8,128)S(1)}, f32[192,128]{1,0:T(8,128)S(1)}, f32[192,128]{1,0:T(8,128)S(1)}, s32[64,128]{1,0:T(8,128)S(1)}) custom-call(f32[8,8192]{1,0:T(8,128)S(1)} %get-tuple-element.72.field_ref, f32[64,128]{1,0:T(8,128)S(1)} %get-tuple-element.73.flag_ref, f32[64,128]{1,0:T(8,128)S(1)} %get-tuple-element.74.inverse_ref, ...), custom_call_target="tpu_custom_call" | custom-call | tf_op jit(solution)/shard_map/pallas_call | solution.py:714
  34.8 1.3 %shard_map.115 = f32[128,128]{1,0:T(8,128)S(1)} custom-call(f32[8,8192]{1,0:T(8,128)S(1)} %get-tuple-element.77.field_ref, s32[64,128]{1,0:T(8,128)S(1)} %get-tuple-element.91.index_ref), custom_call_target="tpu_custom_call" | custom-call | tf_op jit(solution)/shard_map/pallas_call | solution.py:714
  36.1 2.5 %shard_map.113 = (f32[512,128]{1,0:T(8,128)S(1)}, s32[64,128]{1,0:T(8,128)S(1)}, s32[64,128]{1,0:T(8,128)S(1)}, s32[8,640]{1,0:T(8,128)S(1)}, s32[8,128]{1,0:T(8,128)S(1)}, /*index=5*/f32[16512,128]{1,0:T(8,128)S(1)}) custom-call(s32[1]{0:T(128)S(6)} %copy.17.count_ref, f32[8,8192]{1,0:T(8,128)S(1)} %get-tuple-element.77.field_ref, ...), custom_call_target="tpu_custom_call" | custom-call | tf_op jit(solution)/shard_map/pallas_call | solution.py:714
  38.7 2.0 %collective-permute-done.5 = f32[192,128]{1,0:T(8,128)S(1)} collective-permute-done((f32[192,128]{1,0:T(8,128)S(1)}, f32[192,128]{1,0:T(8,128)S(1)}, u32[]{:S(2)}, u32[]{:S(2)}) %collective-permute-start.5) | collective-permute-done | bytes 98336 | tf_op jit(solution)/shard_map/ppermute | solution.py:44
  40.8 2.2 %collective-permute-start.6 = (f32[192,128]{1,0:T(8,128)S(1)}, f32[192,128]{1,0:T(8,128)S(1)}, u32[]{:S(2)}, u32[]{:S(2)}) collective-permute-start(f32[192,128]{1,0:T(8,128)S(1)} %pad_maximum_fusion), channel_id=1, source_target_pairs={{0,3},{1,0},{2,1},{3,2},{4,7},{5,4},{6,5},{7,6},{8,11},{9,8},{10,9... | collective-permute-start | bytes 294920 | tf_op jit(solution)/shard_map/ppermute | solution.py:23
  43.2 5.1 %shard_map.114 = (f32[1024,128]{1,0:T(8,128)S(1)}, f32[2064,128]{1,0:T(8,128)S(1)}, f32[6192,128]{1,0:T(8,128)S(1)}) custom-call(s32[8,640]{1,0:T(8,128)S(1)} %get-tuple-element.79.list_ref, s32[8,128]{1,0:T(8,128)S(1)} %get-tuple-element.83.length_ref, f32[8,8192]{1,0:T(8,128)S(1)} %get-tuple-element.77.field_ref, ...), custom_call_target="tpu_custom_call" | custom-call | tf_op jit(solution)/shard_map/pallas_call | solution.py:714
  48.7 5.3 %shard_map.116 = (f32[64,128]{1,0:T(8,128)S(1)}, f32[24,128]{1,0:T(8,128)S(1)}, f32[16,128]{1,0:T(8,128)S(1)}, f32[24,128]{1,0:T(8,128)S(1)}, f32[1024,128]{1,0:...) custom-call(s32[8,640]{1,0:T(8,128)S(1)} %get-tuple-element.79.list_ref, ...), custom_call_target="tpu_custom_call", output_to_operand_aliasing={{5}: (5, {})} | custom-call | tf_op jit(solution)/shard_map/pallas_call | solution.py:714
  54.1 4.7 %shard_map.117 = (f32[1024,128]{1,0:T(8,128)S(1)}, f32[1024,128]{1,0:T(8,128)S(1)}, f32[64,128]{1,0:T(8,128)S(1)}, f32[2064,128]{1,0:T(8,128)S(1)}, f32[4128,128]{1,0:T(8,128)S(1)}) custom-call(s32[8,640]{1,0:T(8,128)S(1)} %get-tuple-element.79.list_ref, s32[8,128]{1,0:T(8,128)S(1)} %get-tuple-element.83.length_ref, ...), custom_call_target="tpu_custom_call" | custom-call | tf_op jit(solution)/shard_map/pallas_call | solution.py:714
  59.0 1.6 %collective-permute-start.10 = (f32[24,128]{1,0:T(8,128)S(1)}, f32[24,128]{1,0:T(8,128)S(1)}, u32[]{:S(2)}, u32[]{:S(2)}) collective-permute-start(f32[24,128]{1,0:T(8,128)S(1)} %pad_maximum_fusion.2), channel_id=1, source_target_pairs={{0,3},{1,0},{2,1},{3,2},{4,7},{5,4},{6,5},{7,6},{8,11},{9,8},{10,9... | collective-permute-start | bytes 36872 | tf_op jit(solution)/shard_map/ppermute | solution.py:23
  61.1 2.5 %shard_map.118 = (f32[4128,128]{1,0:T(8,128)S(1)}, f32[1024,128]{1,0:T(8,128)S(1)}, f32[1024,128]{1,0:T(8,128)S(1)}) custom-call(s32[8,640]{1,0:T(8,128)S(1)} %get-tuple-element.79.list_ref, s32[8,128]{1,0:T(8,128)S(1)} %get-tuple-element.83.length_ref, f32[16512,128]{1,0:T(8,128)S(1)} %get-tuple-element.85.expanded_ref, ...), custom_call_target="tpu_custom_call" | custom-call | tf_op jit(solution)/shard_map/pallas_call | solution.py:714
  63.6 1.5 %collective-permute-done.11.up_ref = f32[24,128]{1,0:T(8,128)S(1)} collective-permute-done((f32[24,128]{1,0:T(8,128)S(1)}, f32[24,128]{1,0:T(8,128)S(1)}, u32[]{:S(2)}, u32[]{:S(2)}) %collective-permute-start.11) | collective-permute-done | bytes 12320 | tf_op jit(solution)/shard_map/ppermute | solution.py:23
  65.1 7.4 %shard_map.119 = (f32[3,8192]{1,0:T(4,128)}, f32[64,128]{1,0:T(8,128)}, f32[4128,128]{1,0:T(8,128)S(1)}, f32[4128,128]{1,0:T(8,128)S(1)}) custom-call(s32[8,640]{1,0:T(8,128)S(1)} %get-tuple-element.79.list_ref, s32[8,128]{1,0:T(8,128)S(1)} %get-tuple-element.83.length_ref, ...), custom_call_target="tpu_custom_call", output_to_operand_aliasing={{2}: (13, {}), {3}: (14, {})} | custom-call | tf_op jit(solution)/shard_map/pallas_call | solution.py:714
  (41 shorter events, 6.6 us)
Async XLA Ops:
  0.6 27.6 %copy-start.1 = (s32[8,1024]{1,0:T(8,128)S(1)}, s32[8,1024]{1,0:T(8,128)}, u32[]{:S(2)}) copy-start(s32[8,1024]{1,0:T(8,128)} %export_ref.3) | copy-start | bytes 98308
  1.4 0.9 %copy-start = (f32[8,8192]{1,0:T(8,128)S(1)}, f32[8,8192]{1,0:T(8,128)}, u32[]{:S(2)}) copy-start(f32[8,8192]{1,0:T(8,128)} %particle_ref.1) | copy-start | bytes 786436
  2.4 0.8 %copy-start.2 = (s32[4,2048]{1,0:T(4,128)S(1)}, s32[4,2048]{1,0:T(4,128)}, u32[]{:S(2)}) copy-start(s32[4,2048]{1,0:T(4,128)} %send_in_ref.1) | copy-start | bytes 98308
  3.1 33.0 %copy-start.3 = (s32[2,512]{1,0:T(2,128)S(1)}, s32[2,512]{1,0:T(2,128)}, u32[]{:S(2)}) copy-start(s32[2,512]{1,0:T(2,128)} %pair_ref.1) | copy-start | bytes 12292
  4.5 8.3 %collective-permute-start = (f32[160,128]{1,0:T(8,128)S(1)}, f32[160,128]{1,0:T(8,128)S(1)}, u32[]{:S(2)}, u32[]{:S(2)}) collective-permute-start(f32[160,128]{1,0:T(8,128)S(1)} %get-tuple-element.61), channel_id=1, source_target_pairs={{0,16},{16,0},{4,20},{20,4},{8,24},{24,8},{12,28},{28,12},{1,17},{... | collective-permute-start | bytes 245768 | tf_op jit(solution)/shard_map/ppermute | solution.py:33
  8.6 0.7 copy-start.4
  13.2 4.5 %collective-permute-start.1 = (f32[160,128]{1,0:T(8,128)S(1)}, f32[160,128]{1,0:T(8,128)S(1)}, u32[]{:S(2)}, u32[]{:S(2)}) collective-permute-start(f32[160,128]{1,0:T(8,128)S(1)} %shard_map.107), channel_id=1, source_target_pairs={{0,8},{8,0},{4,12},{12,4},{16,24},{24,16},{20,28},{28,20},{1,9},{9... | collective-permute-start | bytes 245768 | tf_op jit(solution)/shard_map/ppermute | solution.py:33
  18.2 5.0 %collective-permute-start.2 = (f32[160,128]{1,0:T(8,128)S(1)}, f32[160,128]{1,0:T(8,128)S(1)}, u32[]{:S(2)}, u32[]{:S(2)}) collective-permute-start(f32[160,128]{1,0:T(8,128)S(1)} %shard_map.109), channel_id=1, source_target_pairs={{0,2},{2,0},{1,3},{3,1},{4,6},{6,4},{5,7},{7,5},{8,10},{10,8},{9,1... | collective-permute-start | bytes 245768 | tf_op jit(solution)/shard_map/ppermute | solution.py:33
  23.7 4.5 %collective-permute-start.3 = (f32[160,128]{1,0:T(8,128)S(1)}, f32[160,128]{1,0:T(8,128)S(1)}, u32[]{:S(2)}, u32[]{:S(2)}) collective-permute-start(f32[160,128]{1,0:T(8,128)S(1)} %shard_map.111), channel_id=1, source_target_pairs={{0,1},{1,0},{2,3},{3,2},{4,5},{5,4},{6,7},{7,6},{8,9},{9,8},{10,11... | collective-permute-start | bytes 245768 | tf_op jit(solution)/shard_map/ppermute | solution.py:33
  33.9 6.8 %collective-permute-start.5 = (f32[192,128]{1,0:T(8,128)S(1)}, f32[192,128]{1,0:T(8,128)S(1)}, u32[]{:S(2)}, u32[]{:S(2)}) collective-permute-start(f32[192,128]{1,0:T(8,128)S(1)} %get-tuple-element.115), channel_id=1, source_target_pairs={{0,28},{4,8},{8,4},{12,16},{16,12},{20,24},{24,20},{28,0},{1,29},{... | collective-permute-start | bytes 294920 | tf_op jit(solution)/shard_map/ppermute | solution.py:44
  34.6 6.1 %collective-permute-start.4 = (f32[192,128]{1,0:T(8,128)S(1)}, f32[192,128]{1,0:T(8,128)S(1)}, u32[]{:S(2)}, u32[]{:S(2)}) collective-permute-start(f32[192,128]{1,0:T(8,128)S(1)} %get-tuple-element.116), channel_id=1, source_target_pairs={{0,4},{4,0},{8,12},{12,8},{16,20},{20,16},{24,28},{28,24},{1,5},{5... | collective-permute-start | bytes 294920 | tf_op jit(solution)/shard_map/ppermute | solution.py:43
  40.8 7.6 %collective-permute-start.6 = (f32[192,128]{1,0:T(8,128)S(1)}, f32[192,128]{1,0:T(8,128)S(1)}, u32[]{:S(2)}, u32[]{:S(2)}) collective-permute-start(f32[192,128]{1,0:T(8,128)S(1)} %pad_maximum_fusion), channel_id=1, source_target_pairs={{0,3},{1,0},{2,1},{3,2},{4,7},{5,4},{6,5},{7,6},{8,11},{9,8},{10,9... | collective-permute-start | bytes 294920 | tf_op jit(solution)/shard_map/ppermute | solution.py:23
  43.0 5.7 %collective-permute-start.7 = (f32[192,128]{1,0:T(8,128)S(1)}, f32[192,128]{1,0:T(8,128)S(1)}, u32[]{:S(2)}, u32[]{:S(2)}) collective-permute-start(f32[192,128]{1,0:T(8,128)S(1)} %pad_maximum_fusion.1), channel_id=1, source_target_pairs={{0,1},{1,2},{2,3},{3,0},{4,5},{5,6},{6,7},{7,4},{8,9},{9,10},{10,1... | collective-permute-start | bytes 294920 | tf_op jit(solution)/shard_map/ppermute | solution.py:23
  54.0 4.9 %collective-permute-start.9 = (f32[24,128]{1,0:T(8,128)S(1)}, f32[24,128]{1,0:T(8,128)S(1)}, u32[]{:S(2)}, u32[]{:S(2)}) collective-permute-start(f32[24,128]{1,0:T(8,128)S(1)} %get-tuple-element.125), channel_id=1, source_target_pairs={{0,28},{4,8},{8,4},{12,16},{16,12},{20,24},{24,20},{28,0},{1,29},{... | collective-permute-start | bytes 36872 | tf_op jit(solution)/shard_map/ppermute | solution.py:44
  54.0 4.9 %collective-permute-start.8 = (f32[24,128]{1,0:T(8,128)S(1)}, f32[24,128]{1,0:T(8,128)S(1)}, u32[]{:S(2)}, u32[]{:S(2)}) collective-permute-start(f32[24,128]{1,0:T(8,128)S(1)} %get-tuple-element.126), channel_id=1, source_target_pairs={{0,4},{4,0},{8,12},{12,8},{16,20},{20,16},{24,28},{28,24},{1,5},{5... | collective-permute-start | bytes 36872 | tf_op jit(solution)/shard_map/ppermute | solution.py:43
  59.0 4.6 %collective-permute-start.10 = (f32[24,128]{1,0:T(8,128)S(1)}, f32[24,128]{1,0:T(8,128)S(1)}, u32[]{:S(2)}, u32[]{:S(2)}) collective-permute-start(f32[24,128]{1,0:T(8,128)S(1)} %pad_maximum_fusion.2), channel_id=1, source_target_pairs={{0,3},{1,0},{2,1},{3,2},{4,7},{5,4},{6,5},{7,6},{8,11},{9,8},{10,9... | collective-permute-start | bytes 36872 | tf_op jit(solution)/shard_map/ppermute | solution.py:23
  60.5 4.6 %collective-permute-start.11 = (f32[24,128]{1,0:T(8,128)S(1)}, f32[24,128]{1,0:T(8,128)S(1)}, u32[]{:S(2)}, u32[]{:S(2)}) collective-permute-start(f32[24,128]{1,0:T(8,128)S(1)} %pad_maximum_fusion.3), channel_id=1, source_target_pairs={{0,1},{1,2},{2,3},{3,0},{4,5},{5,6},{6,7},{7,4},{8,9},{9,10},{10,1... | collective-permute-start | bytes 36872 | tf_op jit(solution)/shard_map/ppermute | solution.py:23

commit v4 on v3

--- a/solution.py
+++ b/solution.py
@@ -175,9 +175,21 @@
         inverse_ref[...] = both[:tile_rows] * 64.0 + both[tile_rows:]
 
 
-def ahead_first_kernel(field_ref, flag_ref, inverse_ref, send_ref, partial_ref, pick_ref, index_ref):
+EARLY = 16
+
+
+def ahead_first_kernel(field_ref, flag_ref, inverse_ref, send_ref, last_ref, export_ref, partial_ref, pick_ref, export_index_ref, export_pick_ref, index_ref):
     stage_index(send_ref, 1, index_ref)
     gather_outgoing(field_ref, flag_ref, index_ref, partial_ref, inverse_ref, pick_ref)
+    blocks = export_ref.shape[1] // LANES
+    for number in range(8):
+        for block in range(blocks):
+            at = number * blocks + block
+            export_index_ref[at : at + 1, :] = export_ref[number : number + 1, LANES * block : LANES * (block + 1)]
+    zero = jnp.zeros((8, LANES), F32)
+    for part in range(blocks):
+        rows = slice(8 * part, 8 * part + 8)
+        export_pick_ref[rows, :] = pick_rows([last_ref], export_index_ref[rows, :], [zero])[0].astype(I32)
 
 
 def ahead_kernel(level, field_ref, flag_ref, before_ref, in_ref, inverse_ref, send_ref, new_field_ref, new_flag_ref, partial_ref, pick_ref, index_ref, flag_in_ref):
@@ -206,35 +218,36 @@
             out_ref[place, :] = value
 
 
-def apply_kernel(field_ref, flag_ref, inverse_ref, in_ref, new_field_ref, new_flag_ref, flag_in_ref):
+def ahead_last_kernel(field_ref, flag_ref, inverse_ref, in_ref, index_ref, new_field_ref, new_flag_ref, early_ref, flag_in_ref):
     apply_incoming(field_ref, flag_ref, inverse_ref, in_ref, new_field_ref, new_flag_ref, flag_in_ref)
-
-
-def gather_exports(field_ref, index_ref, first, count, out_ref):
+    gather_exports(new_field_ref, index_ref, 0, EARLY, early_ref, 0)
+
+
+def gather_exports(field_ref, index_ref, first, count, out_ref, skip, in_ref=None, pick_ref=None):
     def body(step, carry):
         row = index_ref[pl.ds(first + step, 1), :]
-        out_ref[pl.ds(aligned(step * 8), 8), :] = pick_fields(
-            lane_blocks(field_ref), row, jnp.zeros((8, LANES), F32)
-        )
+        found = pick_fields(lane_blocks(field_ref), row, jnp.zeros((8, LANES), F32))
+        if in_ref is not None:
+            slot = pick_ref[pl.ds(first + step, 1), :] - 1
+            found = pick_fields(row_blocks(in_ref, in_ref.shape[0] // 10), slot, found)
+        out_ref[pl.ds(aligned((skip + step) * 8), 8), :] = found
         return carry
 
     lax.fori_loop(0, count, body, 0, unroll=8)
 
 
-def last_kernel(field_ref, flag_ref, inverse_ref, in_ref, export_ref, new_field_ref, new_flag_ref, low_ref, high_ref, index_ref, flag_in_ref):
-    blocks = export_ref.shape[1] // LANES
-    for number in range(8):
-        for block in range(blocks):
-            at = number * blocks + block
-            index_ref[at : at + 1, :] = export_ref[number : number + 1, LANES * block : LANES * (block + 1)]
-    apply_incoming(field_ref, flag_ref, inverse_ref, in_ref, new_field_ref, new_flag_ref, flag_in_ref)
-    gather_exports(new_field_ref, index_ref, 0, 3 * blocks, low_ref)
-    gather_exports(new_field_ref, index_ref, 5 * blocks, 3 * blocks, high_ref)
-
-
-def middle_kernel(field_ref, index_ref, out_ref):
+def last_kernel(field_ref, in_ref, index_ref, early_ref, pick_ref, low_ref, high_ref):
     blocks = index_ref.shape[0] // 8
-    gather_exports(field_ref, index_ref, 3 * blocks, 2 * blocks, out_ref)
+
+    def body(step, carry):
+        where = pl.ds(aligned(step * 8), 8)
+        slot = pick_ref[pl.ds(step, 1), :] - 1
+        low_ref[where, :] = pick_fields(row_blocks(in_ref, in_ref.shape[0] // 10), slot, early_ref[where, :])
+        return carry
+
+    lax.fori_loop(0, EARLY, body, 0, unroll=True)
+    gather_exports(field_ref, index_ref, EARLY, 3 * blocks - EARLY, low_ref, EARLY, in_ref, pick_ref)
+    gather_exports(field_ref, index_ref, 5 * blocks, 3 * blocks, high_ref, 0, in_ref, pick_ref)
 
 
 EXPANDED = 8
@@ -272,9 +285,12 @@
                             expanded_ref[pl.ds(aligned(first), 8), :] = value
 
 
-def target_kernel(count_ref, field_ref, flag_ref, pair_ref,
-                  compact_ref, rank_ref, order_ref, list_ref, length_ref, expanded_ref,
-                  stack_ref):
+def target_kernel(count_ref, old_field_ref, old_flag_ref, inverse_ref, in_ref, index_ref, pair_ref,
+                  field_ref, flag_ref, middle_ref, compact_ref, rank_ref, order_ref, list_ref, length_ref, expanded_ref,
+                  flag_in_ref, stack_ref):
+    apply_incoming(old_field_ref, old_flag_ref, inverse_ref, in_ref, field_ref, flag_ref, flag_in_ref)
+    blocks = index_ref.shape[0] // 8
+    gather_exports(field_ref, index_ref, 3 * blocks, 2 * blocks, middle_ref, 0)
     tile_rows = flag_ref.shape[0]
     groups = tile_rows // 16
     tile_count = 2 * tile_rows
@@ -761,8 +777,12 @@
     )
     incoming = swap(outgoing, 0)
     inverse = call(inverse_kernel, [row] * levels, [], [send_count[:, 0], send_rows], scalars=1)
-    partial, pick = call(
-        ahead_first_kernel, [offered, picked], [index_scratch], [fields, flag, inverse[0], send_rows]
+    export_rows_shape = ((8 * dense_unit, LANES), I32)
+    partial, pick, export_index, export_pick = call(
+        ahead_first_kernel,
+        [offered, picked, export_rows_shape, export_rows_shape],
+        [index_scratch],
+        [fields, flag, inverse[0], send_rows, inverse[3], export_rows],
     )
     (outgoing,) = call(fix_kernel, [offered], [], [partial, pick, incoming])
     before = incoming
@@ -787,20 +807,25 @@
     (outgoing,) = call(fix_kernel, [offered], [], [partial, pick, incoming])
     before = incoming
     incoming = swap(outgoing, 3)
-    fields, flag = call(
-        apply_kernel, [whole, row], [flag_scratch], [fields, flag, inverse[2], before]
-    )
-    fields, flag, low, high, export_index = call(
+    fields, flag, early = call(
+        ahead_last_kernel,
+        [whole, row, ((8 * EARLY, LANES), F32)],
+        [flag_scratch],
+        [fields, flag, inverse[2], before, export_index],
+    )
+    low, high = call(
         last_kernel,
-        [whole, row, exported[0], exported[2], ((8 * dense_unit, LANES), I32)],
-        [flag_scratch],
-        [fields, flag, inverse[3], incoming, export_rows],
+        [exported[0], exported[2]],
+        [],
+        [fields, incoming, export_index, early, export_pick],
     )
     low, high = along_x(low, high)
-    (middle,) = call(middle_kernel, [exported[1]], [], [fields, export_index])
-    compact, rank, order, lists, lengths, expanded = call(
+    fields, flag, middle, compact, rank, order, lists, lengths, expanded = call(
         target_kernel,
         [
+            whole,
+            row,
+            exported[1],
             ((8 * tile_rows, LANES), F32),
             ((tile_rows, LANES), I32),
             ((tile_rows, LANES), I32),
@@ -808,8 +833,8 @@
             ((8, LANES), I32),
             ((2 * EXPANDED * region, LANES), F32),
         ],
-        [((LANES, LANES), F32)],
-        [pair_count, fields, flag, pair_tiles],
+        [flag_scratch, ((LANES, LANES), F32)],
+        [pair_count, fields, flag, inverse[3], incoming, export_index, pair_tiles],
         scalars=1,
     )
     low, high, lengths = lax.optimization_barrier((low, high, lengths))

time: 72.2 us -> 71.4 us (0.989); the launches traced: 72.6 us -> 70.5 us
  waiting for transfers between devices: 5.47 us -> 1.16 us
  starting transfers between devices: 14 us -> 15.6 us
  local copies, waits for them, and re-layouts: 2.4 us -> 3.15 us
    ppermute x2, waiting for transfers between devices: 2.17 us -> 0.01 us  [along_x(): before = lax.ppermute(jnp.where(even, low, high), 'gx', second)]
    ppermute x2, starting transfers between devices: 0.35 us -> 2.11 us  [along_x(): after = lax.ppermute(jnp.where(even, high, low), 'gx', first)]
    ppermute x4, waiting for transfers between devices: 1.41 us -> 0.01 us  [from_partner(): return lax.ppermute(block, axis, route)]
    unnamed x10 -> x12, local copies, waits for them, and re-layouts: 2.37 us -> 3.12 us
    ppermute x4, waiting for transfers between devices: 1.89 us -> 1.14 us  [from_behind(): return lax.ppermute(value, axis, pairs)]
    pallas_call x17 -> x16, Pallas kernels: 48.3 us -> 48.2 us  [call(): pl.pallas_call(kernel, out_shape=[jax.ShapeDtypeStruct(shape, dtype) for...]
  transfers between devices with their start and end apart: 12 -> 12, of which waited for: 7 -> 2; matrix products, arithmetic and copies ran while one was open for 0% -> 0% of each run, Pallas kernels for 38% -> 43%
where the time goes in v4:
time: 71.4 us; the launch traced here: 70.5 us
  Pallas kernels  48.2 us (68%)
  starting transfers between devices  15.6 us (22%)
  local copies, waits for them, and re-layouts  3.15 us (4%)
  between operations  1.53 us (2%)
  waiting for transfers between devices  1.16 us (2%)
  other arithmetic  0.86 us (1%)
    pallas_call x16, Pallas kernels, call(): pl.pallas_call(kernel, out_shape=[jax.ShapeDtypeStruct(shape, dtype) for...  48.2 us
    ppermute x4, starting transfers between devices, from_partner(): return lax.ppermute(block, axis, route)  8.88 us
    ppermute x4, starting transfers between devices, from_behind(): return lax.ppermute(value, axis, pairs)  4.19 us
    unnamed x12, local copies, waits for them, and re-layouts  3.12 us
    ppermute x2, starting transfers between devices, along_x(): after = lax.ppermute(jnp.where(even, high, low), 'gx', first)  2.11 us
  transfers between devices with their start and end apart: 12, of which 2 were waited for; matrix products, arithmetic and copies ran while one was open for 0% of the time, Pallas kernels for 43%

profile of v4, /device:TPU:0, one launch (start us, length us, event | category | flops | bytes accessed | tf_op | source)
XLA Modules:
  0.0 70.5 jit_solution(12543020495519230047)
XLA Ops:
  0.6 0.8 %fusion.flag_ref.refs_1_ = f32[64,128]{1,0:T(8,128)S(1)} fusion(f32[8192]{0:T(1024)} %param.9, s32[8192]{0:T(1024)} %param.10), kind=kLoop, calls=%fused_computation.7 | loop fusion | flops 24576 | bytes 98304 | tf_op jit(solution)/shard_map/reshape | solution.py:771
  1.4 0.9 %copy-done = f32[8,8192]{1,0:T(8,128)S(1)} copy-done((f32[8,8192]{1,0:T(8,128)S(1)}, f32[8,8192]{1,0:T(8,128)}, u32[]{:S(2)}) %copy-start) | copy-done | bytes 262168
  2.4 0.8 %copy-done.3 = s32[4,2048]{1,0:T(4,128)S(1)} copy-done((s32[4,2048]{1,0:T(4,128)S(1)}, s32[4,2048]{1,0:T(4,128)}, u32[]{:S(2)}) %copy-start.3) | copy-done | bytes 32792
  3.1 1.3 %shard_map.103 = (f32[8,8192]{1,0:T(8,128)S(1)}, f32[160,128]{1,0:T(8,128)S(1)}, s32[4,2048]{1,0:T(4,128)S(1)}) custom-call(f32[8,8192]{1,0:T(8,128)S(1)} %copy-done, f32[64,128]{1,0:T(8,128)S(1)} %fusion.flag_ref.refs_1_, s32[4,2048]{1,0:T(4,128)S(1)} %copy-done.3), custom_call_target="tpu_custom_call" | custom-call | tf_op jit(solution)/shard_map/pallas_call | solution.py:730
  4.5 4.1 %collective-permute-start = (f32[160,128]{1,0:T(8,128)S(1)}, f32[160,128]{1,0:T(8,128)S(1)}, u32[]{:S(2)}, u32[]{:S(2)}) collective-permute-start(f32[160,128]{1,0:T(8,128)S(1)} %get-tuple-element.64), channel_id=1, source_target_pairs={{0,16},{16,0},{4,20},{20,4},{8,24},{24,8},{12,28},{28,12},{1,17},{... | collective-permute-start | bytes 245768 | tf_op jit(solution)/shard_map/ppermute | solution.py:33
  9.2 1.4 %shard_map.104 = (f32[64,128]{1,0:T(8,128)S(1)}, f32[64,128]{1,0:T(8,128)S(1)}, f32[64,128]{1,0:T(8,128)S(1)}, f32[64,128]{1,0:T(8,128)S(1)}) custom-call(s32[4]{0:T(128)S(1)} %bitcast.5, s32[4,2048]{1,0:T(4,128)S(1)} %get-tuple-element.62.send_ref.refs_5_), custom_call_target="tpu_custom_call" | custom-call | tf_op jit(solution)/shard_map/pallas_call | solution.py:730
  11.4 2.0 %shard_map.106 = (f32[160,128]{1,0:T(8,128)S(1)}, s32[16,128]{1,0:T(8,128)S(1)}, s32[64,128]{1,0:T(8,128)S(1)}, s32[64,128]{1,0:T(8,128)S(1)}) custom-call(f32[8,8192]{1,0:T(8,128)S(1)} %get-tuple-element.61.refs_0_.field_ref, f32[64,128]{1,0:T(8,128)S(1)} %fusion.flag_ref.refs_1_, f32[64,128]{1,0:T(8,128)S(1)} %get-tuple-element.63.refs_2_.inverse_ref, ...), custom_call_target="tpu_custom_call" | custom-call | tf_op jit(solution)/shard_map/pallas_call | solution.py:730
  13.9 1.6 %collective-permute-start.1 = (f32[160,128]{1,0:T(8,128)S(1)}, f32[160,128]{1,0:T(8,128)S(1)}, u32[]{:S(2)}, u32[]{:S(2)}) collective-permute-start(f32[160,128]{1,0:T(8,128)S(1)} %shard_map.107), channel_id=1, source_target_pairs={{0,8},{8,0},{4,12},{12,4},{16,24},{24,16},{20,28},{28,20},{1,9},{9... | collective-permute-start | bytes 245768 | tf_op jit(solution)/shard_map/ppermute | solution.py:33
  15.6 3.2 %shard_map.105 = (f32[8,8192]{1,0:T(8,128)S(1)}, f32[64,128]{1,0:T(8,128)S(1)}, f32[160,128]{1,0:T(8,128)S(1)}, s32[16,128]{1,0:T(8,128)S(1)}) custom-call(f32[8,8192]{1,0:T(8,128)S(1)} %get-tuple-element.61.refs_0_.field_ref, f32[64,128]{1,0:T(8,128)S(1)} %fusion.flag_ref.refs_1_, f32[64,128]{1,0:T(8,128)S(1)} %get-tuple-element.63.refs_2_.inverse_ref, ...), custom_call_target="tpu_custom_call" | custom-call | tf_op jit(solution)/shard_map/pallas_call | solution.py:730
  19.3 1.6 %collective-permute-start.2 = (f32[160,128]{1,0:T(8,128)S(1)}, f32[160,128]{1,0:T(8,128)S(1)}, u32[]{:S(2)}, u32[]{:S(2)}) collective-permute-start(f32[160,128]{1,0:T(8,128)S(1)} %shard_map.109), channel_id=1, source_target_pairs={{0,2},{2,0},{1,3},{3,1},{4,6},{6,4},{5,7},{7,5},{8,10},{10,8},{9,1... | collective-permute-start | bytes 245768 | tf_op jit(solution)/shard_map/ppermute | solution.py:33
  20.9 3.2 %shard_map.108 = (f32[8,8192]{1,0:T(8,128)S(1)}, f32[64,128]{1,0:T(8,128)S(1)}, f32[160,128]{1,0:T(8,128)S(1)}, s32[16,128]{1,0:T(8,128)S(1)}) custom-call(f32[8,8192]{1,0:T(8,128)S(1)} %get-tuple-element.66.refs_0_, f32[64,128]{1,0:T(8,128)S(1)} %get-tuple-element.67.refs_1_, f32[64,128]{1,0:T(8,128)S(1)} %get-tuple-element.65.refs_4_.refs_2_, ...), custom_call_target="tpu_custom_call" | custom-call | tf_op jit(solution)/shard_map/pallas_call | solution.py:730
  24.5 1.6 %collective-permute-start.3 = (f32[160,128]{1,0:T(8,128)S(1)}, f32[160,128]{1,0:T(8,128)S(1)}, u32[]{:S(2)}, u32[]{:S(2)}) collective-permute-start(f32[160,128]{1,0:T(8,128)S(1)} %shard_map.111), channel_id=1, source_target_pairs={{0,1},{1,0},{2,3},{3,2},{4,5},{5,4},{6,7},{7,6},{8,9},{9,8},{10,11... | collective-permute-start | bytes 245768 | tf_op jit(solution)/shard_map/ppermute | solution.py:33
  26.7 3.1 %shard_map.110 = (f32[8,8192]{1,0:T(8,128)S(1)}, f32[64,128]{1,0:T(8,128)S(1)}, f32[128,128]{1,0:T(8,128)S(1)}) custom-call(f32[8,8192]{1,0:T(8,128)S(1)} %get-tuple-element.72.field_ref, f32[64,128]{1,0:T(8,128)S(1)} %get-tuple-element.73.flag_ref, f32[64,128]{1,0:T(8,128)S(1)} %get-tuple-element.71.refs_4_.inverse_ref, ...), custom_call_target="tpu_custom_call" | custom-call | tf_op jit(solution)/shard_map/pallas_call | solution.py:730
  29.9 3.5 %shard_map.113 = (f32[192,128]{1,0:T(8,128)S(1)}, f32[192,128]{1,0:T(8,128)S(1)}) custom-call(f32[8,8192]{1,0:T(8,128)S(1)} %get-tuple-element.77.old_field_ref.field_ref, f32[160,128]{1,0:T(8,128)S(1)} %collective-permute-done.3.in_ref, s32[64,128]{1,0:T(8,128)S(1)} %get-tuple-element.76.index_ref, f32[128,128]{1,0:T(8,128)S(1)} %get-tuple-element.82.early_ref, ...), custom_call_target="tpu_custom_call" | custom-call | tf_op jit(solution)/shard_map/pallas_call | solution.py:730
  33.8 1.0 %collective-permute-start.4 = (f32[192,128]{1,0:T(8,128)S(1)}, f32[192,128]{1,0:T(8,128)S(1)}, u32[]{:S(2)}, u32[]{:S(2)}) collective-permute-start(f32[192,128]{1,0:T(8,128)S(1)} %get-tuple-element.122), channel_id=1, source_target_pairs={{0,4},{4,0},{8,12},{12,8},{16,20},{20,16},{24,28},{28,24},{1,5},{5... | collective-permute-start | bytes 294920 | tf_op jit(solution)/shard_map/ppermute | solution.py:43
  34.8 5.6 %shard_map.112 = (f32[8,8192]{1,0:T(8,128)S(1)}, f32[64,128]{1,0:T(8,128)S(1)}, f32[128,128]{1,0:T(8,128)S(1)}, f32[512,128]{1,0:T(8,128)S(1)}, s32[64,128]{1,0:...) custom-call(s32[1]{0:T(128)S(6)} %copy.17.count_ref, ...), custom_call_target="tpu_custom_call" | custom-call | tf_op jit(solution)/shard_map/pallas_call | solution.py:730
  40.5 1.4 %collective-permute-start.6 = (f32[192,128]{1,0:T(8,128)S(1)}, f32[192,128]{1,0:T(8,128)S(1)}, u32[]{:S(2)}, u32[]{:S(2)}) collective-permute-start(f32[192,128]{1,0:T(8,128)S(1)} %pad_maximum_fusion), channel_id=1, source_target_pairs={{0,3},{1,0},{2,1},{3,2},{4,7},{5,4},{6,5},{7,6},{8,11},{9,8},{10,9... | collective-permute-start | bytes 294920 | tf_op jit(solution)/shard_map/ppermute | solution.py:23
  42.6 4.8 %shard_map.114 = (f32[1024,128]{1,0:T(8,128)S(1)}, f32[2064,128]{1,0:T(8,128)S(1)}, f32[6192,128]{1,0:T(8,128)S(1)}) custom-call(s32[8,640]{1,0:T(8,128)S(1)} %get-tuple-element.81.list_ref, s32[8,128]{1,0:T(8,128)S(1)} %get-tuple-element.87.length_ref, f32[8,8192]{1,0:T(8,128)S(1)} %get-tuple-element.90.field_ref, ...), custom_call_target="tpu_custom_call" | custom-call | tf_op jit(solution)/shard_map/pallas_call | solution.py:730
  48.0 5.1 %shard_map.115 = (f32[64,128]{1,0:T(8,128)S(1)}, f32[24,128]{1,0:T(8,128)S(1)}, f32[16,128]{1,0:T(8,128)S(1)}, f32[24,128]{1,0:T(8,128)S(1)}, f32[1024,128]{1,0:...) custom-call(s32[8,640]{1,0:T(8,128)S(1)} %get-tuple-element.81.list_ref, ...), custom_call_target="tpu_custom_call", output_to_operand_aliasing={{5}: (5, {})} | custom-call | tf_op jit(solution)/shard_map/pallas_call | solution.py:730
  53.1 1.2 %collective-permute-start.8 = (f32[24,128]{1,0:T(8,128)S(1)}, f32[24,128]{1,0:T(8,128)S(1)}, u32[]{:S(2)}, u32[]{:S(2)}) collective-permute-start(f32[24,128]{1,0:T(8,128)S(1)} %get-tuple-element.132), channel_id=1, source_target_pairs={{0,4},{4,0},{8,12},{12,8},{16,20},{20,16},{24,28},{28,24},{1,5},{5... | collective-permute-start | bytes 36872 | tf_op jit(solution)/shard_map/ppermute | solution.py:43
  54.2 4.7 %shard_map.116 = (f32[1024,128]{1,0:T(8,128)S(1)}, f32[1024,128]{1,0:T(8,128)S(1)}, f32[64,128]{1,0:T(8,128)S(1)}, f32[2064,128]{1,0:T(8,128)S(1)}, f32[4128,128]{1,0:T(8,128)S(1)}) custom-call(s32[8,640]{1,0:T(8,128)S(1)} %get-tuple-element.81.list_ref, s32[8,128]{1,0:T(8,128)S(1)} %get-tuple-element.87.length_ref, ...), custom_call_target="tpu_custom_call" | custom-call | tf_op jit(solution)/shard_map/pallas_call | solution.py:730
  59.1 2.0 %collective-permute-start.11 = (f32[24,128]{1,0:T(8,128)S(1)}, f32[24,128]{1,0:T(8,128)S(1)}, u32[]{:S(2)}, u32[]{:S(2)}) collective-permute-start(f32[24,128]{1,0:T(8,128)S(1)} %pad_maximum_fusion.3), channel_id=1, source_target_pairs={{0,1},{1,2},{2,3},{3,0},{4,5},{5,6},{6,7},{7,4},{8,9},{9,10},{10,1... | collective-permute-start | bytes 36872 | tf_op jit(solution)/shard_map/ppermute | solution.py:23
  61.1 2.0 %shard_map.117 = (f32[4128,128]{1,0:T(8,128)S(1)}, f32[1024,128]{1,0:T(8,128)S(1)}, f32[1024,128]{1,0:T(8,128)S(1)}) custom-call(s32[8,640]{1,0:T(8,128)S(1)} %get-tuple-element.81.list_ref, s32[8,128]{1,0:T(8,128)S(1)} %get-tuple-element.87.length_ref, f32[16512,128]{1,0:T(8,128)S(1)} %get-tuple-element.89.expanded_ref, ...), custom_call_target="tpu_custom_call" | custom-call | tf_op jit(solution)/shard_map/pallas_call | solution.py:730
  63.7 6.8 %shard_map.118 = (f32[3,8192]{1,0:T(4,128)}, f32[64,128]{1,0:T(8,128)}, f32[4128,128]{1,0:T(8,128)S(1)}, f32[4128,128]{1,0:T(8,128)S(1)}) custom-call(s32[8,640]{1,0:T(8,128)S(1)} %get-tuple-element.81.list_ref, s32[8,128]{1,0:T(8,128)S(1)} %get-tuple-element.87.length_ref, ...), custom_call_target="tpu_custom_call", output_to_operand_aliasing={{2}: (13, {}), {3}: (14, {})} | custom-call | tf_op jit(solution)/shard_map/pallas_call | solution.py:730
  (42 shorter events, 5.3 us)
Async XLA Ops:
  0.6 34.1 %copy-start.4 = (s32[2,512]{1,0:T(2,128)S(1)}, s32[2,512]{1,0:T(2,128)}, u32[]{:S(2)}) copy-start(s32[2,512]{1,0:T(2,128)} %pair_ref.1) | copy-start | bytes 12292
  1.4 0.9 %copy-start = (f32[8,8192]{1,0:T(8,128)S(1)}, f32[8,8192]{1,0:T(8,128)}, u32[]{:S(2)}) copy-start(f32[8,8192]{1,0:T(8,128)} %particle_ref.1) | copy-start | bytes 786436
  2.4 0.8 %copy-start.3 = (s32[4,2048]{1,0:T(4,128)S(1)}, s32[4,2048]{1,0:T(4,128)}, u32[]{:S(2)}) copy-start(s32[4,2048]{1,0:T(4,128)} %send_in_ref.1) | copy-start | bytes 98308
  4.5 9.0 %collective-permute-start = (f32[160,128]{1,0:T(8,128)S(1)}, f32[160,128]{1,0:T(8,128)S(1)}, u32[]{:S(2)}, u32[]{:S(2)}) collective-permute-start(f32[160,128]{1,0:T(8,128)S(1)} %get-tuple-element.64), channel_id=1, source_target_pairs={{0,16},{16,0},{4,20},{20,4},{8,24},{24,8},{12,28},{28,12},{1,17},{... | collective-permute-start | bytes 245768 | tf_op jit(solution)/shard_map/ppermute | solution.py:33
  8.6 0.7 copy-start.5
  10.7 0.8 %copy-start.1 = (s32[8,1024]{1,0:T(8,128)S(1)}, s32[8,1024]{1,0:T(8,128)}, u32[]{:S(2)}) copy-start(s32[8,1024]{1,0:T(8,128)} %export_ref.3) | copy-start | bytes 98308
  13.9 4.9 %collective-permute-start.1 = (f32[160,128]{1,0:T(8,128)S(1)}, f32[160,128]{1,0:T(8,128)S(1)}, u32[]{:S(2)}, u32[]{:S(2)}) collective-permute-start(f32[160,128]{1,0:T(8,128)S(1)} %shard_map.107), channel_id=1, source_target_pairs={{0,8},{8,0},{4,12},{12,4},{16,24},{24,16},{20,28},{28,20},{1,9},{9... | collective-permute-start | bytes 245768 | tf_op jit(solution)/shard_map/ppermute | solution.py:33
  19.3 4.8 %collective-permute-start.2 = (f32[160,128]{1,0:T(8,128)S(1)}, f32[160,128]{1,0:T(8,128)S(1)}, u32[]{:S(2)}, u32[]{:S(2)}) collective-permute-start(f32[160,128]{1,0:T(8,128)S(1)} %shard_map.109), channel_id=1, source_target_pairs={{0,2},{2,0},{1,3},{3,1},{4,6},{6,4},{5,7},{7,5},{8,10},{10,8},{9,1... | collective-permute-start | bytes 245768 | tf_op jit(solution)/shard_map/ppermute | solution.py:33
  24.5 5.3 %collective-permute-start.3 = (f32[160,128]{1,0:T(8,128)S(1)}, f32[160,128]{1,0:T(8,128)S(1)}, u32[]{:S(2)}, u32[]{:S(2)}) collective-permute-start(f32[160,128]{1,0:T(8,128)S(1)} %shard_map.111), channel_id=1, source_target_pairs={{0,1},{1,0},{2,3},{3,2},{4,5},{5,4},{6,7},{7,6},{8,9},{9,8},{10,11... | collective-permute-start | bytes 245768 | tf_op jit(solution)/shard_map/ppermute | solution.py:33
  33.4 7.0 %collective-permute-start.5 = (f32[192,128]{1,0:T(8,128)S(1)}, f32[192,128]{1,0:T(8,128)S(1)}, u32[]{:S(2)}, u32[]{:S(2)}) collective-permute-start(f32[192,128]{1,0:T(8,128)S(1)} %get-tuple-element.121), channel_id=1, source_target_pairs={{0,28},{4,8},{8,4},{12,16},{16,12},{20,24},{24,20},{28,0},{1,29},{... | collective-permute-start | bytes 294920 | tf_op jit(solution)/shard_map/ppermute | solution.py:44
  33.8 6.6 %collective-permute-start.4 = (f32[192,128]{1,0:T(8,128)S(1)}, f32[192,128]{1,0:T(8,128)S(1)}, u32[]{:S(2)}, u32[]{:S(2)}) collective-permute-start(f32[192,128]{1,0:T(8,128)S(1)} %get-tuple-element.122), channel_id=1, source_target_pairs={{0,4},{4,0},{8,12},{12,8},{16,20},{20,16},{24,28},{28,24},{1,5},{5... | collective-permute-start | bytes 294920 | tf_op jit(solution)/shard_map/ppermute | solution.py:43
  40.5 7.0 %collective-permute-start.6 = (f32[192,128]{1,0:T(8,128)S(1)}, f32[192,128]{1,0:T(8,128)S(1)}, u32[]{:S(2)}, u32[]{:S(2)}) collective-permute-start(f32[192,128]{1,0:T(8,128)S(1)} %pad_maximum_fusion), channel_id=1, source_target_pairs={{0,3},{1,0},{2,1},{3,2},{4,7},{5,4},{6,5},{7,6},{8,11},{9,8},{10,9... | collective-permute-start | bytes 294920 | tf_op jit(solution)/shard_map/ppermute | solution.py:23
  41.9 6.1 %collective-permute-start.7 = (f32[192,128]{1,0:T(8,128)S(1)}, f32[192,128]{1,0:T(8,128)S(1)}, u32[]{:S(2)}, u32[]{:S(2)}) collective-permute-start(f32[192,128]{1,0:T(8,128)S(1)} %pad_maximum_fusion.1), channel_id=1, source_target_pairs={{0,1},{1,2},{2,3},{3,0},{4,5},{5,6},{6,7},{7,4},{8,9},{9,10},{10,1... | collective-permute-start | bytes 294920 | tf_op jit(solution)/shard_map/ppermute | solution.py:23
  42.6 5.4 %copy-start.2 = (s32[8,1024]{1,0:T(8,128)S(1)}, s32[8,1024]{1,0:T(8,128)}, u32[]{:S(2)}) copy-start(s32[8,1024]{1,0:T(8,128)} %export_ref.3) | copy-start | bytes 98308
  53.0 5.9 %collective-permute-start.9 = (f32[24,128]{1,0:T(8,128)S(1)}, f32[24,128]{1,0:T(8,128)S(1)}, u32[]{:S(2)}, u32[]{:S(2)}) collective-permute-start(f32[24,128]{1,0:T(8,128)S(1)} %get-tuple-element.131), channel_id=1, source_target_pairs={{0,28},{4,8},{8,4},{12,16},{16,12},{20,24},{24,20},{28,0},{1,29},{... | collective-permute-start | bytes 36872 | tf_op jit(solution)/shard_map/ppermute | solution.py:44
  53.1 5.9 %collective-permute-start.8 = (f32[24,128]{1,0:T(8,128)S(1)}, f32[24,128]{1,0:T(8,128)S(1)}, u32[]{:S(2)}, u32[]{:S(2)}) collective-permute-start(f32[24,128]{1,0:T(8,128)S(1)} %get-tuple-element.132), channel_id=1, source_target_pairs={{0,4},{4,0},{8,12},{12,8},{16,20},{20,16},{24,28},{28,24},{1,5},{5... | collective-permute-start | bytes 36872 | tf_op jit(solution)/shard_map/ppermute | solution.py:43
  59.0 4.1 %collective-permute-start.10 = (f32[24,128]{1,0:T(8,128)S(1)}, f32[24,128]{1,0:T(8,128)S(1)}, u32[]{:S(2)}, u32[]{:S(2)}) collective-permute-start(f32[24,128]{1,0:T(8,128)S(1)} %pad_maximum_fusion.2), channel_id=1, source_target_pairs={{0,3},{1,0},{2,1},{3,2},{4,7},{5,4},{6,5},{7,6},{8,11},{9,8},{10,9... | collective-permute-start | bytes 36872 | tf_op jit(solution)/shard_map/ppermute | solution.py:23
  59.1 4.6 %collective-permute-start.11 = (f32[24,128]{1,0:T(8,128)S(1)}, f32[24,128]{1,0:T(8,128)S(1)}, u32[]{:S(2)}, u32[]{:S(2)}) collective-permute-start(f32[24,128]{1,0:T(8,128)S(1)} %pad_maximum_fusion.3), channel_id=1, source_target_pairs={{0,1},{1,2},{2,3},{3,0},{4,5},{5,6},{6,7},{7,4},{8,9},{9,10},{10,1... | collective-permute-start | bytes 36872 | tf_op jit(solution)/shard_map/ppermute | solution.py:23

commit v5 on v4

--- a/solution.py
+++ b/solution.py
@@ -839,8 +839,8 @@
     )
     low, high, lengths = lax.optimization_barrier((low, high, lengths))
     down, up = along_y(low, middle, high, unit)
-    pool_shape = ((tile_count * 8, LANES), F32)
-    ghost_pool_shape = ((2 * 8 * dense_unit * 8, LANES), F32)
+    pool_shape = ((tile_count * 8 + 8, LANES), F32)
+    ghost_pool_shape = ((2 * 8 * dense_unit * 8 + 8, LANES), F32)
     own_pool, own_sum, speed = call(
         density_own_kernel,
         [pool_shape, ((2 * region, LANES), F32), ((6 * region, LANES), F32)],

time: 71.4 us -> 72 us (level); the launches traced: 70.5 us -> 72.2 us
  waiting for transfers between devices: 1.16 us -> 2.54 us
  Pallas kernels: 48.2 us -> 49.3 us
  starting transfers between devices: 15.6 us -> 14.8 us
    ppermute x4, waiting for transfers between devices: 1.14 us -> 2.51 us  [from_behind(): return lax.ppermute(value, axis, pairs)]
    ppermute x2, starting transfers between devices: 2.11 us -> 0.96 us  [along_x(): after = lax.ppermute(jnp.where(even, high, low), 'gx', first)]
    pallas_call x16, Pallas kernels: 48.2 us -> 49.3 us  [call(): pl.pallas_call(kernel, out_shape=[jax.ShapeDtypeStruct(shape, dtype) for...]
  transfers between devices with their start and end apart: 12 -> 12, of which waited for: 2 -> 2; matrix products, arithmetic and copies ran while one was open for 0% -> 0% of each run, Pallas kernels for 43% -> 42%
where the time goes in v5:
time: 72 us; the launch traced here: 72.2 us
  Pallas kernels  49.3 us (68%)
  starting transfers between devices  14.8 us (21%)
  local copies, waits for them, and re-layouts  3.15 us (4%)
  waiting for transfers between devices  2.54 us (4%)
  between operations  1.52 us (2%)
  other arithmetic  0.86 us (1%)
    pallas_call x16, Pallas kernels, call(): pl.pallas_call(kernel, out_shape=[jax.ShapeDtypeStruct(shape, dtype) for...  49.3 us
    ppermute x4, starting transfers between devices, from_partner(): return lax.ppermute(block, axis, route)  8.88 us
    ppermute x4, starting transfers between devices, from_behind(): return lax.ppermute(value, axis, pairs)  4.2 us
    unnamed x12, local copies, waits for them, and re-layouts  3.12 us
    ppermute x4, waiting for transfers between devices, from_behind(): return lax.ppermute(value, axis, pairs)  2.51 us
  transfers between devices with their start and end apart: 12, of which 2 were waited for; matrix products, arithmetic and copies ran while one was open for 0% of the time, Pallas kernels for 42%

profile of v5, /device:TPU:0, one launch (start us, length us, event | category | flops | bytes accessed | tf_op | source)
XLA Modules:
  0.0 72.2 jit_solution(3268918848320359675)
XLA Ops:
  0.6 0.8 %fusion.flag_ref.refs_1_ = f32[64,128]{1,0:T(8,128)S(1)} fusion(f32[8192]{0:T(1024)} %param.9, s32[8192]{0:T(1024)} %param.10), kind=kLoop, calls=%fused_computation.7 | loop fusion | flops 24576 | bytes 98304 | tf_op jit(solution)/shard_map/reshape | solution.py:771
  1.4 0.9 %copy-done = f32[8,8192]{1,0:T(8,128)S(1)} copy-done((f32[8,8192]{1,0:T(8,128)S(1)}, f32[8,8192]{1,0:T(8,128)}, u32[]{:S(2)}) %copy-start) | copy-done | bytes 262168
  2.4 0.8 %copy-done.3 = s32[4,2048]{1,0:T(4,128)S(1)} copy-done((s32[4,2048]{1,0:T(4,128)S(1)}, s32[4,2048]{1,0:T(4,128)}, u32[]{:S(2)}) %copy-start.3) | copy-done | bytes 32792
  3.1 1.3 %shard_map.103 = (f32[8,8192]{1,0:T(8,128)S(1)}, f32[160,128]{1,0:T(8,128)S(1)}, s32[4,2048]{1,0:T(4,128)S(1)}) custom-call(f32[8,8192]{1,0:T(8,128)S(1)} %copy-done, f32[64,128]{1,0:T(8,128)S(1)} %fusion.flag_ref.refs_1_, s32[4,2048]{1,0:T(4,128)S(1)} %copy-done.3), custom_call_target="tpu_custom_call" | custom-call | tf_op jit(solution)/shard_map/pallas_call | solution.py:730
  4.5 4.1 %collective-permute-start = (f32[160,128]{1,0:T(8,128)S(1)}, f32[160,128]{1,0:T(8,128)S(1)}, u32[]{:S(2)}, u32[]{:S(2)}) collective-permute-start(f32[160,128]{1,0:T(8,128)S(1)} %get-tuple-element.64), channel_id=1, source_target_pairs={{0,16},{16,0},{4,20},{20,4},{8,24},{24,8},{12,28},{28,12},{1,17},{... | collective-permute-start | bytes 245768 | tf_op jit(solution)/shard_map/ppermute | solution.py:33
  9.2 1.4 %shard_map.104 = (f32[64,128]{1,0:T(8,128)S(1)}, f32[64,128]{1,0:T(8,128)S(1)}, f32[64,128]{1,0:T(8,128)S(1)}, f32[64,128]{1,0:T(8,128)S(1)}) custom-call(s32[4]{0:T(128)S(1)} %bitcast.5, s32[4,2048]{1,0:T(4,128)S(1)} %get-tuple-element.62.send_ref.refs_5_), custom_call_target="tpu_custom_call" | custom-call | tf_op jit(solution)/shard_map/pallas_call | solution.py:730
  11.4 2.0 %shard_map.106 = (f32[160,128]{1,0:T(8,128)S(1)}, s32[16,128]{1,0:T(8,128)S(1)}, s32[64,128]{1,0:T(8,128)S(1)}, s32[64,128]{1,0:T(8,128)S(1)}) custom-call(f32[8,8192]{1,0:T(8,128)S(1)} %get-tuple-element.61.refs_0_.field_ref, f32[64,128]{1,0:T(8,128)S(1)} %fusion.flag_ref.refs_1_, f32[64,128]{1,0:T(8,128)S(1)} %get-tuple-element.63.refs_2_.inverse_ref, ...), custom_call_target="tpu_custom_call" | custom-call | tf_op jit(solution)/shard_map/pallas_call | solution.py:730
  13.9 1.6 %collective-permute-start.1 = (f32[160,128]{1,0:T(8,128)S(1)}, f32[160,128]{1,0:T(8,128)S(1)}, u32[]{:S(2)}, u32[]{:S(2)}) collective-permute-start(f32[160,128]{1,0:T(8,128)S(1)} %shard_map.107), channel_id=1, source_target_pairs={{0,8},{8,0},{4,12},{12,4},{16,24},{24,16},{20,28},{28,20},{1,9},{9... | collective-permute-start | bytes 245768 | tf_op jit(solution)/shard_map/ppermute | solution.py:33
  15.6 3.2 %shard_map.105 = (f32[8,8192]{1,0:T(8,128)S(1)}, f32[64,128]{1,0:T(8,128)S(1)}, f32[160,128]{1,0:T(8,128)S(1)}, s32[16,128]{1,0:T(8,128)S(1)}) custom-call(f32[8,8192]{1,0:T(8,128)S(1)} %get-tuple-element.61.refs_0_.field_ref, f32[64,128]{1,0:T(8,128)S(1)} %fusion.flag_ref.refs_1_, f32[64,128]{1,0:T(8,128)S(1)} %get-tuple-element.63.refs_2_.inverse_ref, ...), custom_call_target="tpu_custom_call" | custom-call | tf_op jit(solution)/shard_map/pallas_call | solution.py:730
  19.3 1.6 %collective-permute-start.2 = (f32[160,128]{1,0:T(8,128)S(1)}, f32[160,128]{1,0:T(8,128)S(1)}, u32[]{:S(2)}, u32[]{:S(2)}) collective-permute-start(f32[160,128]{1,0:T(8,128)S(1)} %shard_map.109), channel_id=1, source_target_pairs={{0,2},{2,0},{1,3},{3,1},{4,6},{6,4},{5,7},{7,5},{8,10},{10,8},{9,1... | collective-permute-start | bytes 245768 | tf_op jit(solution)/shard_map/ppermute | solution.py:33
  20.9 3.2 %shard_map.108 = (f32[8,8192]{1,0:T(8,128)S(1)}, f32[64,128]{1,0:T(8,128)S(1)}, f32[160,128]{1,0:T(8,128)S(1)}, s32[16,128]{1,0:T(8,128)S(1)}) custom-call(f32[8,8192]{1,0:T(8,128)S(1)} %get-tuple-element.66.refs_0_, f32[64,128]{1,0:T(8,128)S(1)} %get-tuple-element.67.refs_1_, f32[64,128]{1,0:T(8,128)S(1)} %get-tuple-element.65.refs_4_.refs_2_, ...), custom_call_target="tpu_custom_call" | custom-call | tf_op jit(solution)/shard_map/pallas_call | solution.py:730
  24.5 1.6 %collective-permute-start.3 = (f32[160,128]{1,0:T(8,128)S(1)}, f32[160,128]{1,0:T(8,128)S(1)}, u32[]{:S(2)}, u32[]{:S(2)}) collective-permute-start(f32[160,128]{1,0:T(8,128)S(1)} %shard_map.111), channel_id=1, source_target_pairs={{0,1},{1,0},{2,3},{3,2},{4,5},{5,4},{6,7},{7,6},{8,9},{9,8},{10,11... | collective-permute-start | bytes 245768 | tf_op jit(solution)/shard_map/ppermute | solution.py:33
  26.7 3.1 %shard_map.110 = (f32[8,8192]{1,0:T(8,128)S(1)}, f32[64,128]{1,0:T(8,128)S(1)}, f32[128,128]{1,0:T(8,128)S(1)}) custom-call(f32[8,8192]{1,0:T(8,128)S(1)} %get-tuple-element.72.field_ref, f32[64,128]{1,0:T(8,128)S(1)} %get-tuple-element.73.flag_ref, f32[64,128]{1,0:T(8,128)S(1)} %get-tuple-element.71.refs_4_.inverse_ref, ...), custom_call_target="tpu_custom_call" | custom-call | tf_op jit(solution)/shard_map/pallas_call | solution.py:730
  29.9 3.5 %shard_map.113 = (f32[192,128]{1,0:T(8,128)S(1)}, f32[192,128]{1,0:T(8,128)S(1)}) custom-call(f32[8,8192]{1,0:T(8,128)S(1)} %get-tuple-element.77.old_field_ref.field_ref, f32[160,128]{1,0:T(8,128)S(1)} %collective-permute-done.3.in_ref, s32[64,128]{1,0:T(8,128)S(1)} %get-tuple-element.76.index_ref, f32[128,128]{1,0:T(8,128)S(1)} %get-tuple-element.82.early_ref, ...), custom_call_target="tpu_custom_call" | custom-call | tf_op jit(solution)/shard_map/pallas_call | solution.py:730
  33.8 1.0 %collective-permute-start.4 = (f32[192,128]{1,0:T(8,128)S(1)}, f32[192,128]{1,0:T(8,128)S(1)}, u32[]{:S(2)}, u32[]{:S(2)}) collective-permute-start(f32[192,128]{1,0:T(8,128)S(1)} %get-tuple-element.122), channel_id=1, source_target_pairs={{0,4},{4,0},{8,12},{12,8},{16,20},{20,16},{24,28},{28,24},{1,5},{5... | collective-permute-start | bytes 294920 | tf_op jit(solution)/shard_map/ppermute | solution.py:43
  34.8 5.6 %shard_map.112 = (f32[8,8192]{1,0:T(8,128)S(1)}, f32[64,128]{1,0:T(8,128)S(1)}, f32[128,128]{1,0:T(8,128)S(1)}, f32[512,128]{1,0:T(8,128)S(1)}, s32[64,128]{1,0:...) custom-call(s32[1]{0:T(128)S(6)} %copy.17.count_ref, ...), custom_call_target="tpu_custom_call" | custom-call | tf_op jit(solution)/shard_map/pallas_call | solution.py:730
  40.5 1.4 %collective-permute-start.6 = (f32[192,128]{1,0:T(8,128)S(1)}, f32[192,128]{1,0:T(8,128)S(1)}, u32[]{:S(2)}, u32[]{:S(2)}) collective-permute-start(f32[192,128]{1,0:T(8,128)S(1)} %pad_maximum_fusion), channel_id=1, source_target_pairs={{0,3},{1,0},{2,1},{3,2},{4,7},{5,4},{6,5},{7,6},{8,11},{9,8},{10,9... | collective-permute-start | bytes 294920 | tf_op jit(solution)/shard_map/ppermute | solution.py:23
  42.6 5.0 %shard_map.114 = (f32[1032,128]{1,0:T(8,128)S(1)}, f32[2064,128]{1,0:T(8,128)S(1)}, f32[6192,128]{1,0:T(8,128)S(1)}) custom-call(s32[8,640]{1,0:T(8,128)S(1)} %get-tuple-element.81.list_ref, s32[8,128]{1,0:T(8,128)S(1)} %get-tuple-element.87.length_ref, f32[8,8192]{1,0:T(8,128)S(1)} %get-tuple-element.90.field_ref, ...), custom_call_target="tpu_custom_call" | custom-call | tf_op jit(solution)/shard_map/pallas_call | solution.py:730
  48.0 5.4 %shard_map.115 = (f32[64,128]{1,0:T(8,128)S(1)}, f32[24,128]{1,0:T(8,128)S(1)}, f32[16,128]{1,0:T(8,128)S(1)}, f32[24,128]{1,0:T(8,128)S(1)}, f32[1032,128]{1,0:...) custom-call(s32[8,640]{1,0:T(8,128)S(1)} %get-tuple-element.81.list_ref, ...), custom_call_target="tpu_custom_call", output_to_operand_aliasing={{5}: (5, {})} | custom-call | tf_op jit(solution)/shard_map/pallas_call | solution.py:730
  53.7 4.7 %shard_map.116 = (f32[1032,128]{1,0:T(8,128)S(1)}, f32[1032,128]{1,0:T(8,128)S(1)}, f32[64,128]{1,0:T(8,128)S(1)}, f32[2064,128]{1,0:T(8,128)S(1)}, f32[4128,128]{1,0:T(8,128)S(1)}) custom-call(s32[8,640]{1,0:T(8,128)S(1)} %get-tuple-element.81.list_ref, s32[8,128]{1,0:T(8,128)S(1)} %get-tuple-element.87.length_ref, ...), custom_call_target="tpu_custom_call" | custom-call | tf_op jit(solution)/shard_map/pallas_call | solution.py:730
  58.5 2.0 %collective-permute-start.10 = (f32[24,128]{1,0:T(8,128)S(1)}, f32[24,128]{1,0:T(8,128)S(1)}, u32[]{:S(2)}, u32[]{:S(2)}) collective-permute-start(f32[24,128]{1,0:T(8,128)S(1)} %pad_maximum_fusion.2), channel_id=1, source_target_pairs={{0,3},{1,0},{2,1},{3,2},{4,7},{5,4},{6,5},{7,6},{8,11},{9,8},{10,9... | collective-permute-start | bytes 36872 | tf_op jit(solution)/shard_map/ppermute | solution.py:23
  60.5 2.4 %shard_map.117 = (f32[4128,128]{1,0:T(8,128)S(1)}, f32[1032,128]{1,0:T(8,128)S(1)}, f32[1032,128]{1,0:T(8,128)S(1)}) custom-call(s32[8,640]{1,0:T(8,128)S(1)} %get-tuple-element.81.list_ref, s32[8,128]{1,0:T(8,128)S(1)} %get-tuple-element.87.length_ref, f32[16512,128]{1,0:T(8,128)S(1)} %get-tuple-element.89.expanded_ref, ...), custom_call_target="tpu_custom_call" | custom-call | tf_op jit(solution)/shard_map/pallas_call | solution.py:730
  62.9 2.2 %collective-permute-done.11.up_ref = f32[24,128]{1,0:T(8,128)S(1)} collective-permute-done((f32[24,128]{1,0:T(8,128)S(1)}, f32[24,128]{1,0:T(8,128)S(1)}, u32[]{:S(2)}, u32[]{:S(2)}) %collective-permute-start.11) | collective-permute-done | bytes 12320 | tf_op jit(solution)/shard_map/ppermute | solution.py:23
  65.1 7.2 %shard_map.118 = (f32[3,8192]{1,0:T(4,128)}, f32[64,128]{1,0:T(8,128)}, f32[4128,128]{1,0:T(8,128)S(1)}, f32[4128,128]{1,0:T(8,128)S(1)}) custom-call(s32[8,640]{1,0:T(8,128)S(1)} %get-tuple-element.81.list_ref, s32[8,128]{1,0:T(8,128)S(1)} %get-tuple-element.87.length_ref, ...), custom_call_target="tpu_custom_call", output_to_operand_aliasing={{2}: (13, {}), {3}: (14, {})} | custom-call | tf_op jit(solution)/shard_map/pallas_call | solution.py:730
  (42 shorter events, 4.9 us)
Async XLA Ops:
  0.6 34.1 %copy-start.4 = (s32[2,512]{1,0:T(2,128)S(1)}, s32[2,512]{1,0:T(2,128)}, u32[]{:S(2)}) copy-start(s32[2,512]{1,0:T(2,128)} %pair_ref.1) | copy-start | bytes 12292
  1.4 0.9 %copy-start = (f32[8,8192]{1,0:T(8,128)S(1)}, f32[8,8192]{1,0:T(8,128)}, u32[]{:S(2)}) copy-start(f32[8,8192]{1,0:T(8,128)} %particle_ref.1) | copy-start | bytes 786436
  2.4 0.8 %copy-start.3 = (s32[4,2048]{1,0:T(4,128)S(1)}, s32[4,2048]{1,0:T(4,128)}, u32[]{:S(2)}) copy-start(s32[4,2048]{1,0:T(4,128)} %send_in_ref.1) | copy-start | bytes 98308
  4.5 9.0 %collective-permute-start = (f32[160,128]{1,0:T(8,128)S(1)}, f32[160,128]{1,0:T(8,128)S(1)}, u32[]{:S(2)}, u32[]{:S(2)}) collective-permute-start(f32[160,128]{1,0:T(8,128)S(1)} %get-tuple-element.64), channel_id=1, source_target_pairs={{0,16},{16,0},{4,20},{20,4},{8,24},{24,8},{12,28},{28,12},{1,17},{... | collective-permute-start | bytes 245768 | tf_op jit(solution)/shard_map/ppermute | solution.py:33
  8.6 0.7 copy-start.5
  10.7 0.8 %copy-start.1 = (s32[8,1024]{1,0:T(8,128)S(1)}, s32[8,1024]{1,0:T(8,128)}, u32[]{:S(2)}) copy-start(s32[8,1024]{1,0:T(8,128)} %export_ref.3) | copy-start | bytes 98308
  13.9 4.9 %collective-permute-start.1 = (f32[160,128]{1,0:T(8,128)S(1)}, f32[160,128]{1,0:T(8,128)S(1)}, u32[]{:S(2)}, u32[]{:S(2)}) collective-permute-start(f32[160,128]{1,0:T(8,128)S(1)} %shard_map.107), channel_id=1, source_target_pairs={{0,8},{8,0},{4,12},{12,4},{16,24},{24,16},{20,28},{28,20},{1,9},{9... | collective-permute-start | bytes 245768 | tf_op jit(solution)/shard_map/ppermute | solution.py:33
  19.3 4.8 %collective-permute-start.2 = (f32[160,128]{1,0:T(8,128)S(1)}, f32[160,128]{1,0:T(8,128)S(1)}, u32[]{:S(2)}, u32[]{:S(2)}) collective-permute-start(f32[160,128]{1,0:T(8,128)S(1)} %shard_map.109), channel_id=1, source_target_pairs={{0,2},{2,0},{1,3},{3,1},{4,6},{6,4},{5,7},{7,5},{8,10},{10,8},{9,1... | collective-permute-start | bytes 245768 | tf_op jit(solution)/shard_map/ppermute | solution.py:33
  24.5 5.3 %collective-permute-start.3 = (f32[160,128]{1,0:T(8,128)S(1)}, f32[160,128]{1,0:T(8,128)S(1)}, u32[]{:S(2)}, u32[]{:S(2)}) collective-permute-start(f32[160,128]{1,0:T(8,128)S(1)} %shard_map.111), channel_id=1, source_target_pairs={{0,1},{1,0},{2,3},{3,2},{4,5},{5,4},{6,7},{7,6},{8,9},{9,8},{10,11... | collective-permute-start | bytes 245768 | tf_op jit(solution)/shard_map/ppermute | solution.py:33
  33.4 7.0 %collective-permute-start.5 = (f32[192,128]{1,0:T(8,128)S(1)}, f32[192,128]{1,0:T(8,128)S(1)}, u32[]{:S(2)}, u32[]{:S(2)}) collective-permute-start(f32[192,128]{1,0:T(8,128)S(1)} %get-tuple-element.121), channel_id=1, source_target_pairs={{0,28},{4,8},{8,4},{12,16},{16,12},{20,24},{24,20},{28,0},{1,29},{... | collective-permute-start | bytes 294920 | tf_op jit(solution)/shard_map/ppermute | solution.py:44
  33.8 6.6 %collective-permute-start.4 = (f32[192,128]{1,0:T(8,128)S(1)}, f32[192,128]{1,0:T(8,128)S(1)}, u32[]{:S(2)}, u32[]{:S(2)}) collective-permute-start(f32[192,128]{1,0:T(8,128)S(1)} %get-tuple-element.122), channel_id=1, source_target_pairs={{0,4},{4,0},{8,12},{12,8},{16,20},{20,16},{24,28},{28,24},{1,5},{5... | collective-permute-start | bytes 294920 | tf_op jit(solution)/shard_map/ppermute | solution.py:43
  40.5 7.1 %collective-permute-start.6 = (f32[192,128]{1,0:T(8,128)S(1)}, f32[192,128]{1,0:T(8,128)S(1)}, u32[]{:S(2)}, u32[]{:S(2)}) collective-permute-start(f32[192,128]{1,0:T(8,128)S(1)} %pad_maximum_fusion), channel_id=1, source_target_pairs={{0,3},{1,0},{2,1},{3,2},{4,7},{5,4},{6,5},{7,6},{8,11},{9,8},{10,9... | collective-permute-start | bytes 294920 | tf_op jit(solution)/shard_map/ppermute | solution.py:23
  41.9 6.1 %collective-permute-start.7 = (f32[192,128]{1,0:T(8,128)S(1)}, f32[192,128]{1,0:T(8,128)S(1)}, u32[]{:S(2)}, u32[]{:S(2)}) collective-permute-start(f32[192,128]{1,0:T(8,128)S(1)} %pad_maximum_fusion.1), channel_id=1, source_target_pairs={{0,1},{1,2},{2,3},{3,0},{4,5},{5,6},{6,7},{7,4},{8,9},{9,10},{10,1... | collective-permute-start | bytes 294920 | tf_op jit(solution)/shard_map/ppermute | solution.py:23
  42.6 5.4 %copy-start.2 = (s32[8,1024]{1,0:T(8,128)S(1)}, s32[8,1024]{1,0:T(8,128)}, u32[]{:S(2)}) copy-start(s32[8,1024]{1,0:T(8,128)} %export_ref.3) | copy-start | bytes 98308
  53.3 5.0 %collective-permute-start.9 = (f32[24,128]{1,0:T(8,128)S(1)}, f32[24,128]{1,0:T(8,128)S(1)}, u32[]{:S(2)}, u32[]{:S(2)}) collective-permute-start(f32[24,128]{1,0:T(8,128)S(1)} %get-tuple-element.131), channel_id=1, source_target_pairs={{0,28},{4,8},{8,4},{12,16},{16,12},{20,24},{24,20},{28,0},{1,29},{... | collective-permute-start | bytes 36872 | tf_op jit(solution)/shard_map/ppermute | solution.py:44
  53.7 4.7 %collective-permute-start.8 = (f32[24,128]{1,0:T(8,128)S(1)}, f32[24,128]{1,0:T(8,128)S(1)}, u32[]{:S(2)}, u32[]{:S(2)}) collective-permute-start(f32[24,128]{1,0:T(8,128)S(1)} %get-tuple-element.132), channel_id=1, source_target_pairs={{0,4},{4,0},{8,12},{12,8},{16,20},{20,16},{24,28},{28,24},{1,5},{5... | collective-permute-start | bytes 36872 | tf_op jit(solution)/shard_map/ppermute | solution.py:43
  58.5 4.4 %collective-permute-start.10 = (f32[24,128]{1,0:T(8,128)S(1)}, f32[24,128]{1,0:T(8,128)S(1)}, u32[]{:S(2)}, u32[]{:S(2)}) collective-permute-start(f32[24,128]{1,0:T(8,128)S(1)} %pad_maximum_fusion.2), channel_id=1, source_target_pairs={{0,3},{1,0},{2,1},{3,2},{4,7},{5,4},{6,5},{7,6},{8,11},{9,8},{10,9... | collective-permute-start | bytes 36872 | tf_op jit(solution)/shard_map/ppermute | solution.py:23
  60.5 4.6 %collective-permute-start.11 = (f32[24,128]{1,0:T(8,128)S(1)}, f32[24,128]{1,0:T(8,128)S(1)}, u32[]{:S(2)}, u32[]{:S(2)}) collective-permute-start(f32[24,128]{1,0:T(8,128)S(1)} %pad_maximum_fusion.3), channel_id=1, source_target_pairs={{0,1},{1,2},{2,3},{3,0},{4,5},{5,6},{6,7},{7,4},{8,9},{9,10},{10,1... | collective-permute-start | bytes 36872 | tf_op jit(solution)/shard_map/ppermute | solution.py:23
